TPU v7x, 512 devices: a whole 4x4x16 slice. The times are simulated.
512 devices in a mesh: trip: 64 (over z, x), aux: 8 (over y, core).
Axes of the slice: x: 4, y: 4, z: 16, core: 2. Of those that a mesh axis runs over, the one named last changes fastest.
Arguments:
- aux_blocks: bfloat16 [576, 1024, 1600], P('trip', 'aux'), may hold values from -6 to 6
- occ_blocks: bfloat16 [576, 1024, 120], P('trip', 'aux'), may hold values from -0.03125 to 0.03125
- intersections: bfloat16 [576, 3, 64, 40], P('trip'), may hold values from -0.75 to 0.75
- tno_energy: float32 [576, 40], P('trip'), may hold values from 0.5 to 3
- occ_energy: float32 [576, 3], P('trip'), may hold values from -1 to -0.3
- tno_rank: int32 [576], P('trip'), may hold values from 20 to 40
- triples_old: float32 [576, 40, 1600], P('trip', 'aux'), may hold values from -6 to 6
- pair_amps: bfloat16 [1024, 4096], P('trip'), may hold values from -6 to 6
- pno_energy: float32 [1024, 64], P('trip'), may hold values from 0.5 to 3
- pair_occ: float32 [1024], P('trip'), may hold values from 0.6 to 2
- pair_rank: int32 [1024], P('trip'), may hold values from 16 to 64
- request_owner: int32 [576, 3, 1], P('trip'), may hold values from 0 to 63; in each aligned block of 27 rows (0 to 26, 27 to 53, ..., all dimensions but the last counted through in order) no two rows name the same one
- request_row: int32 [576, 3], P('trip'), may hold values from 0 to 15
Outputs:
- triples_new: float32 [576, 40, 1600], P('trip', 'aux')
- pairs_new: float32 [1024, 4096], P('trip')
Inputs may be any that keep to these rules, and one draw needn't show every extreme that they name: `request_owner`: within the rows of one device (aligned blocks of 27 rows), no owner is named by more than 1 row, a bound that some block reaches.
All inputs are finite; a program needn't handle non-finite values.
Results may differ from a plain program's by a relative error of at most 0.022.
Values may be sent and summed in bfloat16 or wider, within the bound.
No kernel may reach another device: no remote copies, remote signals or barrier semaphores. Data moves between devices by JAX's collectives and lax.ppermute only.
A program may use at most 128 MiB of HBM per device.

v0:
```python
import jax
import jax.numpy as jnp
from jax import lax
from jax.sharding import PartitionSpec as P

PASSES = 2


SHIFT_LEVEL = 1.0


def body(
    aux_blocks,
    occ_blocks,
    intersections,
    tno_energy,
    occ_energy,
    tno_rank,
    triples_old,
    pair_amps,
    pno_energy,
    pair_occ,
    pair_rank,
    request_owner,
    request_row,
):
    tdev = aux_blocks.shape[0]
    ntno = tno_energy.shape[1]
    npno = pno_energy.shape[1]
    pdev = pair_amps.shape[0]
    naux = lax.axis_size("aux")
    ntrip = lax.axis_size("trip")
    member = lax.axis_index("aux")
    share = ntno // naux
    nreq = 3 * tdev
    capacity = (nreq + ntrip - 1) // ntrip
    slots = ntrip * capacity
    owner = request_owner.reshape(nreq)
    local = request_row.reshape(nreq)
    order = jnp.arange(nreq)
    before = (order[None, :] < order[:, None]) & (owner[None, :] == owner[:, None])
    target = owner * capacity + jnp.sum(before.astype(jnp.int32), axis=1)
    placed = target[:, None] == jnp.arange(slots)[None, :]
    positioned_buffer = placed.astype(jnp.bfloat16)
    wanted = (jnp.sum(jnp.where(placed, local[:, None] + 1, 0), axis=0) - 1).reshape(
        ntrip, capacity
    )
    asked_rows = lax.all_to_all(wanted, "trip", split_axis=0, concat_axis=0, tiled=True)
    own_place = (jnp.arange(pdev)[:, None] == asked_rows.reshape(slots)[None, :]).astype(
        jnp.bfloat16
    )
    integrals = jnp.einsum(
        "tqx,tqy->txy", aux_blocks, occ_blocks, preferred_element_type=jnp.float32
    ).astype(jnp.bfloat16)
    coulomb_matrix = (
        integrals.reshape(tdev, ntno, ntno, 3, ntno)
        .transpose(0, 3, 1, 2, 4)
        .reshape(tdev, 3 * ntno, ntno * ntno)
    )
    live = jnp.arange(npno)[None, :] < pair_rank[:, None]
    pair_keep = (live[:, :, None] & live[:, None, :]).reshape(pdev, npno * npno)
    denom = (
        pno_energy[:, :, None] + pno_energy[:, None, :] + pair_occ[:, None, None] + SHIFT_LEVEL
    ).reshape(pdev, npno * npno)
    amps = pair_amps.astype(jnp.float32)
    occ_sum = jnp.sum(occ_energy, axis=1)
    keep_tno = jnp.arange(ntno)[None, :] < tno_rank[:, None]
    state = triples_old
    tri = (
        lax.dynamic_slice_in_dim(tno_energy, member * share, share, 1)[:, :, None, None]
        + tno_energy[:, None, :, None]
        + tno_energy[:, None, None, :]
        - occ_sum[:, None, None, None]
        + SHIFT_LEVEL
    )
    keep = (
        lax.dynamic_slice_in_dim(keep_tno, member * share, share, 1)[:, :, None, None]
        & keep_tno[:, None, :, None]
        & keep_tno[:, None, None, :]
    )
    tri_den = tri.reshape(tdev, -1, ntno * ntno)
    tri_keep = keep.reshape(tdev, -1, ntno * ntno)
    cover = intersections.astype(jnp.float32)
    for step in range(PASSES):
        outgoing = jnp.where(pair_keep, amps.astype(jnp.bfloat16), jnp.zeros((), jnp.bfloat16))
        found = outgoing[jnp.maximum(asked_rows, 0)]
        arrived = lax.all_to_all(found, "trip", split_axis=0, concat_axis=0, tiled=True)
        fetched = jnp.dot(
            positioned_buffer,
            arrived.reshape(slots, npno * npno),
            preferred_element_type=jnp.float32,
        ).astype(jnp.bfloat16)
        fetched = fetched.reshape(tdev, 3, npno, npno)
        half = jnp.einsum(
            "tmpq,tmqa->tmpa", fetched, intersections, preferred_element_type=jnp.float32
        ).astype(jnp.bfloat16)
        proj = jnp.einsum(
            "tmpa,tmpd->tmad", intersections, half, preferred_element_type=jnp.float32
        ).astype(jnp.bfloat16)
        projected_rows = proj.transpose(0, 2, 1, 3).reshape(tdev, ntno, 3 * ntno)
        partial_intermediate = jnp.einsum(
            "obi,oiy->oby", projected_rows, coulomb_matrix, preferred_element_type=jnp.float32
        )
        summed = lax.psum_scatter(
            partial_intermediate.astype(jnp.bfloat16), "aux", scatter_dimension=1, tiled=True
        ).astype(jnp.float32)
        state = jnp.where(tri_keep, (SHIFT_LEVEL * state + summed) / tri_den, 0.0)
        complete_row_set = lax.all_gather(state.astype(jnp.bfloat16), "aux", axis=1, tiled=True)
        count = complete_row_set.shape[1]
        flattened_view = jnp.einsum(
            "iun,iwn->iuw", complete_row_set, coulomb_matrix, preferred_element_type=jnp.float32
        )
        rpart = flattened_view.reshape(tdev, count, 3, ntno).transpose(0, 2, 1, 3)
        resid = lax.psum(rpart.astype(jnp.bfloat16), "aux").astype(jnp.float32)
        left = jnp.einsum("tmpa,tmad->tmpd", cover, resid, precision=lax.Precision.HIGHEST)
        back = (
            jnp.einsum("tmpd,tmqd->tmpq", left, cover, precision=lax.Precision.HIGHEST)
            .astype(jnp.bfloat16)
            .reshape(nreq, npno * npno)
        )
        sent = (
            jnp.dot(positioned_buffer.T, back, preferred_element_type=jnp.float32)
            .astype(jnp.bfloat16)
            .reshape(ntrip, capacity, npno * npno)
        )
        came = lax.all_to_all(sent, "trip", split_axis=0, concat_axis=0, tiled=True)
        total = jnp.dot(
            own_place, came.reshape(slots, npno * npno), preferred_element_type=jnp.float32
        )
        amps = amps + jnp.where(pair_keep, total / denom, 0.0)
    return (state, amps)


def solution(mesh):
    in_specs = (
        P("trip", "aux", None),
        P("trip", "aux", None),
        P("trip", None, None, None),
        P("trip", None),
        P("trip", None),
        P("trip"),
        P("trip", "aux", None),
        P("trip", None),
        P("trip", None),
        P("trip"),
        P("trip"),
        P("trip", None, None),
        P("trip", None),
    )
    out_specs = (P("trip", "aux", None), P("trip", None))
    return jax.shard_map(body, mesh=mesh, in_specs=in_specs, out_specs=out_specs, check_vma=False)
```

profile of v0, /device:TPU:1, one launch (start us, length us, event | category | flops | bytes accessed | tf_op | source)
XLA Modules:
  0.0 648.7 jit_solution(2849419014451976568)
XLA Ops:
  7.2 0.7 broadcast_add_fusion.2
  8.1 0.8 copy.57
  9.2 0.7 copy.59
  10.0 19.1 %all-to-all-start = ((s32[64,1,1]{2,1,0:T(1,128)}), s32[64,1,1]{2,1,0:T(1,128)S(1)}, u32[]{:S(2)}, u32[]{:S(2)}) async-start(s32[64,1,1]{2,1,0:T(1,128)} %copy.59), calls=%async_computation | async-start | bytes 65536 | tf_op jit(solution)/shard_map/all_to_all | solution.py:48
  29.1 0.7 iota_compare_fusion.9
  30.3 0.9 broadcast_select_fusion
  31.2 11.3 %all-to-all-done = s32[64,1,1]{2,1,0:T(1,128)S(1)} async-done(((s32[64,1,1]{2,1,0:T(1,128)}), s32[64,1,1]{2,1,0:T(1,128)S(1)}, u32[]{:S(2)}, u32[]{:S(2)}) %all-to-all-start) | async-done | bytes 288 | tf_op jit(solution)/shard_map/all_to_all | solution.py:48
  42.5 2.4 fusion.32
  44.8 0.9 gather_fusion
  46.2 0.9 reduce.4
  47.1 1.2 reshape.232
  48.3 4.6 all-to-all-start.1
  53.0 6.3 convolution_convert_fusion.4
  59.3 14.7 %reshape.197 = bf16[9,40,40,3,40]{2,1,4,3,0:T(8,128)(2,1)} reshape(bf16[9,1600,120]{1,2,0:T(8,128)(2,1)} %convolution_convert_fusion.4) | data formatting | bytes 6912000 | tf_op jit(solution)/shard_map/reshape | solution.py:56
  74.0 16.1 %copy.61 = bf16[9,3,40,40,40]{4,3,2,1,0:T(8,128)(2,1)} copy(bf16[9,3,40,40,40]{3,2,4,1,0:T(8,128)(2,1)} %bitcast.78) | data formatting | bytes 6912000 | tf_op jit(solution)/shard_map/transpose | solution.py:57
  90.1 14.4 %reshape.198 = bf16[9,120,1600]{2,1,0:T(8,128)(2,1)} reshape(bf16[9,3,40,40,40]{4,3,2,1,0:T(8,128)(2,1)} %copy.61) | data formatting | bytes 6912000 | tf_op jit(solution)/shard_map/reshape | solution.py:58
  106.7 3.8 convolution_convert_fusion.6
  113.1 1.3 dynamic-slice
  115.0 75.1 %all-reduce.11.cloned.1.call-done = bf16[9,40,1600]{2,1,0:T(8,128)(2,1)} async-done(((bf16[9,40,1600]{2,1,0:T(8,128)(2,1)}), bf16[9,40,1600]{2,1,0:T(8,128)(2,1)}) %all-reduce.11.cloned.1.call-update) | async-done | bytes 1152016
  190.1 1.3 fusion.31
  191.4 0.7 copy.63
  192.2 34.5 %all-gather.3.cloned.1.call-done = bf16[9,40,1600]{2,0,1:T(8,128)(2,1)} async-done(((bf16[9,5,1600]{2,0,1:T(8,128)(2,1)}), bf16[9,40,1600]{2,0,1:T(8,128)(2,1)}) %all-gather.3.cloned.1.call-update) | async-done | bytes 1152016 | tf_op jit(solution)/shard_map/all_gather | solution.py:108
  226.7 4.0 fusion.10
  230.7 0.9 copy.75
  231.6 74.2 %all-reduce.7.cloned.1.call-done = bf16[9,3,40,40]{2,3,1,0:T(8,128)(2,1)} async-done(((bf16[9,3,40,40]{2,3,1,0:T(8,128)(2,1)}), bf16[9,3,40,40]{2,3,1,0:T(8,128)(2,1)}) %all-reduce.7.cloned.1.call-update) | async-done | bytes 86416 | tf_op jit(solution)/shard_map/psum | solution.py:114
  305.9 1.2 fusion.34
  307.1 0.9 convolution_convert_fusion.8
  308.9 0.9 reduce.5
  309.8 1.2 reshape.234
  310.9 14.4 %all-to-all-start.2 = ((bf16[64,2,2048]{2,1,0:T(2,128)(2,1)}), bf16[64,2,2048]{2,1,0:T(2,128)(2,1)S(1)}, u32[]{:S(2)}, u32[]{:S(2)}) async-start(bf16[64,2,2048]{2,1,0:T(2,128)(2,1)} %reshape.234), calls=%async_computation.2 | async-start | bytes 1048576 | tf_op jit(solution)/shard_map/all_to_all | solution.py:126
  325.8 28.8 %all-to-all-done.2 = bf16[64,2,2048]{2,1,0:T(2,128)(2,1)S(1)} async-done(((bf16[64,2,2048]{2,1,0:T(2,128)(2,1)}), bf16[64,2,2048]{2,1,0:T(2,128)(2,1)S(1)}, u32[]{:S(2)}, u32[]{:S(2)}) %all-to-all-start.2) | async-done | bytes 524320 | tf_op jit(solution)/shard_map/all_to_all | solution.py:126
  355.2 2.3 convert_select_fusion
  357.4 0.9 gather_fusion.1
  358.3 0.9 reduce.6
  359.6 37.7 %all_to_all.26 = bf16[64,2,2048]{2,1,0:T(2,128)(2,1)S(1)} all-to-all(bf16[64,2,2048]{2,1,0:T(2,128)(2,1)S(1)} %reshape.236), channel_id=1, replica_groups=mesh['trip'=64,'aux'=8] {'trip'}, dimensions={0} | all-to-all | bytes 1048576 | tf_op jit(solution)/shard_map/all_to_all | solution.py:87
  399.5 3.8 convolution_convert_fusion.5
  403.6 72.3 %all-reduce.13.cloned.1.call-done = bf16[9,40,1600]{2,1,0:T(8,128)(2,1)} async-done(((bf16[9,40,1600]{2,1,0:T(8,128)(2,1)}), bf16[9,40,1600]{2,1,0:T(8,128)(2,1)}) %all-reduce.13.cloned.1.call-update) | async-done | bytes 1152016
  475.9 2.3 fusion.33
  478.3 0.7 copy.69
  479.1 34.0 %all-gather.5.cloned.1.call-done = bf16[9,40,1600]{2,0,1:T(8,128)(2,1)} async-done(((bf16[9,5,1600]{2,0,1:T(8,128)(2,1)}), bf16[9,40,1600]{2,0,1:T(8,128)(2,1)}) %all-gather.5.cloned.1.call-update) | async-done | bytes 1152016 | tf_op jit(solution)/shard_map/all_gather | solution.py:108
  513.1 4.0 fusion.13
  517.1 0.9 copy.76
  518.0 74.2 %all-reduce.9.cloned.1.call-done = bf16[9,3,40,40]{2,3,1,0:T(8,128)(2,1)} async-done(((bf16[9,3,40,40]{2,3,1,0:T(8,128)(2,1)}), bf16[9,3,40,40]{2,3,1,0:T(8,128)(2,1)}) %all-reduce.9.cloned.1.call-update) | async-done | bytes 86416 | tf_op jit(solution)/shard_map/psum | solution.py:114
  592.2 1.2 fusion.35
  593.5 0.9 convolution_convert_fusion.7
  595.2 0.9 reduce.7
  596.5 43.5 %all_to_all.27 = bf16[64,2,2048]{2,1,0:T(2,128)(2,1)S(1)} all-to-all(bf16[64,2,2048]{2,1,0:T(2,128)(2,1)S(1)} %reshape.238), channel_id=1, replica_groups=mesh['trip'=64,'aux'=8] {'trip'}, dimensions={0} | all-to-all | bytes 1048576 | tf_op jit(solution)/shard_map/all_to_all | solution.py:126
  640.5 1.4 fusion.3
  (76 shorter events, 12.8 us)
Async XLA Ops:
  7.2 45.9 %copy-start = (bf16[9,128,120]{1,2,0:T(8,128)(2,1)S(1)}, bf16[9,128,120]{1,2,0:T(8,128)(2,1)}, u32[]{:S(2)}) copy-start(bf16[9,128,120]{1,2,0:T(8,128)(2,1)} %param.14) | copy-start | bytes 829444
  10.0 32.5 %all-to-all-start = ((s32[64,1,1]{2,1,0:T(1,128)}), s32[64,1,1]{2,1,0:T(1,128)S(1)}, u32[]{:S(2)}, u32[]{:S(2)}) async-start(s32[64,1,1]{2,1,0:T(1,128)} %copy.59), calls=%async_computation | async-start | bytes 65536 | tf_op jit(solution)/shard_map/all_to_all | solution.py:48
  48.3 56.2 %all-to-all-start.1 = ((bf16[64,2,2048]{2,1,0:T(2,128)(2,1)}), bf16[64,2,2048]{2,1,0:T(2,128)(2,1)S(1)}, u32[]{:S(2)}, u32[]{:S(2)}) async-start(bf16[64,2,2048]{2,1,0:T(2,128)(2,1)} %reshape.232), calls=%async_computation.1 | async-start | bytes 1048576 | tf_op jit(solution)/shard_map/all_to_all | solution.py:87
  53.0 137.1 %all-reduce.11.cloned.1.call-start = ((), (), s32[]{:S(2)}) async-start(), calls=%async_computation.9 | async-start | bytes 2396160
  90.1 14.4 %copy-start.4 = (f32[9,40]{1,0:T(8,128)S(1)}, f32[9,40]{1,0:T(8,128)}, u32[]{:S(2)}) copy-start(f32[9,40]{1,0:T(8,128)} %param.16) | copy-start | bytes 4324
  90.1 16.1 %copy-start.2 = (bf16[9,3,64,40]{2,3,1,0:T(8,128)(2,1)S(1)}, bf16[9,3,64,40]{2,3,1,0:T(8,128)(2,1)}, u32[]{:S(2)}) copy-start(bf16[9,3,64,40]{2,3,1,0:T(8,128)(2,1)} %param.15) | copy-start | bytes 414724
  106.7 5.0 copy-start.7
  110.5 2.6 copy-start.6
  110.5 79.6 %copy-start.3 = (f32[9,5,1600]{2,1,0:T(8,128)S(1)}, f32[9,5,1600]{2,1,0:T(8,128)}, u32[]{:S(2)}) copy-start(f32[9,5,1600]{2,1,0:T(8,128)} %param.19) | copy-start | bytes 864004
  110.5 116.2 %all-gather.3.cloned.1.call-start = ((), (), s32[]{:S(2)}) async-start(), calls=%async_computation.5 | async-start | bytes 2396160 | tf_op jit(solution)/shard_map/all_gather | solution.py:108
  192.2 113.7 %all-reduce.7.cloned.1.call-start = ((), (), s32[]{:S(2)}) async-start(), calls=%async_computation.6 | async-start | bytes 552960 | tf_op jit(solution)/shard_map/psum | solution.py:114
  231.6 93.8 %copy-start.5 = (f32[16,64]{1,0:T(8,128)S(1)}, f32[16,64]{1,0:T(8,128)}, u32[]{:S(2)}) copy-start(f32[16,64]{1,0:T(8,128)} %param.21) | copy-start | bytes 12292
  308.0 47.1 %copy-start.8 = (f32[16]{0:T(128)S(1)}, f32[16]{0:T(128)}, u32[]{:S(2)}) copy-start(f32[16]{0:T(128)} %param.22) | copy-start | bytes 196
  310.9 43.7 %all-to-all-start.2 = ((bf16[64,2,2048]{2,1,0:T(2,128)(2,1)}), bf16[64,2,2048]{2,1,0:T(2,128)(2,1)S(1)}, u32[]{:S(2)}, u32[]{:S(2)}) async-start(bf16[64,2,2048]{2,1,0:T(2,128)(2,1)} %reshape.234), calls=%async_computation.2 | async-start | bytes 1048576 | tf_op jit(solution)/shard_map/all_to_all | solution.py:126
  325.3 150.6 %all-reduce.13.cloned.1.call-start = ((), (), s32[]{:S(2)}) async-start(), calls=%async_computation.10 | async-start | bytes 2396160
  403.3 109.8 %all-gather.5.cloned.1.call-start = ((), (), s32[]{:S(2)}) async-start(), calls=%async_computation.7 | async-start | bytes 2396160 | tf_op jit(solution)/shard_map/all_gather | solution.py:108
  479.0 113.2 %all-reduce.9.cloned.1.call-start = ((), (), s32[]{:S(2)}) async-start(), calls=%async_computation.8 | async-start | bytes 552960 | tf_op jit(solution)/shard_map/psum | solution.py:114
  593.5 47.0 %copy-start.9 = (f32[16,4096]{1,0:T(8,128)S(1)}, f32[16,4096]{1,0:T(8,128)}, u32[]{:S(2)}) copy-start(f32[16,4096]{1,0:T(8,128)} %get-tuple-element.7) | copy-start | bytes 786436
  594.4 47.5 %copy-start.1 = (bf16[9,128,120]{1,2,0:T(8,128)(2,1)S(1)}, bf16[9,128,120]{1,2,0:T(8,128)(2,1)}, u32[]{:S(2)}) copy-start(bf16[9,128,120]{1,2,0:T(8,128)(2,1)} %param.14) | copy-start | bytes 829444
Sparse Core Ops, SparseCore 0:
  110.6 79.4 all-reduce.10
  192.8 33.8 all-gather.2
  231.8 74.0 all-reduce.6
  403.4 72.4 all-reduce.12
  479.2 33.8 all-gather.4
  518.1 74.0 all-reduce.8
where the time goes:
time: 653 us; the launch traced here: 649 us
  waiting for transfers between devices  405 us (62%)
  blocking collectives  81.1 us (12%)
  local copies, waits for them, and re-layouts  63 us (10%)
  starting transfers between devices  38.8 us (6%)
  matrix products  33.1 us (5%)
  between operations  15.2 us (2%)
  other arithmetic  13 us (2%)
    psum x2, waiting for transfers between devices, body(): resid = lax.psum(rpart.astype(jnp.bfloat16), 'aux').astype(jnp.float32)  148 us
    unnamed x8, waiting for transfers between devices  148 us
    all_gather x2, waiting for transfers between devices, body(): lax.all_gather(state.astype(jnp.bfloat16), 'aux', axis=1, tiled=True)  68.5 us
    all_to_all x1, blocking collectives, body(): came = lax.all_to_all(sent, 'trip', split_axis=0, concat_axis=0, tiled=True)  43.5 us
    all_to_all x1, blocking collectives, body(): lax.all_to_all(found, 'trip', split_axis=0, concat_axis=0, tiled=True)  37.7 us
    all_to_all x1, waiting for transfers between devices, body(): came = lax.all_to_all(sent, 'trip', split_axis=0, concat_axis=0, tiled=True)  28.8 us
    all_to_all x1, starting transfers between devices, body(): lax.all_to_all(wanted, 'trip', split_axis=0, concat_axis=0, tiled=True)  19.1 us
    transpose x1, local copies, waits for them, and re-layouts, body(): coulomb_matrix = integrals.reshape(tdev, ntno, ntno, 3, ntno).transpose(0...  16.1 us
  transfers between devices with their start and end apart: 9, of which 8 were waited for; matrix products, arithmetic and copies ran while one was open for 9% of the time, Pallas kernels for 0%

commit v1 on v0

v1 whole, which is shorter than its diff:
```python
import jax
import jax.numpy as jnp
from jax import lax
from jax.sharding import PartitionSpec as P

PASSES = 2
SHIFT_LEVEL = 1.0
BF = jnp.bfloat16
F32 = jnp.float32


def mm(x, y):
    return jnp.dot(x, y, preferred_element_type=F32)


def swap(x, axis):
    return lax.all_to_all(x, axis, split_axis=0, concat_axis=0, tiled=True)


def integral_blocks(aux_blocks, occ_blocks):
    naux = lax.axis_size("aux")
    tdev, _, nsq = aux_blocks.shape
    ntno = occ_blocks.shape[2] // 3
    full = jnp.einsum(
        "tqx,tqy->txy", aux_blocks, occ_blocks, preferred_element_type=F32
    ).astype(BF)
    last = full[naux].reshape(ntno, naux, ntno // naux, 3 * ntno).transpose(1, 2, 0, 3)
    last = last.reshape(naux, nsq // naux, 3 * ntno)
    return jnp.concatenate([full[:naux], last], axis=1)


def integral_matrix(rows, ntno, share):
    nsq = ntno * ntno
    own = rows[:nsq].reshape(ntno, ntno, 3, ntno).transpose(2, 0, 1, 3).reshape(3 * ntno, nsq)
    last = rows[nsq:].reshape(share, ntno, 3, ntno).transpose(2, 1, 0, 3)
    return own, last.reshape(3 * ntno, share * ntno)


def body(
    aux_blocks,
    occ_blocks,
    intersections,
    tno_energy,
    occ_energy,
    tno_rank,
    triples_old,
    pair_amps,
    pno_energy,
    pair_occ,
    pair_rank,
    request_owner,
    request_row,
):
    tdev = aux_blocks.shape[0]
    ntno = tno_energy.shape[1]
    npno = pno_energy.shape[1]
    pdev = pair_amps.shape[0]
    naux = lax.axis_size("aux")
    ntrip = lax.axis_size("trip")
    member = lax.axis_index("aux")
    share = ntno // naux
    nreq = 3 * tdev
    nsq = ntno * ntno
    prow = npno // naux
    chunk = prow * npno // 128
    owner = request_owner.reshape(nreq)
    local = request_row.reshape(nreq)

    placed = owner[:, None] == jnp.arange(ntrip)[None, :]
    wanted = jnp.sum(jnp.where(placed, local[:, None] + 1, 0), axis=0) - 1
    asked = swap(wanted.reshape(ntrip, 1), "trip")

    rows = lax.psum_scatter(
        integral_blocks(aux_blocks, occ_blocks), "aux", scatter_dimension=0, tiled=True
    )[0]

    number = jnp.arange(naux * 6 * chunk)
    dest, k, piece = number // (6 * chunk), (number // chunk) % 6, number % chunk
    request = jnp.where(k < 3, 3 * dest + k, 3 * naux + k - 3)
    req_owner = jnp.sum(
        jnp.where(request[:, None] == jnp.arange(nreq)[None, :], owner[None, :], 0), axis=1
    )
    column = jnp.arange(ntrip * chunk)
    route = (req_owner * chunk + piece)[:, None] == column[None, :]
    route = route.astype(BF)
    route_back = route.T
    own_rows = jnp.arange(pdev * chunk)
    serve = (asked * chunk + jnp.arange(chunk)[None, :]).reshape(ntrip * chunk)
    serve = jnp.where(jnp.repeat(asked.reshape(ntrip) >= 0, chunk), serve, -1)
    serve = (serve[:, None] == own_rows[None, :]).astype(BF)
    serve_back = serve.T

    live = jnp.arange(npno)[None, :] < pair_rank[:, None]
    live_p = lax.dynamic_slice_in_dim(live, member * prow, prow, 1)
    energy_p = lax.dynamic_slice_in_dim(pno_energy, member * prow, prow, 1)
    pair_keep = (live_p[:, :, None] & live[:, None, :]).reshape(pdev * chunk, 128)
    pair_den = (
        energy_p[:, :, None] + pno_energy[:, None, :] + pair_occ[:, None, None] + SHIFT_LEVEL
    ).reshape(pdev * chunk, 128)
    amps = (
        lax.dynamic_slice_in_dim(pair_amps, member * prow * npno, prow * npno, 1)
        .reshape(pdev * chunk, 128)
        .astype(F32)
    )
    gain = jnp.zeros_like(amps)

    def two(x):
        return lax.dynamic_slice_in_dim(x, member, 1, 0)[0], x[naux]

    old = triples_old.astype(BF)
    old_last = old[naux].reshape(share, naux, share * ntno).transpose(1, 0, 2)
    old = swap(jnp.concatenate([old[:naux], old_last], axis=2), "aux")
    old = old.reshape(ntno, nsq + share * ntno).astype(F32)
    states = [old[:, :nsq], old[:, nsq:]]
    energies, sums, ranks, covers = (
        two(tno_energy),
        two(jnp.sum(occ_energy, axis=1)),
        two(tno_rank),
        two(intersections),
    )
    dens, keeps = [], []
    for which in range(2):
        e, low = energies[which], 0
        live_t = jnp.arange(ntno) < ranks[which]
        e_b, live_b = e, live_t
        if which == 1:
            e_b = lax.dynamic_slice_in_dim(e, member * share, share, 0)
            live_b = lax.dynamic_slice_in_dim(live_t, member * share, share, 0)
        den = e[:, None, None] + e_b[None, :, None] + e[None, None, :] - sums[which] + SHIFT_LEVEL
        keep = live_t[:, None, None] & live_b[None, :, None] & live_t[None, None, :]
        dens.append(den.reshape(ntno, -1))
        keeps.append(keep.reshape(ntno, -1))
    matrices = integral_matrix(rows, ntno, share)

    for step in range(PASSES):
        outgoing = jnp.where(pair_keep, amps.astype(BF), jnp.zeros((), BF))
        found = mm(serve, outgoing).astype(BF).reshape(ntrip, chunk, 128)
        arrived = swap(found, "trip").reshape(ntrip * chunk, 128)
        handed = mm(route, arrived).astype(BF).reshape(naux, 6 * chunk, 128)
        fetched = swap(handed, "aux").reshape(naux, 6, prow, npno)
        fetched = fetched.transpose(1, 0, 2, 3).reshape(2, 3, npno, npno)
        backs = []
        for which in range(2):
            cover = covers[which]
            half = jnp.einsum(
                "mpq,mqa->mpa", fetched[which], cover, preferred_element_type=F32
            ).astype(BF)
            proj = jnp.einsum("mpa,mpd->amd", cover, half, preferred_element_type=F32)
            proj = proj.astype(BF).reshape(ntno, 3 * ntno)
            w = mm(proj, matrices[which])
            state = jnp.where(keeps[which], (SHIFT_LEVEL * states[which] + w) / dens[which], 0.0)
            states[which] = state
            resid = jnp.einsum(
                "an,xn->ax", state.astype(BF), matrices[which], preferred_element_type=F32
            ).reshape(ntno, 3, ntno)
            cover = cover.astype(F32)
            left = jnp.einsum("mpa,amd->mpd", cover, resid, precision=lax.Precision.HIGHEST)
            back = jnp.einsum("mpd,mqd->mpq", left, cover, precision=lax.Precision.HIGHEST)
            backs.append(back.astype(BF))
        back = jnp.stack(backs).reshape(6, naux, chunk, 128).transpose(1, 0, 2, 3)
        came = swap(back.reshape(naux, 6 * chunk, 128), "aux").reshape(naux * 6 * chunk, 128)
        sent = mm(route_back, came).astype(BF).reshape(ntrip, chunk, 128)
        came = swap(sent, "trip").reshape(ntrip * chunk, 128)
        total = mm(serve_back, came)
        change = jnp.where(pair_keep, total / pair_den, 0.0)
        gain = gain + change
        amps = amps + change

    new = jnp.concatenate(states, axis=1).reshape(naux, share, nsq + share * ntno)
    new = swap(new.astype(BF), "aux").astype(F32)
    last = new[:, :, nsq:].transpose(1, 0, 2).reshape(1, share, nsq)
    triples_new = jnp.concatenate([new[:, :, :nsq], last], axis=0)
    gains = jnp.broadcast_to(gain.astype(BF)[None], (naux, pdev * chunk, 128))
    gains = swap(gains, "aux").reshape(naux, pdev, prow * npno).transpose(1, 0, 2)
    pairs_new = pair_amps.astype(F32) + gains.reshape(pdev, npno * npno).astype(F32)
    return triples_new, pairs_new


def solution(mesh):
    in_specs = (
        P("trip", "aux", None),
        P("trip", "aux", None),
        P("trip", None, None, None),
        P("trip", None),
        P("trip", None),
        P("trip"),
        P("trip", "aux", None),
        P("trip", None),
        P("trip", None),
        P("trip"),
        P("trip"),
        P("trip", None, None),
        P("trip", None),
    )
    out_specs = (P("trip", "aux", None), P("trip", None))
    return jax.shard_map(body, mesh=mesh, in_specs=in_specs, out_specs=out_specs, check_vma=False)
```

time: 653 us -> 282 us (0.43)
  waiting for transfers between devices: 405 us -> 82 us
  blocking collectives: 81.1 us -> 38.3 us
  starting transfers between devices: 38.8 us -> 78.8 us
  local copies, waits for them, and re-layouts: 63 us -> 33.5 us
  matrix products: 33.1 us -> 21.7 us
    psum x2 -> x0, waiting for transfers between devices: 148 us -> none  [body(): resid = lax.psum(rpart.astype(jnp.bfloat16), 'aux').astype(jnp.float32)]
    unnamed x8 -> x2, waiting for transfers between devices: 148 us -> 22.2 us
    all_gather x2 -> x0, waiting for transfers between devices: 68.5 us -> none  [body(): lax.all_gather(state.astype(jnp.bfloat16), 'aux', axis=1, tiled=True)]
    all_to_all x2 -> x3, blocking collectives: 81.1 us -> 38.3 us  [swap(): return lax.all_to_all(x, axis, split_axis=0, concat_axis=0, tiled=True)]
    all_to_all x3 -> x9, starting transfers between devices: 38.1 us -> 78.8 us  [swap(): return lax.all_to_all(x, axis, split_axis=0, concat_axis=0, tiled=True)]
    reshape x7 -> x16, local copies, waits for them, and re-layouts: 30.7 us -> 6.73 us  [the longest x3 3.33 us: integral_matrix(): rows[:nsq].reshape(ntno, ntno, 3, ntno).transpose(2, 0, 1, 3)]
    all_to_all x3 -> x9, waiting for transfers between devices: 40.1 us -> 59.8 us  [swap(): return lax.all_to_all(x, axis, split_axis=0, concat_axis=0, tiled=True)]
    transpose x1 -> x5, local copies, waits for them, and re-layouts: 16.1 us -> 2.59 us  [the longest x1 2.15 us: integral_blocks(): full[naux].reshape(ntno, naux, ntno // naux, 3 * ntno).transpose(1, 2, 0, 3)]
  transfers between devices with their start and end apart: 9 -> 10, of which waited for: 8 -> 8; matrix products, arithmetic and copies ran while one was open for 9% -> 15% of each run, Pallas kernels for 0% -> 0%
where the time goes in v1:
time: 282 us; the launch traced here: 280 us
  waiting for transfers between devices  82 us (29%)
  starting transfers between devices  78.8 us (28%)
  blocking collectives  38.3 us (14%)
  local copies, waits for them, and re-layouts  33.5 us (12%)
  matrix products  21.7 us (8%)
  between operations  14.8 us (5%)
  other arithmetic  11.1 us (4%)
    all_to_all x9, starting transfers between devices, swap(): return lax.all_to_all(x, axis, split_axis=0, concat_axis=0, tiled=True)  78.8 us
    all_to_all x9, waiting for transfers between devices, swap(): return lax.all_to_all(x, axis, split_axis=0, concat_axis=0, tiled=True)  59.8 us
    all_to_all x3, blocking collectives, swap(): return lax.all_to_all(x, axis, split_axis=0, concat_axis=0, tiled=True)  38.3 us
    unnamed x2, waiting for transfers between devices  22.2 us
    dot_general x12, matrix products, mm(): return jnp.dot(x, y, preferred_element_type=F32)  9.72 us
  transfers between devices with their start and end apart: 10, of which 8 were waited for; matrix products, arithmetic and copies ran while one was open for 15% of the time, Pallas kernels for 0%

profile of v1, /device:TPU:1, one launch (start us, length us, event | category | flops | bytes accessed | tf_op | source)
XLA Modules:
  0.0 280.1 jit_solution(8012456665554141606)
XLA Ops:
  9.8 19.1 %all-to-all-start.1 = ((s32[64,1,1]{2,1,0:T(1,128)}), s32[64,1,1]{2,1,0:T(1,128)S(1)}, u32[]{:S(2)}, u32[]{:S(2)}) async-start(s32[64,1,1]{2,1,0:T(1,128)} %copy.123), calls=%async_computation.1 | async-start | bytes 65536 | tf_op jit(solution)/shard_map/all_to_all | solution.py:17
  28.9 4.4 %convolution_convert_fusion = bf16[9,1600,120]{1,2,0:T(8,128)(2,1)S(1)} fusion(bf16[9,128,1600]{1,2,0:T(8,128)(2,1)} %param.13, bf16[9,128,120]{1,2,0:T(8,128)(2,1)S(1)} %copy-done), kind=kOutput, calls=%fused_computation | convolution fusion | flops 444096000 | bytes 7418880 | tf_op jit(solution)/shard_map/tqx,tqy->txy/dot_general | solution.py:24
  34.4 1.9 copy.125
  36.3 2.0 reshape_squeeze.7
  38.4 2.1 copy.126
  40.5 2.0 copy.127
  42.5 3.3 %pad_maximum_fusion = bf16[8,1800,120]{1,2,0:T(8,128)(2,1)} fusion(bf16[8,200,120]{1,2,0:T(8,128)(2,1)} %copy.127, bf16[8,1600,120]{1,2,0:T(8,128)(2,1)S(1)} %slice.82), kind=kLoop, calls=%fused_computation.1 | loop fusion | flops 6912000 | bytes 6912000 | tf_op jit(solution)/shard_map/concatenate | solution.py:29
  50.6 1.2 multiply_reduce_fusion
  51.8 1.2 compare_reduce_fusion
  53.3 0.9 convolution_convert_fusion.4
  54.1 14.5 %all-to-all-start.2 = ((bf16[64,4,128]{2,1,0:T(4,128)(2,1)}), bf16[64,4,128]{2,1,0:T(4,128)(2,1)S(1)}, u32[]{:S(2)}, u32[]{:S(2)}) async-start(bf16[64,4,128]{2,1,0:T(4,128)(2,1)} %bitcast.3), calls=%async_computation.2 | async-start | bytes 131072 | tf_op jit(solution)/shard_map/all_to_all | solution.py:17
  69.8 12.9 %all-to-all-done.2 = bf16[64,4,128]{2,1,0:T(4,128)(2,1)S(1)} async-done(((bf16[64,4,128]{2,1,0:T(4,128)(2,1)}), bf16[64,4,128]{2,1,0:T(4,128)(2,1)S(1)}, u32[]{:S(2)}, u32[]{:S(2)}) %all-to-all-start.2) | async-done | bytes 65568 | tf_op jit(solution)/shard_map/all_to_all | solution.py:17
  82.7 7.2 %all-to-all-start = ((bf16[8,5,1800]{2,1,0:T(8,128)(2,1)}), bf16[8,5,1800]{2,1,0:T(8,128)(2,1)S(1)}, u32[]{:S(2)}, u32[]{:S(2)}) async-start(bf16[8,5,1800]{2,1,0:T(8,128)(2,1)} %pad_maximum_fusion.2), calls=%async_computation | async-start | bytes 491520 | tf_op jit(solution)/shard_map/all_to_all | solution.py:17
  89.9 0.8 convolution_convert_fusion.10
  90.7 5.5 %all-to-all-done = bf16[8,5,1800]{2,1,0:T(8,128)(2,1)S(1)} async-done(((bf16[8,5,1800]{2,1,0:T(8,128)(2,1)}), bf16[8,5,1800]{2,1,0:T(8,128)(2,1)S(1)}, u32[]{:S(2)}, u32[]{:S(2)}) %all-to-all-start) | async-done | bytes 144032 | tf_op jit(solution)/shard_map/all_to_all | solution.py:17
  96.2 4.3 %all-to-all-start.3 = ((bf16[8,24,128]{2,1,0:T(8,128)(2,1)}), bf16[8,24,128]{2,1,0:T(8,128)(2,1)S(1)}, u32[]{:S(2)}, u32[]{:S(2)}) async-start(bf16[8,24,128]{2,1,0:T(8,128)(2,1)} %bitcast.5), calls=%async_computation.3 | async-start | bytes 98304 | tf_op jit(solution)/shard_map/all_to_all | solution.py:17
  103.5 1.0 add.279
  104.8 1.0 and.135
  106.5 1.3 dynamic-slice.1
  108.8 1.7 convolution_convert_fusion.17
  110.5 1.7 convolution_convert_fusion.15
  112.2 22.2 %all-reduce.3.cloned.1.call-done = bf16[8,1800,120]{1,2,0:T(8,128)(2,1)} async-done(((bf16[8,1800,120]{1,2,0:T(8,128)(2,1)}), bf16[8,1800,120]{1,2,0:T(8,128)(2,1)}) %all-reduce.3.cloned.1.call-update) | async-done | bytes 3456016
  134.3 1.6 constant_dynamic-slice_fusion.6
  136.6 1.7 constant_dynamic-slice_fusion.5
  138.2 1.1 reshape.446
  139.3 1.4 copy.128
  140.8 0.9 dot_general.109
  141.7 0.9 reshape.447
  142.7 1.6 fusion.12
  144.6 0.9 fusion.52
  145.9 1.8 fusion.3
  148.6 10.0 %all_to_all.61 = bf16[8,24,128]{2,1,0:T(8,128)(2,1)S(1)} all-to-all(bf16[8,24,128]{2,1,0:T(8,128)(2,1)S(1)} %copy.139), channel_id=1, replica_groups=mesh['trip'=64,'aux'=8] {'aux'}, dimensions={0} | all-to-all | bytes 98304 | tf_op jit(solution)/shard_map/all_to_all | solution.py:17
  158.6 1.0 convolution_convert_fusion.3
  159.6 15.3 %all-to-all-start.5 = ((bf16[64,4,128]{2,1,0:T(4,128)(2,1)}), bf16[64,4,128]{2,1,0:T(4,128)(2,1)S(1)}, u32[]{:S(2)}, u32[]{:S(2)}) async-start(bf16[64,4,128]{2,1,0:T(4,128)(2,1)} %bitcast.35), calls=%async_computation.5 | async-start | bytes 131072 | tf_op jit(solution)/shard_map/all_to_all | solution.py:17
  175.1 13.8 %all-to-all-done.5 = bf16[64,4,128]{2,1,0:T(4,128)(2,1)S(1)} async-done(((bf16[64,4,128]{2,1,0:T(4,128)(2,1)}), bf16[64,4,128]{2,1,0:T(4,128)(2,1)S(1)}, u32[]{:S(2)}, u32[]{:S(2)}) %all-to-all-start.5) | async-done | bytes 65568 | tf_op jit(solution)/shard_map/all_to_all | solution.py:17
  189.4 17.9 %all_to_all.62 = bf16[64,4,128]{2,1,0:T(4,128)(2,1)S(1)} all-to-all(bf16[64,4,128]{2,1,0:T(4,128)(2,1)S(1)} %bitcast.181), channel_id=1, replica_groups=mesh['trip'=64,'aux'=8] {'trip'}, dimensions={0} | all-to-all | bytes 131072 | tf_op jit(solution)/shard_map/all_to_all | solution.py:17
  207.5 10.5 %all_to_all.63 = bf16[8,24,128]{2,1,0:T(8,128)(2,1)S(1)} all-to-all(bf16[8,24,128]{2,1,0:T(8,128)(2,1)S(1)} %bitcast.192), channel_id=1, replica_groups=mesh['trip'=64,'aux'=8] {'aux'}, dimensions={0} | all-to-all | bytes 98304 | tf_op jit(solution)/shard_map/all_to_all | solution.py:17
  219.5 0.9 fusion.4
  222.6 4.0 %all-to-all-start.9 = ((bf16[8,24,128]{2,1,0:T(8,128)(2,1)}), bf16[8,24,128]{2,1,0:T(8,128)(2,1)S(1)}, u32[]{:S(2)}, u32[]{:S(2)}) async-start(bf16[8,24,128]{2,1,0:T(8,128)(2,1)} %copy.147), calls=%async_computation.9 | async-start | bytes 98304 | tf_op jit(solution)/shard_map/all_to_all | solution.py:17
  227.5 4.0 %all-to-all-done.9 = bf16[8,24,128]{2,1,0:T(8,128)(2,1)S(1)} async-done(((bf16[8,24,128]{2,1,0:T(8,128)(2,1)}), bf16[8,24,128]{2,1,0:T(8,128)(2,1)S(1)}, u32[]{:S(2)}, u32[]{:S(2)}) %all-to-all-start.9) | async-done | bytes 49184 | tf_op jit(solution)/shard_map/all_to_all | solution.py:17
  231.5 4.1 %all-to-all-start.8 = ((bf16[8,5,1800]{2,1,0:T(8,128)(2,1)}), bf16[8,5,1800]{2,1,0:T(8,128)(2,1)S(1)}, u32[]{:S(2)}, u32[]{:S(2)}) async-start(bf16[8,5,1800]{2,1,0:T(8,128)(2,1)} %convert_element_type.151), calls=%async_computation.8 | async-start | bytes 491520 | tf_op jit(solution)/shard_map/all_to_all | solution.py:17
  235.5 1.0 convolution_convert_fusion.1
  236.5 5.4 %all-to-all-done.8 = bf16[8,5,1800]{2,1,0:T(8,128)(2,1)S(1)} async-done(((bf16[8,5,1800]{2,1,0:T(8,128)(2,1)}), bf16[8,5,1800]{2,1,0:T(8,128)(2,1)S(1)}, u32[]{:S(2)}, u32[]{:S(2)}) %all-to-all-start.8) | async-done | bytes 144032 | tf_op jit(solution)/shard_map/all_to_all | solution.py:17
  241.9 4.6 %all-to-all-start.10 = ((bf16[64,4,128]{2,1,0:T(4,128)(2,1)}), bf16[64,4,128]{2,1,0:T(4,128)(2,1)S(1)}, u32[]{:S(2)}, u32[]{:S(2)}) async-start(bf16[64,4,128]{2,1,0:T(4,128)(2,1)} %bitcast.55), calls=%async_computation.10 | async-start | bytes 131072 | tf_op jit(solution)/shard_map/all_to_all | solution.py:17
  246.8 13.7 %all-to-all-done.10 = bf16[64,4,128]{2,1,0:T(4,128)(2,1)S(1)} async-done(((bf16[64,4,128]{2,1,0:T(4,128)(2,1)}), bf16[64,4,128]{2,1,0:T(4,128)(2,1)S(1)}, u32[]{:S(2)}, u32[]{:S(2)}) %all-to-all-start.10) | async-done | bytes 65568 | tf_op jit(solution)/shard_map/all_to_all | solution.py:17
  261.5 5.7 %all-to-all-start.11 = ((bf16[8,64,128]{2,1,0:T(8,128)(2,1)}), bf16[8,64,128]{2,1,0:T(8,128)(2,1)S(1)}, u32[]{:S(2)}, u32[]{:S(2)}) async-start(bf16[8,64,128]{2,1,0:T(8,128)(2,1)} %broadcast_in_dim.92), calls=%async_computation.11 | async-start | bytes 262144 | tf_op jit(solution)/shard_map/all_to_all | solution.py:17
  267.2 0.8 pad_maximum_fusion.1
  268.0 4.5 %all-to-all-done.11 = bf16[8,64,128]{2,1,0:T(8,128)(2,1)S(1)} async-done(((bf16[8,64,128]{2,1,0:T(8,128)(2,1)}), bf16[8,64,128]{2,1,0:T(8,128)(2,1)S(1)}, u32[]{:S(2)}, u32[]{:S(2)}) %all-to-all-start.11) | async-done | bytes 131104 | tf_op jit(solution)/shard_map/all_to_all | solution.py:17
  (145 shorter events, 24.3 us)
Async XLA Ops:
  7.2 21.8 %copy-start = (bf16[9,128,120]{1,2,0:T(8,128)(2,1)S(1)}, bf16[9,128,120]{1,2,0:T(8,128)(2,1)}, u32[]{:S(2)}) copy-start(bf16[9,128,120]{1,2,0:T(8,128)(2,1)} %param.14) | copy-start | bytes 829444
  9.8 40.9 %all-to-all-start.1 = ((s32[64,1,1]{2,1,0:T(1,128)}), s32[64,1,1]{2,1,0:T(1,128)S(1)}, u32[]{:S(2)}, u32[]{:S(2)}) async-start(s32[64,1,1]{2,1,0:T(1,128)} %copy.123), calls=%async_computation.1 | async-start | bytes 65536 | tf_op jit(solution)/shard_map/all_to_all | solution.py:17
  28.9 105.5 %all-reduce.3.cloned.1.call-start = ((), (), s32[]{:S(2)}) async-start(), calls=%async_computation.12 | async-start | bytes 7372800
  45.8 0.7 copy-start.17
  45.8 1.7 copy-start.12
  45.8 23.0 %copy-start.2 = (f32[9,5,1600]{2,1,0:T(8,128)S(1)}, f32[9,5,1600]{2,1,0:T(8,128)}, u32[]{:S(2)}) copy-start(f32[9,5,1600]{2,1,0:T(8,128)} %param.19) | copy-start | bytes 864004
  45.8 23.2 %copy-start.11 = (f32[9,3]{0,1:T(4,128)S(1)}, f32[9,3]{0,1:T(4,128)}, u32[]{:S(2)}) copy-start(f32[9,3]{0,1:T(4,128)} %param.17) | copy-start | bytes 328
  46.8 49.5 %copy-start.14 = (s32[192]{0:T(256)}, s32[192]{0:T(256)S(1)}, u32[]{:S(2)}) copy-start(s32[192]{0:T(256)S(1)} %fusion.103) | copy-start | bytes 2308
  54.1 28.5 %all-to-all-start.2 = ((bf16[64,4,128]{2,1,0:T(4,128)(2,1)}), bf16[64,4,128]{2,1,0:T(4,128)(2,1)S(1)}, u32[]{:S(2)}, u32[]{:S(2)}) async-start(bf16[64,4,128]{2,1,0:T(4,128)(2,1)} %bitcast.3), calls=%async_computation.2 | async-start | bytes 131072 | tf_op jit(solution)/shard_map/all_to_all | solution.py:17
  82.7 13.6 %all-to-all-start = ((bf16[8,5,1800]{2,1,0:T(8,128)(2,1)}), bf16[8,5,1800]{2,1,0:T(8,128)(2,1)S(1)}, u32[]{:S(2)}, u32[]{:S(2)}) async-start(bf16[8,5,1800]{2,1,0:T(8,128)(2,1)} %pad_maximum_fusion.2), calls=%async_computation | async-start | bytes 491520 | tf_op jit(solution)/shard_map/all_to_all | solution.py:17
  96.2 12.4 %all-to-all-start.3 = ((bf16[8,24,128]{2,1,0:T(8,128)(2,1)}), bf16[8,24,128]{2,1,0:T(8,128)(2,1)S(1)}, u32[]{:S(2)}, u32[]{:S(2)}) async-start(bf16[8,24,128]{2,1,0:T(8,128)(2,1)} %bitcast.5), calls=%async_computation.3 | async-start | bytes 98304 | tf_op jit(solution)/shard_map/all_to_all | solution.py:17
  140.7 4.8 %copy-start.1 = (bf16[9,3,64,40]{2,3,1,0:T(8,128)(2,1)S(1)}, bf16[9,3,64,40]{2,3,1,0:T(8,128)(2,1)}, u32[]{:S(2)}) copy-start(bf16[9,3,64,40]{2,3,1,0:T(8,128)(2,1)} %param.15) | copy-start | bytes 414724
  140.7 5.1 %copy-start.3 = (f32[40,1800]{1,0:T(8,128)S(1)}, f32[40,1800]{1,0:T(8,128)}, u32[]{:S(2)}) copy-start(f32[40,1800]{1,0:T(8,128)} %reshape.468) | copy-start | bytes 864004
  140.8 5.1 %copy-start.6 = (pred[40,1600]{1,0:T(8,128)(4,1)S(1)}, pred[40,1600]{1,0:T(8,128)(4,1)}, u32[]{:S(2)}) copy-start(pred[40,1600]{1,0:T(8,128)(4,1)} %and.135) | copy-start | bytes 192004
  140.8 5.1 %copy-start.9 = (bf16[3,40,40]{2,1,0:T(8,128)(2,1)S(1)}, bf16[3,40,40]{2,1,0:T(8,128)(2,1)}, u32[]{:S(2)}) copy-start(bf16[3,40,40]{2,1,0:T(8,128)(2,1)} %convolution_convert_fusion.17) | copy-start | bytes 28804
  140.8 5.1 %copy-start.10 = (pred[1600]{0:T(1024)(128)(4,1)S(1)}, pred[1600]{0:T(1024)(128)(4,1)}, u32[]{:S(2)}) copy-start(pred[1600]{0:T(1024)(128)(4,1)} %and.136) | copy-start | bytes 4804
  140.8 17.8 %copy-start.15 = (s32[192]{0:T(256)S(1)}, s32[192]{0:T(256)}, u32[]{:S(2)}) copy-start(s32[192]{0:T(256)} %copy-done.14) | copy-start | bytes 2308
  140.8 34.0 %copy-start.8 = (f32[16,64]{1,0:T(8,128)S(1)}, f32[16,64]{1,0:T(8,128)}, u32[]{:S(2)}) copy-start(f32[16,64]{1,0:T(8,128)} %param.21) | copy-start | bytes 12292
  140.8 34.1 %copy-start.16 = (f32[16]{0:T(128)S(1)}, f32[16]{0:T(128)}, u32[]{:S(2)}) copy-start(f32[16]{0:T(128)} %param.22) | copy-start | bytes 196
  141.7 76.7 %copy-start.13 = (f32[200]{0:T(256)S(1)}, f32[200]{0:T(256)}, u32[]{:S(2)}) copy-start(f32[200]{0:T(256)} %add.295) | copy-start | bytes 2404
  141.7 76.7 %copy-start.18 = (pred[200]{0:T(512)(128)(4,1)S(1)}, pred[200]{0:T(512)(128)(4,1)}, u32[]{:S(2)}) copy-start(pred[200]{0:T(512)(128)(4,1)} %and.153) | copy-start | bytes 604
  142.6 75.8 %copy-start.7 = (f32[40,200]{1,0:T(8,128)S(1)}, f32[40,200]{1,0:T(8,128)}, u32[]{:S(2)}) copy-start(f32[40,200]{1,0:T(8,128)} %copy.134) | copy-start | bytes 96004
  142.6 76.9 %copy-start.4 = (f32[40,1600]{1,0:T(8,128)S(1)}, f32[40,1600]{1,0:T(8,128)}, u32[]{:S(2)}) copy-start(f32[40,1600]{1,0:T(8,128)} %add.279) | copy-start | bytes 768004
  159.6 29.4 %all-to-all-start.5 = ((bf16[64,4,128]{2,1,0:T(4,128)(2,1)}), bf16[64,4,128]{2,1,0:T(4,128)(2,1)S(1)}, u32[]{:S(2)}, u32[]{:S(2)}) async-start(bf16[64,4,128]{2,1,0:T(4,128)(2,1)} %bitcast.35), calls=%async_computation.5 | async-start | bytes 131072 | tf_op jit(solution)/shard_map/all_to_all | solution.py:17
  221.1 51.5 %copy-start.5 = (bf16[16,4096]{1,0:T(8,128)(2,1)S(1)}, bf16[16,4096]{1,0:T(8,128)(2,1)}, u32[]{:S(2)}) copy-start(bf16[16,4096]{1,0:T(8,128)(2,1)} %param.20) | copy-start | bytes 393220
  222.6 8.8 %all-to-all-start.9 = ((bf16[8,24,128]{2,1,0:T(8,128)(2,1)}), bf16[8,24,128]{2,1,0:T(8,128)(2,1)S(1)}, u32[]{:S(2)}, u32[]{:S(2)}) async-start(bf16[8,24,128]{2,1,0:T(8,128)(2,1)} %copy.147), calls=%async_computation.9 | async-start | bytes 98304 | tf_op jit(solution)/shard_map/all_to_all | solution.py:17
  231.5 10.4 %all-to-all-start.8 = ((bf16[8,5,1800]{2,1,0:T(8,128)(2,1)}), bf16[8,5,1800]{2,1,0:T(8,128)(2,1)S(1)}, u32[]{:S(2)}, u32[]{:S(2)}) async-start(bf16[8,5,1800]{2,1,0:T(8,128)(2,1)} %convert_element_type.151), calls=%async_computation.8 | async-start | bytes 491520 | tf_op jit(solution)/shard_map/all_to_all | solution.py:17
  241.9 18.6 %all-to-all-start.10 = ((bf16[64,4,128]{2,1,0:T(4,128)(2,1)}), bf16[64,4,128]{2,1,0:T(4,128)(2,1)S(1)}, u32[]{:S(2)}, u32[]{:S(2)}) async-start(bf16[64,4,128]{2,1,0:T(4,128)(2,1)} %bitcast.55), calls=%async_computation.10 | async-start | bytes 131072 | tf_op jit(solution)/shard_map/all_to_all | solution.py:17
  261.5 11.0 %all-to-all-start.11 = ((bf16[8,64,128]{2,1,0:T(8,128)(2,1)}), bf16[8,64,128]{2,1,0:T(8,128)(2,1)S(1)}, u32[]{:S(2)}, u32[]{:S(2)}) async-start(bf16[8,64,128]{2,1,0:T(8,128)(2,1)} %broadcast_in_dim.92), calls=%async_computation.11 | async-start | bytes 262144 | tf_op jit(solution)/shard_map/all_to_all | solution.py:17
Sparse Core Ops, SparseCore 0:
  45.9 88.3 all-reduce.2

commit v2 on v1

--- a/solution.py
+++ b/solution.py
@@ -19,21 +19,24 @@
 
 def integral_blocks(aux_blocks, occ_blocks):
     naux = lax.axis_size("aux")
-    tdev, _, nsq = aux_blocks.shape
+    nsq = aux_blocks.shape[2]
     ntno = occ_blocks.shape[2] // 3
+    share = ntno // naux
     full = jnp.einsum(
-        "tqx,tqy->txy", aux_blocks, occ_blocks, preferred_element_type=F32
+        "tqy,tqx->tyx", occ_blocks, aux_blocks, preferred_element_type=F32
     ).astype(BF)
-    last = full[naux].reshape(ntno, naux, ntno // naux, 3 * ntno).transpose(1, 2, 0, 3)
-    last = last.reshape(naux, nsq // naux, 3 * ntno)
-    return jnp.concatenate([full[:naux], last], axis=1)
+    last = full[naux].reshape(3, naux, share, nsq).transpose(1, 0, 2, 3)
+    last = last.reshape(naux, 3 * share, nsq)
+    both = jnp.concatenate([full[:naux], last], axis=1)
+    return jnp.pad(both, ((0, 0), (0, -both.shape[1] % 16), (0, -nsq % 128)))
 
 
 def integral_matrix(rows, ntno, share):
     nsq = ntno * ntno
-    own = rows[:nsq].reshape(ntno, ntno, 3, ntno).transpose(2, 0, 1, 3).reshape(3 * ntno, nsq)
-    last = rows[nsq:].reshape(share, ntno, 3, ntno).transpose(2, 1, 0, 3)
-    return own, last.reshape(3 * ntno, share * ntno)
+    rows = rows[: 3 * (ntno + share), :nsq].reshape(3 * (ntno + share), ntno, ntno)
+    own = rows[: 3 * ntno].reshape(3, ntno, ntno, ntno).transpose(0, 2, 3, 1)
+    last = rows[3 * ntno :].reshape(3, share, ntno, ntno).transpose(0, 2, 3, 1)
+    return own.reshape(3 * ntno, nsq), last.reshape(3 * ntno, share * ntno)
 
 
 def body(
@@ -68,11 +71,9 @@
 
     placed = owner[:, None] == jnp.arange(ntrip)[None, :]
     wanted = jnp.sum(jnp.where(placed, local[:, None] + 1, 0), axis=0) - 1
+    blocks, wanted = lax.optimization_barrier((integral_blocks(aux_blocks, occ_blocks), wanted))
+    rows = lax.psum_scatter(blocks, "aux", scatter_dimension=0, tiled=True)[0]
     asked = swap(wanted.reshape(ntrip, 1), "trip")
-
-    rows = lax.psum_scatter(
-        integral_blocks(aux_blocks, occ_blocks), "aux", scatter_dimension=0, tiled=True
-    )[0]
 
     number = jnp.arange(naux * 6 * chunk)
     dest, k, piece = number // (6 * chunk), (number // chunk) % 6, number % chunk
@@ -108,7 +109,8 @@
         return lax.dynamic_slice_in_dim(x, member, 1, 0)[0], x[naux]
 
     old = triples_old.astype(BF)
-    old_last = old[naux].reshape(share, naux, share * ntno).transpose(1, 0, 2)
+    old_last = old[naux].reshape(share, ntno, naux, share).transpose(2, 0, 1, 3)
+    old_last = old_last.reshape(naux, share, ntno * share)
     old = swap(jnp.concatenate([old[:naux], old_last], axis=2), "aux")
     old = old.reshape(ntno, nsq + share * ntno).astype(F32)
     states = [old[:, :nsq], old[:, nsq:]]
@@ -120,14 +122,14 @@
     )
     dens, keeps = [], []
     for which in range(2):
-        e, low = energies[which], 0
+        e = energies[which]
         live_t = jnp.arange(ntno) < ranks[which]
-        e_b, live_b = e, live_t
+        e_c, live_c = e, live_t
         if which == 1:
-            e_b = lax.dynamic_slice_in_dim(e, member * share, share, 0)
-            live_b = lax.dynamic_slice_in_dim(live_t, member * share, share, 0)
-        den = e[:, None, None] + e_b[None, :, None] + e[None, None, :] - sums[which] + SHIFT_LEVEL
-        keep = live_t[:, None, None] & live_b[None, :, None] & live_t[None, None, :]
+            e_c = lax.dynamic_slice_in_dim(e, member * share, share, 0)
+            live_c = lax.dynamic_slice_in_dim(live_t, member * share, share, 0)
+        den = e[:, None, None] + e[None, :, None] + e_c[None, None, :] - sums[which] + SHIFT_LEVEL
+        keep = live_t[:, None, None] & live_t[None, :, None] & live_c[None, None, :]
         dens.append(den.reshape(ntno, -1))
         keeps.append(keep.reshape(ntno, -1))
     matrices = integral_matrix(rows, ntno, share)
@@ -166,10 +168,11 @@
         gain = gain + change
         amps = amps + change
 
-    new = jnp.concatenate(states, axis=1).reshape(naux, share, nsq + share * ntno)
-    new = swap(new.astype(BF), "aux").astype(F32)
-    last = new[:, :, nsq:].transpose(1, 0, 2).reshape(1, share, nsq)
-    triples_new = jnp.concatenate([new[:, :, :nsq], last], axis=0)
+    new = jnp.concatenate(states, axis=1).astype(BF)
+    new = lax.all_gather(new, "aux", axis=0, tiled=False)
+    new = lax.dynamic_slice_in_dim(new, member * share, share, 1).astype(F32)
+    last = new[:, :, nsq:].reshape(naux, share, ntno, share).transpose(1, 2, 0, 3)
+    triples_new = jnp.concatenate([new[:, :, :nsq], last.reshape(1, share, nsq)], axis=0)
     gains = jnp.broadcast_to(gain.astype(BF)[None], (naux, pdev * chunk, 128))
     gains = swap(gains, "aux").reshape(naux, pdev, prow * npno).transpose(1, 0, 2)
     pairs_new = pair_amps.astype(F32) + gains.reshape(pdev, npno * npno).astype(F32)

time: 282 us -> 226 us (0.80)
  waiting for transfers between devices: 82 us -> 39.7 us
  starting transfers between devices: 78.8 us -> 40.7 us
  blocking collectives: 38.3 us -> 73.5 us
  local copies, waits for them, and re-layouts: 33.5 us -> 25.6 us
  matrix products: 21.7 us -> 17.7 us
    all_to_all x9 -> x5, starting transfers between devices: 78.8 us -> 40.7 us  [swap(): return lax.all_to_all(x, axis, split_axis=0, concat_axis=0, tiled=True)]
    all_to_all x3 -> x6, blocking collectives: 38.3 us -> 73.5 us  [swap(): return lax.all_to_all(x, axis, split_axis=0, concat_axis=0, tiled=True)]
    unnamed x2, waiting for transfers between devices: 22.2 us -> 0.03 us
    all_to_all x9 -> x5, waiting for transfers between devices: 59.8 us -> 39.6 us  [swap(): return lax.all_to_all(x, axis, split_axis=0, concat_axis=0, tiled=True)]
    slice x8, local copies, waits for them, and re-layouts: 6.38 us -> 2.98 us  [the longest x1 1.03 us: integral_matrix(): own = rows[:3 * ntno].reshape(3, ntno, ntno, ntno).transpose(0, 2, 3, 1)]
    reshape x7 -> x11, local copies, waits for them, and re-layouts: 5.66 us -> 5.73 us  [the longest x2 2.48 us: integral_matrix(): own = rows[:3 * ntno].reshape(3, ntno, ntno, ntno).transpose(0, 2, 3, 1)]
  transfers between devices with their start and end apart: 10 -> 7, of which waited for: 8 -> 4; matrix products, arithmetic and copies ran while one was open for 15% -> 10% of each run, Pallas kernels for 0% -> 0%
where the time goes in v2:
time: 226 us; the launch traced here: 225 us
  blocking collectives  73.5 us (33%)
  starting transfers between devices  40.7 us (18%)
  waiting for transfers between devices  39.7 us (18%)
  local copies, waits for them, and re-layouts  25.6 us (11%)
  matrix products  17.7 us (8%)
  between operations  14.9 us (7%)
  other arithmetic  13 us (6%)
    all_to_all x6, blocking collectives, swap(): return lax.all_to_all(x, axis, split_axis=0, concat_axis=0, tiled=True)  73.5 us
    all_to_all x5, starting transfers between devices, swap(): return lax.all_to_all(x, axis, split_axis=0, concat_axis=0, tiled=True)  40.7 us
    all_to_all x5, waiting for transfers between devices, swap(): return lax.all_to_all(x, axis, split_axis=0, concat_axis=0, tiled=True)  39.6 us
    dot_general x12, matrix products, mm(): return jnp.dot(x, y, preferred_element_type=F32)  8.09 us
  transfers between devices with their start and end apart: 7, of which 4 were waited for; matrix products, arithmetic and copies ran while one was open for 10% of the time, Pallas kernels for 0%

profile of v2, /device:TPU:1, one launch (start us, length us, event | category | flops | bytes accessed | tf_op | source)
XLA Modules:
  0.0 225.0 jit_solution(1990891425580457731)
XLA Ops:
  7.2 0.9 copy-done
  8.1 4.4 %convolution_convert_fusion = bf16[9,120,1600]{2,1,0:T(8,128)(2,1)S(1)} fusion(bf16[9,128,120]{1,2,0:T(8,128)(2,1)S(1)} %copy-done, bf16[9,128,1600]{1,2,0:T(8,128)(2,1)} %param.13), kind=kOutput, calls=%fused_computation.7 | convolution fusion | flops 444096000 | bytes 7418880 | tf_op jit(solution)/shard_map/tqy,tqx->tyx/dot_general | solution.py:25
  12.5 0.8 slice.85
  13.5 2.0 reshape_squeeze.7
  15.6 1.1 copy.124
  16.7 0.8 copy.125
  18.0 4.1 %fusion.5 = bf16[8,144,1664]{2,1,0:T(8,128)(2,1)} fusion(bf16[8,15,1600]{2,1,0:T(8,128)(2,1)} %copy.125, bf16[8,120,1600]{2,1,0:T(8,128)(2,1)S(1)} %slice.84), kind=kLoop, calls=%fused_computation.8 | loop fusion | flops 21086208 | bytes 7289856 | tf_op jit(solution)/shard_map/concatenate | solution.py:30
  22.8 19.1 %all-to-all-start.1 = ((s32[64,1,1]{2,1,0:T(1,128)}), s32[64,1,1]{2,1,0:T(1,128)S(1)}, u32[]{:S(2)}, u32[]{:S(2)}) async-start(s32[64,1,1]{2,1,0:T(1,128)} %copy.127), calls=%async_computation.1 | async-start | bytes 65536 | tf_op jit(solution)/shard_map/all_to_all | solution.py:17
  46.2 9.1 %all-to-all-done.1 = s32[64,1,1]{2,1,0:T(1,128)S(1)} async-done(((s32[64,1,1]{2,1,0:T(1,128)}), s32[64,1,1]{2,1,0:T(1,128)S(1)}, u32[]{:S(2)}, u32[]{:S(2)}) %all-to-all-start.1) | async-done | bytes 288 | tf_op jit(solution)/shard_map/all_to_all | solution.py:17
  55.3 1.2 multiply_reduce_fusion
  56.5 1.2 compare_reduce_fusion
  58.0 0.9 convolution_convert_fusion.4
  58.8 5.4 %all-to-all-start.2 = ((bf16[64,4,128]{2,1,0:T(4,128)(2,1)}), bf16[64,4,128]{2,1,0:T(4,128)(2,1)S(1)}, u32[]{:S(2)}, u32[]{:S(2)}) async-start(bf16[64,4,128]{2,1,0:T(4,128)(2,1)} %bitcast.5), calls=%async_computation.2 | async-start | bytes 131072 | tf_op jit(solution)/shard_map/all_to_all | solution.py:17
  65.0 0.8 reshape_squeeze.6
  66.2 0.8 pad_maximum_fusion.1
  66.9 11.3 %all-to-all-done.2 = bf16[64,4,128]{2,1,0:T(4,128)(2,1)S(1)} async-done(((bf16[64,4,128]{2,1,0:T(4,128)(2,1)}), bf16[64,4,128]{2,1,0:T(4,128)(2,1)S(1)}, u32[]{:S(2)}, u32[]{:S(2)}) %all-to-all-start.2) | async-done | bytes 65568 | tf_op jit(solution)/shard_map/all_to_all | solution.py:17
  78.3 7.2 %all-to-all-start = ((bf16[8,5,1800]{2,1,0:T(8,128)(2,1)}), bf16[8,5,1800]{2,1,0:T(8,128)(2,1)S(1)}, u32[]{:S(2)}, u32[]{:S(2)}) async-start(bf16[8,5,1800]{2,1,0:T(8,128)(2,1)} %pad_maximum_fusion.1), calls=%async_computation | async-start | bytes 491520 | tf_op jit(solution)/shard_map/all_to_all | solution.py:17
  85.5 0.8 convolution_convert_fusion.10
  86.3 5.5 %all-to-all-done = bf16[8,5,1800]{2,1,0:T(8,128)(2,1)S(1)} async-done(((bf16[8,5,1800]{2,1,0:T(8,128)(2,1)}), bf16[8,5,1800]{2,1,0:T(8,128)(2,1)S(1)}, u32[]{:S(2)}, u32[]{:S(2)}) %all-to-all-start) | async-done | bytes 144032 | tf_op jit(solution)/shard_map/all_to_all | solution.py:17
  91.9 4.3 %all-to-all-start.3 = ((bf16[8,24,128]{2,1,0:T(8,128)(2,1)}), bf16[8,24,128]{2,1,0:T(8,128)(2,1)S(1)}, u32[]{:S(2)}, u32[]{:S(2)}) async-start(bf16[8,24,128]{2,1,0:T(8,128)(2,1)} %bitcast.7), calls=%async_computation.3 | async-start | bytes 98304 | tf_op jit(solution)/shard_map/all_to_all | solution.py:17
  98.2 1.0 add.273
  99.5 1.0 and.135
  101.2 0.8 reshape.499
  102.2 0.9 convolution_convert_fusion.17
  103.1 0.9 convolution_convert_fusion.15
  104.0 0.8 slice.90
  104.8 1.0 slice.87
  105.8 1.1 reshape.476
  106.9 1.4 copy.129
  108.4 0.9 dot_general.109
  109.2 0.9 reshape.477
  111.0 0.8 fusion.18
  112.5 1.7 fusion.9
  115.1 9.4 %all_to_all.59 = bf16[8,24,128]{2,1,0:T(8,128)(2,1)S(1)} all-to-all(bf16[8,24,128]{2,1,0:T(8,128)(2,1)S(1)} %copy.139), channel_id=1, replica_groups=mesh['trip'=64,'aux'=8] {'aux'}, dimensions={0} | all-to-all | bytes 98304 | tf_op jit(solution)/shard_map/all_to_all | solution.py:17
  124.5 1.0 convolution_convert_fusion.3
  125.5 4.6 %all-to-all-start.5 = ((bf16[64,4,128]{2,1,0:T(4,128)(2,1)}), bf16[64,4,128]{2,1,0:T(4,128)(2,1)S(1)}, u32[]{:S(2)}, u32[]{:S(2)}) async-start(bf16[64,4,128]{2,1,0:T(4,128)(2,1)} %bitcast.34), calls=%async_computation.6 | async-start | bytes 131072 | tf_op jit(solution)/shard_map/all_to_all | solution.py:17
  130.4 13.7 %all-to-all-done.5 = bf16[64,4,128]{2,1,0:T(4,128)(2,1)S(1)} async-done(((bf16[64,4,128]{2,1,0:T(4,128)(2,1)}), bf16[64,4,128]{2,1,0:T(4,128)(2,1)S(1)}, u32[]{:S(2)}, u32[]{:S(2)}) %all-to-all-start.5) | async-done | bytes 65568 | tf_op jit(solution)/shard_map/all_to_all | solution.py:17
  144.6 18.4 %all_to_all.60 = bf16[64,4,128]{2,1,0:T(4,128)(2,1)S(1)} all-to-all(bf16[64,4,128]{2,1,0:T(4,128)(2,1)S(1)} %bitcast.189), channel_id=1, replica_groups=mesh['trip'=64,'aux'=8] {'trip'}, dimensions={0} | all-to-all | bytes 131072 | tf_op jit(solution)/shard_map/all_to_all | solution.py:17
  163.3 10.0 %all_to_all.61 = bf16[8,24,128]{2,1,0:T(8,128)(2,1)S(1)} all-to-all(bf16[8,24,128]{2,1,0:T(8,128)(2,1)S(1)} %bitcast.200), channel_id=1, replica_groups=mesh['trip'=64,'aux'=8] {'aux'}, dimensions={0} | all-to-all | bytes 98304 | tf_op jit(solution)/shard_map/all_to_all | solution.py:17
  173.6 0.8 fusion.22
  174.7 0.9 fusion.10
  176.1 0.7 pad_maximum_fusion.2
  178.0 8.0 %all_to_all.62 = bf16[8,24,128]{2,1,0:T(8,128)(2,1)S(1)} all-to-all(bf16[8,24,128]{2,1,0:T(8,128)(2,1)S(1)} %copy.148), channel_id=1, replica_groups=mesh['trip'=64,'aux'=8] {'aux'}, dimensions={0} | all-to-all | bytes 98304 | tf_op jit(solution)/shard_map/all_to_all | solution.py:17
  186.4 17.8 %all_to_all.63 = bf16[64,4,128]{2,1,0:T(4,128)(2,1)S(1)} all-to-all(bf16[64,4,128]{2,1,0:T(4,128)(2,1)S(1)} %bitcast.196), channel_id=1, replica_groups=mesh['trip'=64,'aux'=8] {'trip'}, dimensions={0} | all-to-all | bytes 131072 | tf_op jit(solution)/shard_map/all_to_all | solution.py:17
  204.5 9.9 %all_to_all.64 = bf16[8,64,128]{2,1,0:T(8,128)(2,1)S(1)} all-to-all(bf16[8,64,128]{2,1,0:T(8,128)(2,1)S(1)} %broadcast_in_dim.92), channel_id=1, replica_groups=mesh['trip'=64,'aux'=8] {'aux'}, dimensions={0} | all-to-all | bytes 262144 | tf_op jit(solution)/shard_map/all_to_all | solution.py:17
  214.5 0.7 convert_add_fusion
  215.2 1.1 dynamic-slice_convert_fusion
  217.4 0.8 pad_maximum_fusion
  (151 shorter events, 17.5 us)
Async XLA Ops:
  7.2 1.0 copy-start
  7.2 96.8 %reduce-scatter.2.cloned.1.call-start = ((), (), s32[]{:S(2)}) async-start(), calls=%async_computation.12 | async-start | bytes 4313088 | tf_op jit(solution)/shard_map/reduce_scatter | solution.py:75
  13.3 4.2 %copy-start.10 = (s32[9,3]{0,1:T(4,128)S(1)}, s32[9,3]{0,1:T(4,128)}, u32[]{:S(2)}) copy-start(s32[9,3]{0,1:T(4,128)} %param.25) | copy-start | bytes 328
  13.3 4.4 %copy-start.12 = (s32[9,3,1]{0,2,1:T(1,128)S(1)}, s32[9,3,1]{0,2,1:T(1,128)}, u32[]{:S(2)}) copy-start(s32[9,3,1]{0,2,1:T(1,128)} %param.24) | copy-start | bytes 328
  22.1 19.9 %copy-start.11 = (s32[9]{0:T(128)S(1)}, s32[9]{0:T(128)}, u32[]{:S(2)}) copy-start(s32[9]{0:T(128)} %param.18) | copy-start | bytes 112
  22.1 21.9 %copy-start.18 = (s32[16]{0:T(128)S(1)}, s32[16]{0:T(128)}, u32[]{:S(2)}) copy-start(s32[16]{0:T(128)} %param.23) | copy-start | bytes 196
  22.1 24.1 %copy-start.9 = (f32[9,3]{0,1:T(4,128)S(1)}, f32[9,3]{0,1:T(4,128)}, u32[]{:S(2)}) copy-start(f32[9,3]{0,1:T(4,128)} %param.17) | copy-start | bytes 328
  22.1 42.9 %copy-start.2 = (f32[9,5,1600]{2,1,0:T(8,128)S(1)}, f32[9,5,1600]{2,1,0:T(8,128)}, u32[]{:S(2)}) copy-start(f32[9,5,1600]{2,1,0:T(8,128)} %param.19) | copy-start | bytes 864004
  22.8 32.5 %all-to-all-start.1 = ((s32[64,1,1]{2,1,0:T(1,128)}), s32[64,1,1]{2,1,0:T(1,128)S(1)}, u32[]{:S(2)}, u32[]{:S(2)}) async-start(s32[64,1,1]{2,1,0:T(1,128)} %copy.127), calls=%async_computation.1 | async-start | bytes 65536 | tf_op jit(solution)/shard_map/all_to_all | solution.py:17
  44.2 52.1 %copy-start.13 = (s32[192]{0:T(256)}, s32[192]{0:T(256)S(1)}, u32[]{:S(2)}) copy-start(s32[192]{0:T(256)S(1)} %fusion.109) | copy-start | bytes 2308
  58.8 19.5 %all-to-all-start.2 = ((bf16[64,4,128]{2,1,0:T(4,128)(2,1)}), bf16[64,4,128]{2,1,0:T(4,128)(2,1)S(1)}, u32[]{:S(2)}, u32[]{:S(2)}) async-start(bf16[64,4,128]{2,1,0:T(4,128)(2,1)} %bitcast.5), calls=%async_computation.2 | async-start | bytes 131072 | tf_op jit(solution)/shard_map/all_to_all | solution.py:17
  65.0 37.2 %copy-start.1 = (bf16[9,3,64,40]{2,3,1,0:T(8,128)(2,1)S(1)}, bf16[9,3,64,40]{2,3,1,0:T(8,128)(2,1)}, u32[]{:S(2)}) copy-start(bf16[9,3,64,40]{2,3,1,0:T(8,128)(2,1)} %param.15) | copy-start | bytes 414724
  78.3 13.6 %all-to-all-start = ((bf16[8,5,1800]{2,1,0:T(8,128)(2,1)}), bf16[8,5,1800]{2,1,0:T(8,128)(2,1)S(1)}, u32[]{:S(2)}, u32[]{:S(2)}) async-start(bf16[8,5,1800]{2,1,0:T(8,128)(2,1)} %pad_maximum_fusion.1), calls=%async_computation | async-start | bytes 491520 | tf_op jit(solution)/shard_map/all_to_all | solution.py:17
  91.9 10.2 %all-to-all-start.3 = ((bf16[8,24,128]{2,1,0:T(8,128)(2,1)}), bf16[8,24,128]{2,1,0:T(8,128)(2,1)S(1)}, u32[]{:S(2)}, u32[]{:S(2)}) async-start(bf16[8,24,128]{2,1,0:T(8,128)(2,1)} %bitcast.7), calls=%async_computation.3 | async-start | bytes 98304 | tf_op jit(solution)/shard_map/all_to_all | solution.py:17
  108.3 2.7 %copy-start.3 = (f32[40,1800]{1,0:T(8,128)S(1)}, f32[40,1800]{1,0:T(8,128)}, u32[]{:S(2)}) copy-start(f32[40,1800]{1,0:T(8,128)} %reshape.499) | copy-start | bytes 864004
  108.3 2.7 %copy-start.15 = (f32[200]{0:T(256)S(1)}, f32[200]{0:T(256)}, u32[]{:S(2)}) copy-start(f32[200]{0:T(256)} %add.289) | copy-start | bytes 2404
  108.3 2.7 %copy-start.19 = (pred[200]{0:T(512)(128)(4,1)S(1)}, pred[200]{0:T(512)(128)(4,1)}, u32[]{:S(2)}) copy-start(pred[200]{0:T(512)(128)(4,1)} %and.153) | copy-start | bytes 604
  108.3 2.7 %copy-start.21 = (bf16[3,40,40]{2,1,0:T(8,128)(2,1)S(1)}, bf16[3,40,40]{2,1,0:T(8,128)(2,1)}, u32[]{:S(2)}) copy-start(bf16[3,40,40]{2,1,0:T(8,128)(2,1)} %convolution_convert_fusion.15) | copy-start | bytes 28804
  108.3 4.2 %copy-start.4 = (f32[40,1600]{1,0:T(8,128)S(1)}, f32[40,1600]{1,0:T(8,128)}, u32[]{:S(2)}) copy-start(f32[40,1600]{1,0:T(8,128)} %add.273) | copy-start | bytes 768004
  108.3 4.2 %copy-start.6 = (pred[40,1600]{1,0:T(8,128)(4,1)S(1)}, pred[40,1600]{1,0:T(8,128)(4,1)}, u32[]{:S(2)}) copy-start(pred[40,1600]{1,0:T(8,128)(4,1)} %and.135) | copy-start | bytes 192004
  109.2 15.3 %copy-start.14 = (s32[192]{0:T(256)S(1)}, s32[192]{0:T(256)}, u32[]{:S(2)}) copy-start(s32[192]{0:T(256)} %copy-done.13) | copy-start | bytes 2308
  109.2 20.9 %copy-start.7 = (f32[16,64]{1,0:T(8,128)S(1)}, f32[16,64]{1,0:T(8,128)}, u32[]{:S(2)}) copy-start(f32[16,64]{1,0:T(8,128)} %param.21) | copy-start | bytes 12292
  110.1 20.1 %copy-start.17 = (f32[16]{0:T(128)S(1)}, f32[16]{0:T(128)}, u32[]{:S(2)}) copy-start(f32[16]{0:T(128)} %param.22) | copy-start | bytes 196
  110.1 63.5 %copy-start.16 = (f32[200]{0:T(256)S(1)}, f32[200]{0:T(256)}, u32[]{:S(2)}) copy-start(f32[200]{0:T(256)} %add.289) | copy-start | bytes 2404
  110.1 63.5 %copy-start.20 = (pred[200]{0:T(512)(128)(4,1)S(1)}, pred[200]{0:T(512)(128)(4,1)}, u32[]{:S(2)}) copy-start(pred[200]{0:T(512)(128)(4,1)} %and.153) | copy-start | bytes 604
  110.3 64.4 %copy-start.8 = (f32[1600]{0:T(1024)S(1)}, f32[1600]{0:T(1024)}, u32[]{:S(2)}) copy-start(f32[1600]{0:T(1024)} %add.274) | copy-start | bytes 19204
  125.5 18.6 %all-to-all-start.5 = ((bf16[64,4,128]{2,1,0:T(4,128)(2,1)}), bf16[64,4,128]{2,1,0:T(4,128)(2,1)S(1)}, u32[]{:S(2)}, u32[]{:S(2)}) async-start(bf16[64,4,128]{2,1,0:T(4,128)(2,1)} %bitcast.34), calls=%async_computation.6 | async-start | bytes 131072 | tf_op jit(solution)/shard_map/all_to_all | solution.py:17
  130.1 85.1 %all-gather.2.cloned.1.call-start = ((), (), s32[]{:S(2)}) async-start(), calls=%async_computation.13 | async-start | bytes 1382400 | tf_op jit(solution)/shard_map/all_gather | solution.py:172
  130.3 84.1 %copy-start.5 = (bf16[16,4096]{1,0:T(8,128)(2,1)S(1)}, bf16[16,4096]{1,0:T(8,128)(2,1)}, u32[]{:S(2)}) copy-start(bf16[16,4096]{1,0:T(8,128)(2,1)} %param.20) | copy-start | bytes 393220
Sparse Core Ops, SparseCore 0:
  22.2 48.4 reduce-scatter.1
  177.0 19.8 all-gather.1

commit v3 on v2

v3 whole, which is shorter than its diff:
```python
import functools
import jax
import jax.numpy as jnp
from jax import lax
from jax.experimental import pallas as pl
from jax.experimental.pallas import tpu as pltpu
from jax.sharding import PartitionSpec as P

PASSES = 2
SHIFT_LEVEL = 1.0
BF = jnp.bfloat16
F32 = jnp.float32
LANES = 128
VMEM_LIMIT = 48 * 2**20


def mm(x, y):
    return jnp.dot(x, y, preferred_element_type=F32)


def mm_nt(x, y):
    return lax.dot_general(x, y, (((1,), (1,)), ((), ())), preferred_element_type=F32)


def mm_tn(x, y):
    return lax.dot_general(x, y, (((0,), (0,)), ((), ())), preferred_element_type=F32)


def high_low(x):
    high = x.astype(BF)
    return high, (x - high.astype(F32)).astype(BF)


def swap(x, axis):
    return lax.all_to_all(x, axis, split_axis=0, concat_axis=0, tiled=True)


def up(n, m):
    return -(-n // m) * m


def call(kernel, outs, scratch=()):
    return pl.pallas_call(
        kernel,
        out_shape=outs,
        scratch_shapes=list(scratch),
        compiler_params=pltpu.CompilerParams(vmem_limit_bytes=VMEM_LIMIT),
    )


def blocks_kernel(naux, share, aux_ref, occ_ref, out_ref, last_ref):
    nsq, depth = aux_ref.shape[1:]
    width = occ_ref.shape[1]
    ntno = share * naux
    for t in range(0, naux, 2):
        left = jnp.concatenate([aux_ref[t], aux_ref[t + 1]], axis=1)
        none = jnp.zeros((LANES - width, depth), BF)
        zero = jnp.zeros((LANES, depth), BF)
        first = jnp.concatenate([occ_ref[t], none, zero], axis=0)
        second = jnp.concatenate([zero, occ_ref[t + 1], none], axis=0)
        right = jnp.concatenate([first, second], axis=1)
        both = mm_nt(left, right).astype(BF)
        out_ref[t, :nsq, :] = both[:, :LANES]
        out_ref[t + 1, :nsq, :] = both[:, LANES:]
    none = jnp.zeros((LANES - width, depth), BF)
    last_ref[...] = mm_nt(aux_ref[naux], jnp.concatenate([occ_ref[naux], none], axis=0))
    rest = out_ref.shape[1] - nsq - share * ntno
    for member in range(naux):
        parts = [
            last_ref[pl.ds(member * share + b, ntno, stride=ntno), :] for b in range(share)
        ]
        parts.append(jnp.zeros((rest, LANES), F32))
        out_ref[member, nsq:, :] = jnp.concatenate(parts, axis=0).astype(BF)


def integral_blocks(aux_blocks, occ_blocks, naux):
    _, depth, nsq = aux_blocks.shape
    ntno = occ_blocks.shape[2] // 3
    share = ntno // naux
    rows = up(nsq + share * ntno, 16)
    return call(
        functools.partial(blocks_kernel, naux, share),
        jax.ShapeDtypeStruct((naux, rows, LANES), BF),
        [pltpu.VMEM((nsq, LANES), F32)],
    )(aux_blocks.transpose(0, 2, 1), occ_blocks.transpose(0, 2, 1))


def pack_kernel(naux, route_ref, arrived_ref, old_ref, out_ref):
    share, nsq = old_ref.shape[1:]
    slab = nsq // naux
    part = out_ref.shape[0] // naux
    handed = mm(route_ref[...], arrived_ref[...]).astype(BF)
    pieces = handed.shape[0] // out_ref.shape[0]
    span = out_ref.shape[1] - pieces * LANES
    for x in range(pieces):
        out_ref[:, span + x * LANES : span + (x + 1) * LANES] = handed[
            x * out_ref.shape[0] : (x + 1) * out_ref.shape[0]
        ]
    rows = []
    for member in range(naux):
        row = jnp.concatenate(
            [
                old_ref[member],
                jnp.zeros((share, LANES * (nsq // LANES + 1) - nsq), F32),
                old_ref[naux][:, member * slab : (member + 1) * slab],
                jnp.zeros((share, span - LANES * (nsq // LANES + 1) - slab), F32),
            ],
            axis=1,
        )
        rows.append(jnp.concatenate([row, jnp.zeros((part - share, span), F32)], axis=0))
    out_ref[:, :span] = jnp.concatenate(rows, axis=0).astype(BF)


def block_mask(rows, row_block, cols, col_block):
    row = lax.broadcasted_iota(jnp.int32, (rows, cols), 0) // row_block
    return row == lax.broadcasted_iota(jnp.int32, (rows, cols), 1) // col_block


def fetch_order(naux, chunk, first):
    size = naux * 6 * chunk
    here = lax.broadcasted_iota(jnp.int32, (size, size), 0)
    there = lax.broadcasted_iota(jnp.int32, (size, size), 1)
    k, source, piece = here // (naux * chunk), (here // chunk) % naux, here % chunk
    if first:
        part = 6 * chunk // 3
        at = k * chunk + piece
        spot = (at // part) * (naux * part) + source * part + at % part
    else:
        spot = source * 6 * chunk + k * chunk + piece
    return (spot == there).astype(BF)


def triple_work(naux, chunk, ordered, covers, pieces, state, col, row, matrix):
    ntno = matrix.shape[0] // 3
    npno = covers.shape[1]
    half_rows = naux * chunk
    stack = []
    for k in range(3):
        block = ordered[k * half_rows : (k + 1) * half_rows]
        stack += [block[:, :npno], block[:, npno:]]
    stack = jnp.concatenate(stack, axis=0).astype(BF)
    mask = block_mask(3 * npno, npno, 3 * ntno, ntno)
    half = jnp.where(mask, mm_nt(stack, covers), 0.0).astype(BF)
    proj = mm_tn(pieces, half).astype(BF)
    state = (SHIFT_LEVEL * state + mm(proj, matrix)) / (col + row)
    resid = mm_nt(state.astype(BF), matrix)
    high, low = high_low(resid)
    left = jnp.where(mask, mm(pieces, high) + mm(pieces, low), 0.0)
    high, low = high_low(left)
    back = mm(high, covers) + mm(low, covers)
    packed = []
    for k in range(3):
        block = back[2 * k * half_rows : 2 * (k + 1) * half_rows]
        packed.append(jnp.concatenate([block[:half_rows], block[half_rows:]], axis=1))
    return state, jnp.concatenate(packed, axis=0)


def both_triples(naux, chunk, order, came, cover_ref, piece_ref, col_ref, row_ref, states, mats):
    ordered = mm(order, came)
    wide = mats[0].shape[1]
    rows = ordered.shape[0] // 2
    start = up(wide, LANES)
    new, sent = [], []
    for which in range(2):
        low, high = (0, wide) if which == 0 else (start, start + mats[1].shape[1])
        state, back = triple_work(
            naux,
            chunk,
            ordered[which * rows : (which + 1) * rows],
            cover_ref[which],
            piece_ref[which],
            states[which],
            col_ref[which],
            row_ref[:, low:high],
            mats[which],
        )
        new.append(state)
        sent.append(back)
    return new, jnp.concatenate(sent, axis=0).astype(BF)


def first_kernel(
    naux,
    chunk,
    came_ref,
    rows_ref,
    cover_ref,
    piece_ref,
    col_ref,
    row_ref,
    sent_ref,
    own_ref,
    last_ref,
    own_mat_ref,
    last_mat_ref,
    wide_ref,
):
    ntno, nsq = own_ref.shape
    share = ntno // naux
    wide_ref[...] = rows_ref[...].astype(F32)
    own = [wide_ref[pl.ds(b, ntno, stride=ntno), :] for b in range(ntno)]
    last = [wide_ref[pl.ds(nsq + b * ntno, ntno), :] for b in range(share)]
    for parts, out in ((own, own_mat_ref), (last, last_mat_ref)):
        out[...] = jnp.concatenate(
            [
                jnp.concatenate([x[:, m * ntno : (m + 1) * ntno] for x in parts], axis=1)
                for m in range(3)
            ],
            axis=0,
        ).astype(BF)
    came = came_ref[...]
    size = came.shape[0]
    span = came.shape[1] - 3 * LANES
    part = size // naux
    a = lax.broadcasted_iota(jnp.int32, (ntno, size), 0)
    there = lax.broadcasted_iota(jnp.int32, (ntno, size), 1)
    old = mm(((a // share) * part + a % share == there).astype(BF), came[:, :span])
    start = up(nsq, LANES)
    fetched = jnp.concatenate(
        [came[:, span + x * LANES : span + (x + 1) * LANES] for x in range(3)], axis=0
    )
    new, sent = both_triples(
        naux,
        chunk,
        fetch_order(naux, chunk, True),
        fetched,
        cover_ref,
        piece_ref,
        col_ref,
        row_ref,
        (old[:, :nsq], old[:, start : start + share * ntno]),
        (own_mat_ref[...], last_mat_ref[...]),
    )
    own_ref[...] = new[0]
    last_ref[...] = new[1]
    sent_ref[...] = mm_tn(fetch_order(naux, chunk, False), sent).astype(BF)


def later_kernel(
    naux,
    chunk,
    came_ref,
    cover_ref,
    piece_ref,
    col_ref,
    row_ref,
    own_ref,
    last_ref,
    own_mat_ref,
    last_mat_ref,
    sent_ref,
    new_ref,
):
    nsq = own_ref.shape[1]
    order = fetch_order(naux, chunk, False)
    new, sent = both_triples(
        naux,
        chunk,
        order,
        came_ref[...],
        cover_ref,
        piece_ref,
        col_ref,
        row_ref,
        (own_ref[...], last_ref[...]),
        (own_mat_ref[...], last_mat_ref[...]),
    )
    start, slab = up(nsq, LANES), last_ref.shape[1]
    new_ref[:, :nsq] = new[0].astype(BF)
    new_ref[:, start : start + slab] = new[1].astype(BF)
    sent_ref[...] = mm_tn(order, sent).astype(BF)


def body(
    aux_blocks,
    occ_blocks,
    intersections,
    tno_energy,
    occ_energy,
    tno_rank,
    triples_old,
    pair_amps,
    pno_energy,
    pair_occ,
    pair_rank,
    request_owner,
    request_row,
):
    tdev = aux_blocks.shape[0]
    ntno = tno_energy.shape[1]
    npno = pno_energy.shape[1]
    pdev = pair_amps.shape[0]
    naux = lax.axis_size("aux")
    ntrip = lax.axis_size("trip")
    member = lax.axis_index("aux")
    share = ntno // naux
    nreq = 3 * tdev
    nsq = ntno * ntno
    slab = share * ntno
    start = up(nsq, LANES)
    span = start + up(slab, LANES)
    prow = npno // naux
    chunk = prow * npno // LANES
    slots = ntrip * chunk
    owner = request_owner.reshape(nreq)
    local = request_row.reshape(nreq)

    slot = jnp.arange(ntrip)
    wanted = jnp.sum(
        jnp.where(owner[:, None] == slot[None, :], local[:, None] + 1, 0), axis=0
    ) - 1
    piece = jnp.arange(chunk)
    lane = jnp.arange(LANES)
    asking = (wanted[:, None] * chunk + piece[None, :])[:, :, None] == lane[None, None, :]
    asking = (asking & (wanted >= 0)[:, None, None]).astype(BF)

    blocks = integral_blocks(aux_blocks, occ_blocks, naux)
    blocks, asking = lax.optimization_barrier((blocks, asking))
    rows = lax.psum_scatter(blocks, "aux", scatter_dimension=0, tiled=True)[0]
    serve = swap(asking, "trip").reshape(slots, LANES)

    def routing(dest, at):
        k, part = at // chunk, at % chunk
        request = jnp.where(k < 3, 3 * dest + k, 3 * naux + k - 3)
        asked = jnp.sum(
            jnp.where(request[:, None] == jnp.arange(nreq)[None, :], owner[None, :], 0), axis=1
        )
        return ((asked * chunk + part)[:, None] == jnp.arange(slots)[None, :]).astype(BF)

    number = jnp.arange(naux * 6 * chunk)
    route = routing(number // (6 * chunk), number % (6 * chunk))
    part = 6 * chunk // 3
    route_first = routing(
        (number // part) % naux, number // (naux * part) * part + number % part
    )
    route_back = route.T

    live = jnp.arange(npno)[None, :] < pair_rank[:, None]
    live_p = lax.dynamic_slice_in_dim(live, member * prow, prow, 1)
    energy_p = lax.dynamic_slice_in_dim(pno_energy, member * prow, prow, 1)
    pair_keep = (live_p[:, :, None] & live[:, None, :]).reshape(pdev * chunk, LANES)
    pair_den = (
        energy_p[:, :, None] + pno_energy[:, None, :] + pair_occ[:, None, None] + SHIFT_LEVEL
    ).reshape(pdev * chunk, LANES)
    amps = (
        lax.dynamic_slice_in_dim(pair_amps, member * prow * npno, prow * npno, 1)
        .reshape(pdev * chunk, LANES)
        .astype(F32)
    )
    gain = jnp.zeros_like(amps)

    def two(x):
        return jnp.stack([lax.dynamic_slice_in_dim(x, member, 1, 0)[0], x[naux]])

    energy = jnp.where(jnp.arange(ntno)[None, :] < tno_rank[:, None], tno_energy, jnp.inf)
    energy = two(energy)
    col = (energy - two(jnp.sum(occ_energy, axis=1))[:, None] + SHIFT_LEVEL)[:, :, None]
    energy_b = lax.dynamic_slice_in_dim(energy[1], member * share, share, 0)
    row = jnp.concatenate(
        [
            (energy[0][:, None] + energy[0][None, :]).reshape(nsq),
            jnp.zeros((start - nsq,), F32),
            (energy_b[:, None] + energy[1][None, :]).reshape(slab),
            jnp.zeros((span - start - slab,), F32),
        ]
    )[None, :]
    cover = two(intersections)
    flat = cover.transpose(0, 1, 3, 2).reshape(2, 3 * ntno, npno)
    split = cover.reshape(2, 3, npno // 2, 2, ntno).transpose(0, 1, 3, 2, 4)
    split = split.reshape(2, 3 * npno, ntno)

    for step in range(PASSES):
        outgoing = jnp.where(pair_keep, amps.astype(BF), jnp.zeros((), BF))
        pad = serve.shape[1] - outgoing.shape[0]
        found = mm(serve, jnp.pad(outgoing, ((0, pad), (0, 0)))).astype(BF)
        arrived = swap(found.reshape(ntrip, chunk, LANES), "trip").reshape(slots, LANES)
        if step == 0:
            packed = call(
                functools.partial(pack_kernel, naux),
                jax.ShapeDtypeStruct((naux * part, span + 3 * LANES), BF),
            )(route_first, arrived, triples_old)
            came = swap(packed.reshape(naux, part, span + 3 * LANES), "aux")
            sent, own, last, own_mat, last_mat = call(
                functools.partial(first_kernel, naux, chunk),
                (
                    jax.ShapeDtypeStruct((naux * 6 * chunk, LANES), BF),
                    jax.ShapeDtypeStruct((ntno, nsq), F32),
                    jax.ShapeDtypeStruct((ntno, slab), F32),
                    jax.ShapeDtypeStruct((3 * ntno, nsq), BF),
                    jax.ShapeDtypeStruct((3 * ntno, slab), BF),
                ),
                [pltpu.VMEM(rows.shape, F32)],
            )(came.reshape(naux * part, span + 3 * LANES), rows, flat, split, col, row)
        else:
            handed = mm(route, arrived).astype(BF).reshape(naux, 6 * chunk, LANES)
            came = swap(handed, "aux").reshape(naux * 6 * chunk, LANES)
            sent, new = call(
                functools.partial(later_kernel, naux, chunk),
                (
                    jax.ShapeDtypeStruct((naux * 6 * chunk, LANES), BF),
                    jax.ShapeDtypeStruct((ntno, span), BF),
                ),
            )(came, flat, split, col, row, own, last, own_mat, last_mat)
        came = swap(sent.reshape(naux, 6 * chunk, LANES), "aux")
        sent = mm(route_back, came.reshape(naux * 6 * chunk, LANES)).astype(BF)
        came = swap(sent.reshape(ntrip, chunk, LANES), "trip").reshape(slots, LANES)
        total = mm_tn(serve, came)[: pdev * chunk]
        change = jnp.where(pair_keep, total / pair_den, 0.0)
        gain = gain + change
        amps = amps + change

    new = lax.all_gather(new, "aux", axis=0, tiled=False)
    new = lax.dynamic_slice_in_dim(new, member * share, share, 1).astype(F32)
    last = new[:, :, start : start + slab].transpose(1, 0, 2).reshape(1, share, nsq)
    triples_new = jnp.concatenate([new[:, :, :nsq], last], axis=0)
    gains = jnp.broadcast_to(gain.astype(BF)[None], (naux, pdev * chunk, LANES))
    gains = swap(gains, "aux").reshape(naux, pdev, prow * npno).transpose(1, 0, 2)
    pairs_new = pair_amps.astype(F32) + gains.reshape(pdev, npno * npno).astype(F32)
    return triples_new, pairs_new


def solution(mesh):
    in_specs = (
        P("trip", "aux", None),
        P("trip", "aux", None),
        P("trip", None, None, None),
        P("trip", None),
        P("trip", None),
        P("trip"),
        P("trip", "aux", None),
        P("trip", None),
        P("trip", None),
        P("trip"),
        P("trip"),
        P("trip", None, None),
        P("trip", None),
    )
    out_specs = (P("trip", "aux", None), P("trip", None))
    return jax.shard_map(body, mesh=mesh, in_specs=in_specs, out_specs=out_specs, check_vma=False)
```

time: 226 us -> 195 us (0.86)
  local copies, waits for them, and re-layouts: 25.6 us -> 7.87 us
  matrix products: 17.7 us -> 2.8 us
  blocking collectives: 73.5 us -> 64 us
  Pallas kernels: 0 us -> 9.46 us
  waiting for transfers between devices: 39.7 us -> 48.8 us
  other arithmetic: 13 us -> 6.6 us
    all_to_all x6 -> x5, blocking collectives: 73.5 us -> 64 us  [swap(): return lax.all_to_all(x, axis, split_axis=0, concat_axis=0, tiled=True)]
    pallas_call x0 -> x4, Pallas kernels: none -> 9.46 us  [the longest x1 3 us: integral_blocks(): call(functools.partial(blocks_kernel, naux, share), jax.ShapeDtypeStruct(...]
    dot_general x17 -> x2, matrix products: 9.59 us -> 0.38 us  [mm_tn(): lax.dot_general(x, y, (((0,), (0,)), ((), ())), preferred_element_type=F32)]
    all_to_all x5, waiting for transfers between devices: 39.6 us -> 48.8 us  [swap(): return lax.all_to_all(x, axis, split_axis=0, concat_axis=0, tiled=True)]
    reshape x19 -> x1, local copies, waits for them, and re-layouts: 6.16 us -> 0.09 us  [body(): new[:, :, start:start + slab].transpose(1, 0, 2).reshape(1, share, nsq)]
    dot_general x12 -> x5, matrix products: 8.09 us -> 2.41 us  [mm(): return jnp.dot(x, y, preferred_element_type=F32)]
    concatenate x4 -> x1, other arithmetic: 6.41 us -> 0.82 us  [body(): triples_new = jnp.concatenate([new[:, :, :nsq], last], axis=0)]
    unnamed x45 -> x25, local copies, waits for them, and re-layouts: 1.1 us -> 5.03 us
  transfers between devices with their start and end apart: 7 -> 7, of which waited for: 4 -> 5; matrix products, arithmetic and copies ran while one was open for 10% -> 4% of each run, Pallas kernels for 0% -> 0%
where the time goes in v3:
time: 195 us; the launch traced here: 194 us
  blocking collectives  64 us (33%)
  waiting for transfers between devices  48.8 us (25%)
  starting transfers between devices  40.6 us (21%)
  between operations  14.3 us (7%)
  Pallas kernels  9.46 us (5%)
  local copies, waits for them, and re-layouts  7.87 us (4%)
  other arithmetic  6.6 us (3%)
  matrix products  2.8 us (1%)
    all_to_all x5, blocking collectives, swap(): return lax.all_to_all(x, axis, split_axis=0, concat_axis=0, tiled=True)  64 us
    all_to_all x5, waiting for transfers between devices, swap(): return lax.all_to_all(x, axis, split_axis=0, concat_axis=0, tiled=True)  48.8 us
    all_to_all x5, starting transfers between devices, swap(): return lax.all_to_all(x, axis, split_axis=0, concat_axis=0, tiled=True)  40.5 us
    unnamed x25, local copies, waits for them, and re-layouts  5.03 us
  transfers between devices with their start and end apart: 7, of which 5 were waited for; matrix products, arithmetic and copies ran while one was open for 4% of the time, Pallas kernels for 0%

profile of v3, /device:TPU:1, one launch (start us, length us, event | category | flops | bytes accessed | tf_op | source)
XLA Modules:
  0.0 194.4 jit_solution(5344273849012558944)
XLA Ops:
  7.2 0.7 broadcast_add_fusion.3
  7.9 0.1 copy.81
  8.1 0.8 copy.80
  8.9 0.1 select_reduce_fusion.2
  9.1 2.0 %copy-done = bf16[9,128,1600]{1,2,0:T(8,128)(2,1)S(1)} copy-done((bf16[9,128,1600]{1,2,0:T(8,128)(2,1)S(1)}, bf16[9,128,1600]{1,2,0:T(8,128)(2,1)}, u32[]{:S(2)}) %copy-start) | copy-done | bytes 3686424
  11.2 1.0 copy-done.3
  12.1 3.0 %shard_map.140 = bf16[8,1808,128]{2,1,0:T(8,128)(2,1)} custom-call(bf16[9,1600,128]{2,1,0:T(8,128)(2,1)S(1)} %bitcast.56, bf16[9,120,128]{2,1,0:T(8,128)(2,1)S(1)} %bitcast.63), custom_call_target="tpu_custom_call" | custom-call | tf_op jit(solution)/shard_map/pallas_call | solution.py:81
  15.2 0.8 fusion.2
  16.0 19.1 %all-to-all-start = ((bf16[64,4,128]{2,1,0:T(4,128)(2,1)}), bf16[64,4,128]{2,1,0:T(4,128)(2,1)S(1)}, u32[]{:S(2)}, u32[]{:S(2)}) async-start(bf16[64,4,128]{2,1,0:T(4,128)(2,1)} %fusion.2), calls=%async_computation | async-start | bytes 131072 | tf_op jit(solution)/shard_map/all_to_all | solution.py:35
  35.4 0.1 and.163
  35.8 0.6 fusion.39
  36.4 0.1 select_reduce_fusion.1
  36.7 1.4 pad_maximum_fusion.2
  38.1 0.8 constant_dynamic-slice_fusion.2
  38.8 10.3 %all-to-all-done = bf16[64,4,128]{2,1,0:T(4,128)(2,1)S(1)} async-done(((bf16[64,4,128]{2,1,0:T(4,128)(2,1)}), bf16[64,4,128]{2,1,0:T(4,128)(2,1)S(1)}, u32[]{:S(2)}, u32[]{:S(2)}) %all-to-all-start) | async-done | bytes 65568 | tf_op jit(solution)/shard_map/all_to_all | solution.py:35
  49.2 0.8 convolution_convert_fusion.3
  50.0 4.6 %all-to-all-start.1 = ((bf16[64,4,128]{2,1,0:T(4,128)(2,1)}), bf16[64,4,128]{2,1,0:T(4,128)(2,1)S(1)}, u32[]{:S(2)}, u32[]{:S(2)}) async-start(bf16[64,4,128]{2,1,0:T(4,128)(2,1)} %bitcast.3), calls=%async_computation.1 | async-start | bytes 131072 | tf_op jit(solution)/shard_map/all_to_all | solution.py:35
  54.6 0.1 copy.96
  54.8 0.1 copy.95
  54.9 0.1 fusion.route_ref
  55.0 13.7 %all-to-all-done.1 = bf16[64,4,128]{2,1,0:T(4,128)(2,1)S(1)} async-done(((bf16[64,4,128]{2,1,0:T(4,128)(2,1)}), bf16[64,4,128]{2,1,0:T(4,128)(2,1)S(1)}, u32[]{:S(2)}, u32[]{:S(2)}) %all-to-all-start.1) | async-done | bytes 65568 | tf_op jit(solution)/shard_map/all_to_all | solution.py:35
  68.7 0.9 shard_map.141
  69.5 7.8 %all-to-all-start.2 = ((bf16[8,8,2304]{2,1,0:T(8,128)(2,1)}), bf16[8,8,2304]{2,1,0:T(8,128)(2,1)S(1)}, u32[]{:S(2)}, u32[]{:S(2)}) async-start(bf16[8,8,2304]{2,1,0:T(8,128)(2,1)} %bitcast.5), calls=%async_computation.2 | async-start | bytes 589824 | tf_op jit(solution)/shard_map/all_to_all | solution.py:35
  77.4 0.1 copy.84
  77.5 0.1 copy.88
  77.9 6.3 %all-to-all-done.2 = bf16[8,8,2304]{2,1,0:T(8,128)(2,1)S(1)} async-done(((bf16[8,8,2304]{2,1,0:T(8,128)(2,1)}), bf16[8,8,2304]{2,1,0:T(8,128)(2,1)S(1)}, u32[]{:S(2)}, u32[]{:S(2)}) %all-to-all-start.2) | async-done | bytes 294944 | tf_op jit(solution)/shard_map/all_to_all | solution.py:35
  84.1 1.0 copy-done.2
  85.2 3.0 %shard_map.142 = (bf16[192,128]{1,0:T(8,128)(2,1)}, f32[40,1600]{1,0:T(8,128)S(1)}, f32[40,200]{1,0:T(8,128)S(1)}, bf16[120,1600]{1,0:T(8,128)(2,1)S(1)}, bf16[120,200]{1,0:T(8,128)(2,1)S(1)}) custom-call(bf16[64,2304]{1,0:T(8,128)(2,1)S(1)} %bitcast.57, bf16[1808,128]{1,0:T(8,128)(2,1)S(1)} %bitcast.62, bf16[2,120,64]{2,1,0:T(8,128)(2,1)S(1)} %bitcast.60, ...), custom_call_target="tpu_custom_call" | custom-call | tf_op jit(solution)/shard_map/pallas_call | solution.py:383
  88.1 4.3 %all-to-all-start.3 = ((bf16[8,24,128]{2,1,0:T(8,128)(2,1)}), bf16[8,24,128]{2,1,0:T(8,128)(2,1)S(1)}, u32[]{:S(2)}, u32[]{:S(2)}) async-start(bf16[8,24,128]{2,1,0:T(8,128)(2,1)} %bitcast.20), calls=%async_computation.4 | async-start | bytes 98304 | tf_op jit(solution)/shard_map/all_to_all | solution.py:35
  92.5 4.8 %all-to-all-done.3 = bf16[8,24,128]{2,1,0:T(8,128)(2,1)S(1)} async-done(((bf16[8,24,128]{2,1,0:T(8,128)(2,1)}), bf16[8,24,128]{2,1,0:T(8,128)(2,1)S(1)}, u32[]{:S(2)}, u32[]{:S(2)}) %all-to-all-start.3) | async-done | bytes 49184 | tf_op jit(solution)/shard_map/all_to_all | solution.py:35
  97.3 1.0 convolution_convert_fusion.2
  98.2 4.6 %all-to-all-start.4 = ((bf16[64,4,128]{2,1,0:T(4,128)(2,1)}), bf16[64,4,128]{2,1,0:T(4,128)(2,1)S(1)}, u32[]{:S(2)}, u32[]{:S(2)}) async-start(bf16[64,4,128]{2,1,0:T(4,128)(2,1)} %bitcast.22), calls=%async_computation.5 | async-start | bytes 131072 | tf_op jit(solution)/shard_map/all_to_all | solution.py:35
  103.0 0.1 add_add_fusion
  103.2 13.7 %all-to-all-done.4 = bf16[64,4,128]{2,1,0:T(4,128)(2,1)S(1)} async-done(((bf16[64,4,128]{2,1,0:T(4,128)(2,1)}), bf16[64,4,128]{2,1,0:T(4,128)(2,1)S(1)}, u32[]{:S(2)}, u32[]{:S(2)}) %all-to-all-start.4) | async-done | bytes 65568 | tf_op jit(solution)/shard_map/all_to_all | solution.py:35
  116.9 0.2 convolution_bitcast_fusion.1
  117.1 0.1 convolution_convert_fusion.1
  117.2 18.4 %all_to_all.50 = bf16[64,4,128]{2,1,0:T(4,128)(2,1)S(1)} all-to-all(bf16[64,4,128]{2,1,0:T(4,128)(2,1)S(1)} %bitcast.72), channel_id=1, replica_groups=mesh['trip'=64,'aux'=8] {'trip'}, dimensions={0} | all-to-all | bytes 131072 | tf_op jit(solution)/shard_map/all_to_all | solution.py:35
  135.7 0.2 convolution_convert_fusion.4
  135.9 10.0 %all_to_all.51 = bf16[8,24,128]{2,1,0:T(8,128)(2,1)S(1)} all-to-all(bf16[8,24,128]{2,1,0:T(8,128)(2,1)S(1)} %bitcast.77), channel_id=1, replica_groups=mesh['trip'=64,'aux'=8] {'aux'}, dimensions={0} | all-to-all | bytes 98304 | tf_op jit(solution)/shard_map/all_to_all | solution.py:35
  145.8 2.6 %shard_map.143 = (bf16[192,128]{1,0:T(8,128)(2,1)S(1)}, bf16[40,1920]{1,0:T(8,128)(2,1)}) custom-call(bf16[192,128]{1,0:T(8,128)(2,1)S(1)} %bitcast.65, bf16[2,120,64]{2,1,0:T(8,128)(2,1)S(1)} %bitcast.61, bf16[2,192,40]{2,1,0:T(8,128)(2,1)S(1)} %bitcast.59, f32[2,40,1]{2,1,0:T(8,128)S(1)} %broadcast_add_fusion.col_ref, ...), custom_call_target="tpu_custom_call" | custom-call | tf_op jit(solution)/shard_map/pallas_call | solution.py:397
  148.5 7.9 %all_to_all.52 = bf16[8,24,128]{2,1,0:T(8,128)(2,1)S(1)} all-to-all(bf16[8,24,128]{2,1,0:T(8,128)(2,1)S(1)} %bitcast.66), channel_id=1, replica_groups=mesh['trip'=64,'aux'=8] {'aux'}, dimensions={0} | all-to-all | bytes 98304 | tf_op jit(solution)/shard_map/all_to_all | solution.py:35
  156.4 0.3 convolution_convert_fusion
  156.7 17.8 %all_to_all.53 = bf16[64,4,128]{2,1,0:T(4,128)(2,1)S(1)} all-to-all(bf16[64,4,128]{2,1,0:T(4,128)(2,1)S(1)} %bitcast.73), channel_id=1, replica_groups=mesh['trip'=64,'aux'=8] {'trip'}, dimensions={0} | all-to-all | bytes 131072 | tf_op jit(solution)/shard_map/all_to_all | solution.py:35
  174.5 0.2 convolution_bitcast_fusion
  174.8 9.9 %all_to_all.54 = bf16[8,64,128]{2,1,0:T(8,128)(2,1)S(1)} all-to-all(bf16[8,64,128]{2,1,0:T(8,128)(2,1)S(1)} %broadcast_in_dim.96), channel_id=1, replica_groups=mesh['trip'=64,'aux'=8] {'aux'}, dimensions={0} | all-to-all | bytes 262144 | tf_op jit(solution)/shard_map/all_to_all | solution.py:35
  184.8 0.7 convert_add_fusion
  185.5 1.1 dynamic-slice_convert_fusion
  186.8 0.8 pad_maximum_fusion
  (66 shorter events, 1.9 us)
Async XLA Ops:
  7.2 77.0 %reduce-scatter.2.cloned.1.call-start = ((), (), s32[]{:S(2)}) async-start(), calls=%async_computation.11 | async-start | bytes 4165632 | tf_op jit(solution)/shard_map/reduce_scatter | solution.py:319
  9.1 2.0 %copy-start = (bf16[9,128,1600]{1,2,0:T(8,128)(2,1)S(1)}, bf16[9,128,1600]{1,2,0:T(8,128)(2,1)}, u32[]{:S(2)}) copy-start(bf16[9,128,1600]{1,2,0:T(8,128)(2,1)} %param.13) | copy-start | bytes 11059204
  11.2 1.0 copy-start.3
  15.1 20.0 %copy-start.9 = (s32[16]{0:T(128)S(1)}, s32[16]{0:T(128)}, u32[]{:S(2)}) copy-start(s32[16]{0:T(128)} %param.23) | copy-start | bytes 196
  15.1 20.4 %copy-start.4 = (bf16[16,4096]{1,0:T(8,128)(2,1)S(1)}, bf16[16,4096]{1,0:T(8,128)(2,1)}, u32[]{:S(2)}) copy-start(bf16[16,4096]{1,0:T(8,128)(2,1)} %param.20) | copy-start | bytes 393220
  15.1 20.5 %copy-start.7 = (f32[9,3]{0,1:T(4,128)S(1)}, f32[9,3]{0,1:T(4,128)}, u32[]{:S(2)}) copy-start(f32[9,3]{0,1:T(4,128)} %param.17) | copy-start | bytes 328
  15.1 20.5 %copy-start.6 = (f32[9,40]{1,0:T(8,128)S(1)}, f32[9,40]{1,0:T(8,128)}, u32[]{:S(2)}) copy-start(f32[9,40]{1,0:T(8,128)} %param.16) | copy-start | bytes 4324
  15.1 20.5 %copy-start.10 = (s32[9]{0:T(128)S(1)}, s32[9]{0:T(128)}, u32[]{:S(2)}) copy-start(s32[9]{0:T(128)} %param.18) | copy-start | bytes 112
  15.2 53.5 %copy-start.1 = (f32[9,5,1600]{2,1,0:T(8,128)S(1)}, f32[9,5,1600]{2,1,0:T(8,128)}, u32[]{:S(2)}) copy-start(f32[9,5,1600]{2,1,0:T(8,128)} %old_ref.1) | copy-start | bytes 864004
  16.0 86.9 %copy-start.5 = (f32[16,64]{1,0:T(8,128)S(1)}, f32[16,64]{1,0:T(8,128)}, u32[]{:S(2)}) copy-start(f32[16,64]{1,0:T(8,128)} %param.21) | copy-start | bytes 12292
  16.0 87.0 %copy-start.8 = (f32[16]{0:T(128)S(1)}, f32[16]{0:T(128)}, u32[]{:S(2)}) copy-start(f32[16]{0:T(128)} %param.22) | copy-start | bytes 196
  16.0 33.2 %all-to-all-start = ((bf16[64,4,128]{2,1,0:T(4,128)(2,1)}), bf16[64,4,128]{2,1,0:T(4,128)(2,1)S(1)}, u32[]{:S(2)}, u32[]{:S(2)}) async-start(bf16[64,4,128]{2,1,0:T(4,128)(2,1)} %fusion.2), calls=%async_computation | async-start | bytes 131072 | tf_op jit(solution)/shard_map/all_to_all | solution.py:35
  50.0 18.7 %all-to-all-start.1 = ((bf16[64,4,128]{2,1,0:T(4,128)(2,1)}), bf16[64,4,128]{2,1,0:T(4,128)(2,1)S(1)}, u32[]{:S(2)}, u32[]{:S(2)}) async-start(bf16[64,4,128]{2,1,0:T(4,128)(2,1)} %bitcast.3), calls=%async_computation.1 | async-start | bytes 131072 | tf_op jit(solution)/shard_map/all_to_all | solution.py:35
  69.5 14.6 %all-to-all-start.2 = ((bf16[8,8,2304]{2,1,0:T(8,128)(2,1)}), bf16[8,8,2304]{2,1,0:T(8,128)(2,1)S(1)}, u32[]{:S(2)}, u32[]{:S(2)}) async-start(bf16[8,8,2304]{2,1,0:T(8,128)(2,1)} %bitcast.5), calls=%async_computation.2 | async-start | bytes 589824 | tf_op jit(solution)/shard_map/all_to_all | solution.py:35
  84.1 1.0 copy-start.2
  88.1 9.1 %all-to-all-start.3 = ((bf16[8,24,128]{2,1,0:T(8,128)(2,1)}), bf16[8,24,128]{2,1,0:T(8,128)(2,1)S(1)}, u32[]{:S(2)}, u32[]{:S(2)}) async-start(bf16[8,24,128]{2,1,0:T(8,128)(2,1)} %bitcast.20), calls=%async_computation.4 | async-start | bytes 98304 | tf_op jit(solution)/shard_map/all_to_all | solution.py:35
  98.2 18.6 %all-to-all-start.4 = ((bf16[64,4,128]{2,1,0:T(4,128)(2,1)}), bf16[64,4,128]{2,1,0:T(4,128)(2,1)S(1)}, u32[]{:S(2)}, u32[]{:S(2)}) async-start(bf16[64,4,128]{2,1,0:T(4,128)(2,1)} %bitcast.22), calls=%async_computation.5 | async-start | bytes 131072 | tf_op jit(solution)/shard_map/all_to_all | solution.py:35
  102.8 82.7 %all-gather.3.cloned.1.call-start = ((), (), s32[]{:S(2)}) async-start(), calls=%async_computation.12 | async-start | bytes 1382400 | tf_op jit(solution)/shard_map/all_gather | solution.py:412
Sparse Core Ops, SparseCore 0:
  16.1 48.2 reduce-scatter.1
  148.6 19.7 all-gather.2

commit v4 on v3

v4 whole, which is shorter than its diff:
```python
import functools
import jax
import jax.numpy as jnp
from jax import lax
from jax.experimental import pallas as pl
from jax.experimental.pallas import tpu as pltpu
from jax.sharding import PartitionSpec as P

PASSES = 2
SHIFT_LEVEL = 1.0
BF = jnp.bfloat16
F32 = jnp.float32
LANES = 128
VMEM_LIMIT = 48 * 2**20
VMEM_ALL = 63 * 2**20


def mm(x, y):
    return jnp.dot(x, y, preferred_element_type=F32)


def mm_nt(x, y):
    return lax.dot_general(x, y, (((1,), (1,)), ((), ())), preferred_element_type=F32)


def mm_tn(x, y):
    return lax.dot_general(x, y, (((0,), (0,)), ((), ())), preferred_element_type=F32)


def high_low(x):
    high = x.astype(BF)
    return high, (x - high.astype(F32)).astype(BF)


def swap(x, axis):
    return lax.all_to_all(x, axis, split_axis=0, concat_axis=0, tiled=True)


def up(n, m):
    return -(-n // m) * m


def call(kernel, outs, scratch=(), limit=VMEM_LIMIT, **specs):
    return pl.pallas_call(
        kernel,
        out_shape=outs,
        scratch_shapes=list(scratch),
        **specs,
        compiler_params=pltpu.CompilerParams(vmem_limit_bytes=limit),
    )


def blocks_kernel(
    naux,
    share,
    aux_ref,
    occ_far_ref,
    owner_far_ref,
    local_far_ref,
    out_ref,
    asking_out_ref,
    held_ref,
    made_ref,
    last_ref,
    occ_ref,
    owner_ref,
    local_ref,
    asking_ref,
    in_sems,
    out_sems,
    more_sems,
):
    nsq, depth = held_ref.shape[1:]
    width = occ_ref.shape[1]
    ntno = share * naux
    groups = [naux // 2, 0]
    ends = [naux + 1, naux // 2]
    arriving = []
    for n, (t, end) in enumerate(zip(groups, ends)):
        part = pl.ds(t, end - t)
        copy = pltpu.make_async_copy(aux_ref.at[part], held_ref.at[part], in_sems.at[n])
        copy.start()
        arriving.append(copy)
    pairs = ((owner_far_ref, owner_ref), (local_far_ref, local_ref), (occ_far_ref, occ_ref))
    first = [pltpu.make_async_copy(x, y, more_sems.at[n]) for n, (x, y) in enumerate(pairs)]
    for copy in first:
        copy.start()
    for copy in first:
        copy.wait()
    chunk = asking_ref.shape[1]
    asking_ref[...] = jnp.zeros(asking_ref.shape, BF)
    piece = lax.broadcasted_iota(jnp.int32, (chunk, LANES), 0)
    lane = lax.broadcasted_iota(jnp.int32, (chunk, LANES), 1)
    for m in range(local_ref.shape[0]):
        for t in range(local_ref.shape[1]):
            hot = (lane == local_ref[m, t] * chunk + piece).astype(F32).astype(BF)
            asking_ref[pl.ds(owner_ref[m, 0, t], 1)] = hot[None]
    asked = pltpu.make_async_copy(asking_ref, asking_out_ref, more_sems.at[3])
    asked.start()

    none = jnp.zeros((LANES - width, depth), BF)
    zero = jnp.zeros((LANES, depth), BF)
    rest = made_ref.shape[1] - nsq - share * ntno
    leaving = []
    for n, (low, end) in enumerate(zip(groups, ends)):
        arriving[n].wait()
        if end > naux:
            right = jnp.concatenate([occ_ref[naux], none], axis=0)
            last_ref[...] = mm_nt(held_ref[naux], right)
        top = min(end, naux)
        for t in range(low, top, 2):
            left = jnp.concatenate([held_ref[t], held_ref[t + 1]], axis=1)
            upper = jnp.concatenate([occ_ref[t], none, zero], axis=0)
            lower = jnp.concatenate([zero, occ_ref[t + 1], none], axis=0)
            both = mm_nt(left, jnp.concatenate([upper, lower], axis=1)).astype(BF)
            made_ref[t, :nsq, :] = both[:, :LANES]
            made_ref[t + 1, :nsq, :] = both[:, LANES:]
            for member in (t, t + 1):
                parts = [
                    last_ref[pl.ds(member * share + b, ntno, stride=ntno), :]
                    for b in range(share)
                ]
                parts.append(jnp.zeros((rest, LANES), F32))
                made_ref[member, nsq:, :] = jnp.concatenate(parts, axis=0).astype(BF)
        part = pl.ds(low, top - low)
        copy = pltpu.make_async_copy(made_ref.at[part], out_ref.at[part], out_sems.at[n])
        copy.start()
        leaving.append(copy)
    for copy in leaving:
        copy.wait()
    asked.wait()


def integral_blocks(aux_blocks, occ_blocks, request_owner, request_row, naux, ntrip, chunk):
    tdev, depth, nsq = aux_blocks.shape
    ntno = occ_blocks.shape[2] // 3
    share = ntno // naux
    rows = up(nsq + share * ntno, 16)
    far = pl.BlockSpec(memory_space=pltpu.HBM)
    return call(
        functools.partial(blocks_kernel, naux, share),
        (
            jax.ShapeDtypeStruct((naux, rows, LANES), BF),
            jax.ShapeDtypeStruct((ntrip, chunk, LANES), BF),
        ),
        [
            pltpu.VMEM((tdev, nsq, depth), BF),
            pltpu.VMEM((naux, rows, LANES), BF),
            pltpu.VMEM((nsq, LANES), F32),
            pltpu.VMEM((tdev, occ_blocks.shape[2], depth), BF),
            pltpu.SMEM((3, 1, tdev), jnp.int32),
            pltpu.SMEM((3, tdev), jnp.int32),
            pltpu.VMEM((ntrip, chunk, LANES), BF),
            pltpu.SemaphoreType.DMA((2,)),
            pltpu.SemaphoreType.DMA((2,)),
            pltpu.SemaphoreType.DMA((4,)),
        ],
        VMEM_ALL,
        in_specs=[far] * 4,
        out_specs=(far, far),
    )(
        aux_blocks.transpose(0, 2, 1),
        occ_blocks.transpose(0, 2, 1),
        request_owner.transpose(1, 2, 0),
        request_row.T,
    )


def pack_kernel(naux, route_ref, arrived_ref, old_ref, out_ref):
    share, nsq = old_ref.shape[1:]
    slab = nsq // naux
    part = out_ref.shape[0] // naux
    handed = mm(route_ref[...], arrived_ref[...]).astype(BF)
    pieces = handed.shape[0] // out_ref.shape[0]
    span = out_ref.shape[1] - pieces * LANES
    for x in range(pieces):
        out_ref[:, span + x * LANES : span + (x + 1) * LANES] = handed[
            x * out_ref.shape[0] : (x + 1) * out_ref.shape[0]
        ]
    rows = []
    for member in range(naux):
        row = jnp.concatenate(
            [
                old_ref[member],
                jnp.zeros((share, LANES * (nsq // LANES + 1) - nsq), F32),
                old_ref[naux][:, member * slab : (member + 1) * slab],
                jnp.zeros((share, span - LANES * (nsq // LANES + 1) - slab), F32),
            ],
            axis=1,
        )
        rows.append(jnp.concatenate([row, jnp.zeros((part - share, span), F32)], axis=0))
    out_ref[:, :span] = jnp.concatenate(rows, axis=0).astype(BF)


def block_mask(rows, row_block, cols, col_block):
    row = lax.broadcasted_iota(jnp.int32, (rows, cols), 0) // row_block
    return row == lax.broadcasted_iota(jnp.int32, (rows, cols), 1) // col_block


def fetch_order(naux, chunk, first):
    size = naux * 6 * chunk
    here = jnp.arange(size)
    k, source, piece = here // (naux * chunk), (here // chunk) % naux, here % chunk
    if first:
        part = 6 * chunk // 3
        at = k * chunk + piece
        spot = (at // part) * (naux * part) + source * part + at % part
    else:
        spot = source * 6 * chunk + k * chunk + piece
    return (spot[:, None] == jnp.arange(size)[None, :]).astype(BF)


def project(naux, chunk, ordered, covers, pieces):
    npno, width = covers.shape[1], covers.shape[0]
    half_rows = naux * chunk
    stack = []
    for k in range(3):
        block = ordered[k * half_rows : (k + 1) * half_rows]
        stack += [block[:, :npno], block[:, npno:]]
    stack = jnp.concatenate(stack, axis=0).astype(BF)
    mask = block_mask(3 * npno, npno, width, width // 3)
    half = jnp.where(mask, mm_nt(stack, covers), 0.0).astype(BF)
    return mm_tn(pieces, half).astype(BF)


def residual(naux, chunk, new, covers, pieces, matrix):
    npno, width = covers.shape[1], covers.shape[0]
    half_rows = naux * chunk
    mask = block_mask(3 * npno, npno, width, width // 3)
    high, low = high_low(mm_nt(new, matrix))
    left = jnp.where(mask, mm(pieces, high) + mm(pieces, low), 0.0)
    high, low = high_low(left)
    back = mm(high, covers) + mm(low, covers)
    packed = []
    for k in range(3):
        block = back[2 * k * half_rows : 2 * (k + 1) * half_rows]
        packed.append(jnp.concatenate([block[:half_rows], block[half_rows:]], axis=1))
    return jnp.concatenate(packed, axis=0)


def project_both(naux, chunk, order, came, cover_ref, piece_ref):
    ordered = mm(order, came)
    rows = ordered.shape[0] // 2
    return [
        project(
            naux, chunk, ordered[w * rows : (w + 1) * rows], cover_ref[w], piece_ref[w]
        )
        for w in range(2)
    ]


def work_both(naux, chunk, projs, cover_ref, piece_ref, col_ref, row_ref, states, mats):
    wide = mats[0].shape[1]
    start = up(wide, LANES)
    spans = ((0, wide), (start, start + mats[1].shape[1]))
    new, sent = [], []
    for w in range(2):
        den = col_ref[w] + row_ref[:, spans[w][0] : spans[w][1]]
        new.append((SHIFT_LEVEL * states[w] + mm(projs[w], mats[w])) / den)
    halves = [x.astype(BF) for x in new]
    for w in range(2):
        sent.append(residual(naux, chunk, halves[w], cover_ref[w], piece_ref[w], mats[w]))
    return new, halves, jnp.concatenate(sent, axis=0).astype(BF)


def row_spots(ntno, naux, size):
    share, part = ntno // naux, size // naux
    a = lax.broadcasted_iota(jnp.int32, (ntno, size), 0)
    there = lax.broadcasted_iota(jnp.int32, (ntno, size), 1)
    return ((a // share) * part + a % share == there).astype(F32).astype(BF)


def relayout_kernel(ntno, share, rows_ref, own_ref, last_ref, wide_ref):
    nsq = ntno * ntno
    wide_ref[...] = rows_ref[...].astype(F32)
    own = [wide_ref[pl.ds(b, ntno, stride=ntno), :] for b in range(ntno)]
    last = [wide_ref[pl.ds(nsq + b * ntno, ntno), :] for b in range(share)]
    for parts, out in ((own, own_ref), (last, last_ref)):
        out[...] = jnp.concatenate(
            [
                jnp.concatenate([x[:, m * ntno : (m + 1) * ntno] for x in parts], axis=1)
                for m in range(3)
            ],
            axis=0,
        ).astype(BF)


def first_kernel(
    naux,
    chunk,
    came_ref,
    order_ref,
    later_order_ref,
    cover_ref,
    piece_ref,
    col_ref,
    row_ref,
    own_mat_ref,
    last_mat_ref,
    sent_ref,
    own_ref,
    last_ref,
):
    ntno, nsq = own_ref.shape
    slab = last_ref.shape[1]
    came = came_ref[...]
    size = came.shape[0]
    span = came.shape[1] - 3 * LANES
    start = up(nsq, LANES)
    fetched = jnp.concatenate(
        [came[:, span + x * LANES : span + (x + 1) * LANES] for x in range(3)], axis=0
    )
    projs = project_both(naux, chunk, order_ref[...], fetched, cover_ref, piece_ref)
    old = mm(row_spots(ntno, naux, size), came[:, :span])
    new, _, sent = work_both(
        naux,
        chunk,
        projs,
        cover_ref,
        piece_ref,
        col_ref,
        row_ref,
        (old[:, :nsq], old[:, start : start + slab]),
        (own_mat_ref[...], last_mat_ref[...]),
    )
    own_ref[...] = new[0]
    last_ref[...] = new[1]
    sent_ref[...] = mm_tn(later_order_ref[...], sent).astype(BF)


def later_kernel(
    naux,
    chunk,
    came_ref,
    order_ref,
    last_order_ref,
    cover_ref,
    piece_ref,
    col_ref,
    row_ref,
    own_ref,
    last_ref,
    own_mat_ref,
    last_mat_ref,
    out_ref,
    wide_ref,
):
    ntno, nsq = own_ref.shape
    size, width = out_ref.shape
    span = width - 3 * LANES
    start, slab = up(nsq, LANES), last_ref.shape[1]
    projs = project_both(naux, chunk, order_ref[...], came_ref[...], cover_ref, piece_ref)
    _, halves, sent = work_both(
        naux,
        chunk,
        projs,
        cover_ref,
        piece_ref,
        col_ref,
        row_ref,
        (own_ref[...], last_ref[...]),
        (own_mat_ref[...], last_mat_ref[...]),
    )
    wide_ref[...] = jnp.zeros(wide_ref.shape, BF)
    wide_ref[:, :nsq] = halves[0]
    wide_ref[:, start : start + slab] = halves[1]
    out_ref[:, :span] = mm_tn(row_spots(ntno, naux, size), wide_ref[...]).astype(BF)
    sent = mm_tn(last_order_ref[...], sent).astype(BF)
    for x in range(3):
        out_ref[:, span + x * LANES : span + (x + 1) * LANES] = sent[x * size : (x + 1) * size]


def finish_kernel(naux, came_ref, out_ref):
    share, nsq = out_ref.shape[1:]
    start, slab = up(nsq, LANES), nsq // naux
    part = came_ref.shape[0] // naux
    came = came_ref[:, : up(start + slab, LANES)].astype(F32)
    last = []
    for member in range(naux):
        rows = came[member * part : member * part + share]
        out_ref[member] = rows[:, :nsq]
        last.append(rows[:, start : start + slab])
    out_ref[naux] = jnp.concatenate(last, axis=1)


def body(
    aux_blocks,
    occ_blocks,
    intersections,
    tno_energy,
    occ_energy,
    tno_rank,
    triples_old,
    pair_amps,
    pno_energy,
    pair_occ,
    pair_rank,
    request_owner,
    request_row,
):
    tdev = aux_blocks.shape[0]
    ntno = tno_energy.shape[1]
    npno = pno_energy.shape[1]
    pdev = pair_amps.shape[0]
    naux = lax.axis_size("aux")
    ntrip = lax.axis_size("trip")
    member = lax.axis_index("aux")
    share = ntno // naux
    nreq = 3 * tdev
    nsq = ntno * ntno
    slab = share * ntno
    start = up(nsq, LANES)
    span = start + up(slab, LANES)
    prow = npno // naux
    chunk = prow * npno // LANES
    slots = ntrip * chunk
    owner = request_owner.reshape(nreq)

    blocks, asking = integral_blocks(
        aux_blocks, occ_blocks, request_owner, request_row, naux, ntrip, chunk
    )
    rows = lax.psum_scatter(blocks, "aux", scatter_dimension=0, tiled=True)[0]
    serve = swap(asking, "trip").reshape(slots, LANES)

    def routing(dest, at):
        k, part = at // chunk, at % chunk
        request = jnp.where(k < 3, 3 * dest + k, 3 * naux + k - 3)
        asked = jnp.sum(
            jnp.where(request[:, None] == jnp.arange(nreq)[None, :], owner[None, :], 0), axis=1
        )
        return ((asked * chunk + part)[:, None] == jnp.arange(slots)[None, :]).astype(BF)

    number = jnp.arange(naux * 6 * chunk)
    route = routing(number // (6 * chunk), number % (6 * chunk))
    part = 6 * chunk // 3
    route_first = routing(
        (number // part) % naux, number // (naux * part) * part + number % part
    )
    route_back, route_last = route.T, route_first.T
    order, order_first = fetch_order(naux, chunk, False), fetch_order(naux, chunk, True)

    live = jnp.arange(npno)[None, :] < pair_rank[:, None]
    live_p = lax.dynamic_slice_in_dim(live, member * prow, prow, 1)
    energy_p = lax.dynamic_slice_in_dim(pno_energy, member * prow, prow, 1)
    pair_keep = (live_p[:, :, None] & live[:, None, :]).reshape(pdev * chunk, LANES)
    pair_den = (
        energy_p[:, :, None] + pno_energy[:, None, :] + pair_occ[:, None, None] + SHIFT_LEVEL
    ).reshape(pdev * chunk, LANES)
    amps = (
        lax.dynamic_slice_in_dim(pair_amps, member * prow * npno, prow * npno, 1)
        .reshape(pdev * chunk, LANES)
        .astype(F32)
    )
    gain = jnp.zeros_like(amps)

    def two(x):
        return jnp.stack([lax.dynamic_slice_in_dim(x, member, 1, 0)[0], x[naux]])

    masked = jnp.where(jnp.arange(ntno)[None, :] < tno_rank[:, None], tno_energy, jnp.inf)
    energy = two(masked)
    col = two(masked - jnp.sum(occ_energy, axis=1)[:, None] + SHIFT_LEVEL)[:, :, None]
    energy_b = lax.dynamic_slice_in_dim(energy[1], member * share, share, 0)
    row = jnp.concatenate(
        [
            (energy[0][:, None] + energy[0][None, :]).reshape(nsq),
            jnp.zeros((start - nsq,), F32),
            (energy_b[:, None] + energy[1][None, :]).reshape(slab),
            jnp.zeros((span - start - slab,), F32),
        ]
    )[None, :]
    cover = two(intersections)
    flat = cover.transpose(0, 1, 3, 2).reshape(2, 3 * ntno, npno)
    split = cover.reshape(2, 3, npno // 2, 2, ntno).transpose(0, 1, 3, 2, 4)
    split = split.reshape(2, 3 * npno, ntno)

    ready = (
        (serve, route, route_first, route_back, route_last, order, order_first)
        + (pair_keep, pair_den, amps, flat, split, col, row)
    )
    serve, route, route_first, route_back, route_last, order, order_first, *ready = (
        lax.optimization_barrier(ready)
    )
    pair_keep, pair_den, amps, flat, split, col, row = ready
    width = span + 3 * LANES

    for step in range(PASSES):
        outgoing = jnp.where(pair_keep, amps.astype(BF), jnp.zeros((), BF))
        pad = serve.shape[1] - outgoing.shape[0]
        found = mm(serve, jnp.pad(outgoing, ((0, pad), (0, 0)))).astype(BF)
        arrived = swap(found.reshape(ntrip, chunk, LANES), "trip").reshape(slots, LANES)
        if step == 0:
            packed = call(
                functools.partial(pack_kernel, naux),
                jax.ShapeDtypeStruct((naux * part, width), BF),
            )(route_first, arrived, triples_old)
            came = swap(packed.reshape(naux, part, width), "aux")
        else:
            handed = mm(route, arrived).astype(BF).reshape(naux, 6 * chunk, LANES)
            came = swap(handed, "aux")
        if step == 0:
            own_mat, last_mat = call(
                functools.partial(relayout_kernel, ntno, share),
                (
                    jax.ShapeDtypeStruct((3 * ntno, nsq), BF),
                    jax.ShapeDtypeStruct((3 * ntno, slab), BF),
                ),
                [pltpu.VMEM(rows.shape, F32)],
            )(rows)
            sent, own, last = call(
                functools.partial(first_kernel, naux, chunk),
                (
                    jax.ShapeDtypeStruct((naux * 6 * chunk, LANES), BF),
                    jax.ShapeDtypeStruct((ntno, nsq), F32),
                    jax.ShapeDtypeStruct((ntno, slab), F32),
                ),
            )(
                came.reshape(-1, width),
                order_first,
                order,
                flat,
                split,
                col,
                row,
                own_mat,
                last_mat,
            )
            came = swap(sent.reshape(naux, 6 * chunk, LANES), "aux")
            sent = mm(route_back, came.reshape(naux * 6 * chunk, LANES))
        else:
            sent = call(
                functools.partial(later_kernel, naux, chunk),
                jax.ShapeDtypeStruct((naux * part, width), BF),
                [pltpu.VMEM((ntno, span), BF)],
            )(
                came.reshape(-1, LANES),
                order,
                order_first,
                flat,
                split,
                col,
                row,
                own,
                last,
                own_mat,
                last_mat,
            )
            came = swap(sent.reshape(naux, part, width), "aux").reshape(naux * part, width)
            triples_new = call(
                functools.partial(finish_kernel, naux),
                jax.ShapeDtypeStruct((tdev, share, nsq), F32),
            )(came)
            back = [came[:, span + x * LANES : span + (x + 1) * LANES] for x in range(3)]
            sent = mm(route_last, jnp.concatenate(back, axis=0))
        sent = sent.astype(BF).reshape(ntrip, chunk, LANES)
        came = swap(sent, "trip").reshape(slots, LANES)
        total = mm_tn(serve, came)[: pdev * chunk]
        change = jnp.where(pair_keep, total / pair_den, 0.0)
        gain = gain + change
        amps = amps + change

    gains = jnp.broadcast_to(gain.astype(BF)[None], (naux, pdev * chunk, LANES))
    gains = swap(gains, "aux").reshape(naux, pdev, prow * npno).transpose(1, 0, 2)
    pairs_new = pair_amps.astype(F32) + gains.reshape(pdev, npno * npno).astype(F32)
    return triples_new, pairs_new


def solution(mesh):
    in_specs = (
        P("trip", "aux", None),
        P("trip", "aux", None),
        P("trip", None, None, None),
        P("trip", None),
        P("trip", None),
        P("trip"),
        P("trip", "aux", None),
        P("trip", None),
        P("trip", None),
        P("trip"),
        P("trip"),
        P("trip", None, None),
        P("trip", None),
    )
    out_specs = (P("trip", "aux", None), P("trip", None))
    return jax.shard_map(body, mesh=mesh, in_specs=in_specs, out_specs=out_specs, check_vma=False)
```

time: 195 us -> 186 us (0.954)
  blocking collectives: 64 us -> 101 us
  waiting for transfers between devices: 48.8 us -> 20.4 us
  starting transfers between devices: 40.6 us -> 32.4 us
  other arithmetic: 6.6 us -> 1.85 us
  local copies, waits for them, and re-layouts: 7.87 us -> 3.87 us
    all_to_all x5 -> x7, blocking collectives: 64 us -> 101 us  [swap(): return lax.all_to_all(x, axis, split_axis=0, concat_axis=0, tiled=True)]
    all_to_all x5 -> x3, waiting for transfers between devices: 48.8 us -> 20.4 us  [swap(): return lax.all_to_all(x, axis, split_axis=0, concat_axis=0, tiled=True)]
    all_to_all x5 -> x3, starting transfers between devices: 40.5 us -> 32.4 us  [swap(): return lax.all_to_all(x, axis, split_axis=0, concat_axis=0, tiled=True)]
    unnamed x25 -> x23, local copies, waits for them, and re-layouts: 5.03 us -> 1.35 us
    pallas_call x2 -> x4, Pallas kernels: 5.62 us -> 8.04 us  [the longest x1 4.87 us: integral_blocks(): call(functools.partial(blocks_kernel, naux, share), (jax.ShapeDtypeStruct...]
  transfers between devices with their start and end apart: 7 -> 4, of which waited for: 5 -> 3; matrix products, arithmetic and copies ran while one was open for 4% -> 2% of each run, Pallas kernels for 0% -> 1%
where the time goes in v4:
time: 186 us; the launch traced here: 185 us
  blocking collectives  101 us (54%)
  starting transfers between devices  32.4 us (17%)
  waiting for transfers between devices  20.4 us (11%)
  between operations  14.4 us (8%)
  Pallas kernels  10.7 us (6%)
  local copies, waits for them, and re-layouts  3.87 us (2%)
    all_to_all x7, blocking collectives, swap(): return lax.all_to_all(x, axis, split_axis=0, concat_axis=0, tiled=True)  101 us
    all_to_all x3, starting transfers between devices, swap(): return lax.all_to_all(x, axis, split_axis=0, concat_axis=0, tiled=True)  32.4 us
    all_to_all x3, waiting for transfers between devices, swap(): return lax.all_to_all(x, axis, split_axis=0, concat_axis=0, tiled=True)  20.4 us
    pallas_call x1, Pallas kernels, integral_blocks(): call(functools.partial(blocks_kernel, naux, share), (jax.ShapeDtypeStruct...  4.87 us
  transfers between devices with their start and end apart: 4, of which 3 were waited for; matrix products, arithmetic and copies ran while one was open for 2% of the time, Pallas kernels for 1%

profile of v4, /device:TPU:1, one launch (start us, length us, event | category | flops | bytes accessed | tf_op | source)
XLA Modules:
  0.0 185.4 jit_solution(16790798182338275756)
XLA Ops:
  7.3 4.9 %shard_map.140 = (bf16[8,1808,128]{2,1,0:T(8,128)(2,1)}, bf16[64,4,128]{2,1,0:T(4,128)(2,1)}) custom-call(bf16[9,1600,128]{2,1,0:T(8,128)(2,1)} %bitcast.63, bf16[9,120,128]{2,1,0:T(8,128)(2,1)} %bitcast.71, s32[3,1,9]{2,1,0:T(1,128)} %bitcast.81, s32[3,9]{1,0:T(4,128)} %bitcast.82), custom_call_target="tpu_custom_call" | custom-call | tf_op jit(solution)/shard_map/pallas_call | solution.py:140
  12.2 19.3 %all-to-all-start = ((bf16[64,4,128]{2,1,0:T(4,128)(2,1)}), bf16[64,4,128]{2,1,0:T(4,128)(2,1)S(1)}, u32[]{:S(2)}, u32[]{:S(2)}) async-start(bf16[64,4,128]{2,1,0:T(4,128)(2,1)} %get-tuple-element.23), calls=%async_computation | async-start | bytes 131072 | tf_op jit(solution)/shard_map/all_to_all | solution.py:36
  31.5 0.1 copy.34
  31.6 0.1 broadcast_in_dim.42
  31.7 0.8 constant_dynamic-slice_fusion.2
  32.5 0.1 copy.42
  32.6 0.1 copy.43
  33.2 0.1 select_reduce_fusion
  33.4 0.1 broadcast_and_fusion
  33.6 0.1 add_add_fusion
  33.7 0.1 fusion.9.order_ref.last_order_ref
  33.8 0.1 fusion.6
  33.9 0.1 fusion.7.route_ref
  34.0 0.1 fusion.8.later_order_ref.order_ref
  34.1 0.1 and.268
  34.2 0.1 add.385
  34.3 0.1 add.378
  34.4 0.1 concatenate.6
  34.6 0.1 copy.37
  34.7 10.7 %all-to-all-done = bf16[64,4,128]{2,1,0:T(4,128)(2,1)S(1)} async-done(((bf16[64,4,128]{2,1,0:T(4,128)(2,1)}), bf16[64,4,128]{2,1,0:T(4,128)(2,1)S(1)}, u32[]{:S(2)}, u32[]{:S(2)}) %all-to-all-start) | async-done | bytes 65568 | tf_op jit(solution)/shard_map/all_to_all | solution.py:36
  45.5 0.1 convolution_convert_fusion.1
  45.6 17.9 %all_to_all.50 = bf16[64,4,128]{2,1,0:T(4,128)(2,1)S(1)} all-to-all(bf16[64,4,128]{2,1,0:T(4,128)(2,1)S(1)} %bitcast.73), channel_id=1, replica_groups=mesh['trip'=64,'aux'=8] {'trip'}, dimensions={0} | all-to-all | bytes 131072 | tf_op jit(solution)/shard_map/all_to_all | solution.py:36
  63.5 0.9 shard_map.141
  64.4 7.8 %all-to-all-start.2 = ((bf16[8,8,2304]{2,1,0:T(8,128)(2,1)}), bf16[8,8,2304]{2,1,0:T(8,128)(2,1)S(1)}, u32[]{:S(2)}, u32[]{:S(2)}) async-start(bf16[8,8,2304]{2,1,0:T(8,128)(2,1)} %bitcast.16), calls=%async_computation.2 | async-start | bytes 589824 | tf_op jit(solution)/shard_map/all_to_all | solution.py:36
  72.2 0.1 copy.39.col_ref
  72.3 1.0 copy-done.1
  73.3 0.5 shard_map.142
  73.8 5.2 %all-to-all-done.2 = bf16[8,8,2304]{2,1,0:T(8,128)(2,1)S(1)} async-done(((bf16[8,8,2304]{2,1,0:T(8,128)(2,1)}), bf16[8,8,2304]{2,1,0:T(8,128)(2,1)S(1)}, u32[]{:S(2)}, u32[]{:S(2)}) %all-to-all-start.2) | async-done | bytes 294944 | tf_op jit(solution)/shard_map/all_to_all | solution.py:36
  79.0 1.8 shard_map.143
  80.8 8.2 %all_to_all.51 = bf16[8,24,128]{2,1,0:T(8,128)(2,1)S(1)} all-to-all(bf16[8,24,128]{2,1,0:T(8,128)(2,1)S(1)} %bitcast.62), channel_id=1, replica_groups=mesh['trip'=64,'aux'=8] {'aux'}, dimensions={0} | all-to-all | bytes 98304 | tf_op jit(solution)/shard_map/all_to_all | solution.py:36
  89.1 0.2 convolution_convert_fusion.3
  89.3 17.8 %all_to_all.52 = bf16[64,4,128]{2,1,0:T(4,128)(2,1)S(1)} all-to-all(bf16[64,4,128]{2,1,0:T(4,128)(2,1)S(1)} %bitcast.75), channel_id=1, replica_groups=mesh['trip'=64,'aux'=8] {'trip'}, dimensions={0} | all-to-all | bytes 131072 | tf_op jit(solution)/shard_map/all_to_all | solution.py:36
  107.1 0.2 fusion.19
  107.2 0.1 convolution_convert_fusion
  107.4 18.4 %all_to_all.53 = bf16[64,4,128]{2,1,0:T(4,128)(2,1)S(1)} all-to-all(bf16[64,4,128]{2,1,0:T(4,128)(2,1)S(1)} %bitcast.74), channel_id=1, replica_groups=mesh['trip'=64,'aux'=8] {'trip'}, dimensions={0} | all-to-all | bytes 131072 | tf_op jit(solution)/shard_map/all_to_all | solution.py:36
  125.8 0.2 convolution_convert_fusion.4
  126.0 10.0 %all_to_all.54 = bf16[8,24,128]{2,1,0:T(8,128)(2,1)S(1)} all-to-all(bf16[8,24,128]{2,1,0:T(8,128)(2,1)S(1)} %bitcast.77), channel_id=1, replica_groups=mesh['trip'=64,'aux'=8] {'aux'}, dimensions={0} | all-to-all | bytes 98304 | tf_op jit(solution)/shard_map/all_to_all | solution.py:36
  135.9 1.8 shard_map.144
  137.8 10.4 %all_to_all.55 = bf16[8,8,2304]{2,1,0:T(8,128)(2,1)S(1)} all-to-all(bf16[8,8,2304]{2,1,0:T(8,128)(2,1)S(1)} %bitcast.54), channel_id=1, replica_groups=mesh['trip'=64,'aux'=8] {'aux'}, dimensions={0} | all-to-all | bytes 589824 | tf_op jit(solution)/shard_map/all_to_all | solution.py:36
  148.2 0.2 convolution_convert_fusion.2
  148.4 17.8 %all_to_all.56 = bf16[64,4,128]{2,1,0:T(4,128)(2,1)S(1)} all-to-all(bf16[64,4,128]{2,1,0:T(4,128)(2,1)S(1)} %bitcast.80), channel_id=1, replica_groups=mesh['trip'=64,'aux'=8] {'trip'}, dimensions={0} | all-to-all | bytes 131072 | tf_op jit(solution)/shard_map/all_to_all | solution.py:36
  166.2 0.2 fusion.3
  166.4 0.7 broadcast_in_dim.83
  167.1 5.3 %all-to-all-start.9 = ((bf16[8,64,128]{2,1,0:T(8,128)(2,1)}), bf16[8,64,128]{2,1,0:T(8,128)(2,1)S(1)}, u32[]{:S(2)}, u32[]{:S(2)}) async-start(bf16[8,64,128]{2,1,0:T(8,128)(2,1)} %broadcast_in_dim.83), calls=%async_computation.10 | async-start | bytes 262144 | tf_op jit(solution)/shard_map/all_to_all | solution.py:36
  172.4 0.9 shard_map.145
  173.2 4.4 %all-to-all-done.9 = bf16[8,64,128]{2,1,0:T(8,128)(2,1)S(1)} async-done(((bf16[8,64,128]{2,1,0:T(8,128)(2,1)}), bf16[8,64,128]{2,1,0:T(8,128)(2,1)S(1)}, u32[]{:S(2)}, u32[]{:S(2)}) %all-to-all-start.9) | async-done | bytes 131104 | tf_op jit(solution)/shard_map/all_to_all | solution.py:36
  177.7 0.1 reshape.351
  177.8 0.7 convert_add_fusion
  (49 shorter events, 1.0 us)
Async XLA Ops:
  7.2 65.1 %reduce-scatter.2.cloned.1.call-start = ((), (), s32[]{:S(2)}) async-start(), calls=%async_computation.11 | async-start | bytes 4165632 | tf_op jit(solution)/shard_map/reduce_scatter | solution.py:422
  7.2 24.3 %copy-start.5 = (s32[9,3,1]{0,2,1:T(1,128)S(1)}, s32[9,3,1]{0,2,1:T(1,128)}, u32[]{:S(2)}) copy-start(s32[9,3,1]{0,2,1:T(1,128)} %param.24) | copy-start | bytes 328
  7.2 25.4 %copy-start.6 = (f32[9,3]{0,1:T(4,128)S(1)}, f32[9,3]{0,1:T(4,128)}, u32[]{:S(2)}) copy-start(f32[9,3]{0,1:T(4,128)} %param.17) | copy-start | bytes 328
  7.2 25.5 %copy-start.4 = (f32[9,40]{1,0:T(8,128)S(1)}, f32[9,40]{1,0:T(8,128)}, u32[]{:S(2)}) copy-start(f32[9,40]{1,0:T(8,128)} %param.16) | copy-start | bytes 4324
  7.2 25.5 %copy-start.8 = (s32[9]{0:T(128)S(1)}, s32[9]{0:T(128)}, u32[]{:S(2)}) copy-start(s32[9]{0:T(128)} %param.18) | copy-start | bytes 112
  7.3 25.7 %copy-start.9 = (s32[16]{0:T(128)S(1)}, s32[16]{0:T(128)}, u32[]{:S(2)}) copy-start(s32[16]{0:T(128)} %param.23) | copy-start | bytes 196
  7.3 25.8 %copy-start.3 = (f32[16,64]{1,0:T(8,128)S(1)}, f32[16,64]{1,0:T(8,128)}, u32[]{:S(2)}) copy-start(f32[16,64]{1,0:T(8,128)} %param.21) | copy-start | bytes 12292
  7.3 25.9 %copy-start.2 = (bf16[16,4096]{1,0:T(8,128)(2,1)S(1)}, bf16[16,4096]{1,0:T(8,128)(2,1)}, u32[]{:S(2)}) copy-start(bf16[16,4096]{1,0:T(8,128)(2,1)} %param.20) | copy-start | bytes 393220
  7.3 26.3 %copy-start.7 = (f32[16]{0:T(128)S(1)}, f32[16]{0:T(128)}, u32[]{:S(2)}) copy-start(f32[16]{0:T(128)} %param.22) | copy-start | bytes 196
  12.2 51.4 %copy-start = (f32[9,5,1600]{2,1,0:T(8,128)S(1)}, f32[9,5,1600]{2,1,0:T(8,128)}, u32[]{:S(2)}) copy-start(f32[9,5,1600]{2,1,0:T(8,128)} %old_ref.1) | copy-start | bytes 864004
  12.2 33.3 %all-to-all-start = ((bf16[64,4,128]{2,1,0:T(4,128)(2,1)}), bf16[64,4,128]{2,1,0:T(4,128)(2,1)S(1)}, u32[]{:S(2)}, u32[]{:S(2)}) async-start(bf16[64,4,128]{2,1,0:T(4,128)(2,1)} %get-tuple-element.23), calls=%async_computation | async-start | bytes 131072 | tf_op jit(solution)/shard_map/all_to_all | solution.py:36
  64.4 14.6 %all-to-all-start.2 = ((bf16[8,8,2304]{2,1,0:T(8,128)(2,1)}), bf16[8,8,2304]{2,1,0:T(8,128)(2,1)S(1)}, u32[]{:S(2)}, u32[]{:S(2)}) async-start(bf16[8,8,2304]{2,1,0:T(8,128)(2,1)} %bitcast.16), calls=%async_computation.2 | async-start | bytes 589824 | tf_op jit(solution)/shard_map/all_to_all | solution.py:36
  72.3 1.0 copy-start.1
  167.1 10.6 %all-to-all-start.9 = ((bf16[8,64,128]{2,1,0:T(8,128)(2,1)}), bf16[8,64,128]{2,1,0:T(8,128)(2,1)S(1)}, u32[]{:S(2)}, u32[]{:S(2)}) async-start(bf16[8,64,128]{2,1,0:T(8,128)(2,1)} %broadcast_in_dim.83), calls=%async_computation.10 | async-start | bytes 262144 | tf_op jit(solution)/shard_map/all_to_all | solution.py:36
Sparse Core Ops, SparseCore 0:
  12.3 48.2 reduce-scatter.1

commit v5 on v4

--- a/solution.py
+++ b/solution.py
@@ -166,30 +166,84 @@
     )
 
 
-def pack_kernel(naux, route_ref, arrived_ref, old_ref, out_ref):
+def row_spots(ntno, naux, size, parity=None):
+    share, part = ntno // naux, size // naux
+    a = lax.broadcasted_iota(jnp.int32, (ntno, size), 0)
+    there = lax.broadcasted_iota(jnp.int32, (ntno, size), 1)
+    member, place = a // share, a % share
+    if parity is None:
+        hit = member * part + place == there
+    else:
+        hit = (member * part + share + place // 2 == there) & (place % 2 == parity)
+    return hit.astype(F32).astype(BF)
+
+
+def spread(ntno, naux, own, last, pieces, out_ref):
+    size, width = out_ref.shape
+    share, part = ntno // naux, size // naux
+    tiles = 0 if pieces is None else pieces.shape[0] // size
+    first = width - 5 * LANES
+    for parity in range(2):
+        add = mm_tn(row_spots(ntno, naux, size, parity), last)
+        low = first + 2 * parity * LANES
+        out_ref[:, low : low + 2 * LANES] = (own[:, low : low + 2 * LANES] + add).astype(BF)
+    for x in range(tiles):
+        low = x * LANES
+        piece = pieces[x * size : (x + 1) * size]
+        out_ref[:, low : low + LANES] = (own[:, low : low + LANES] + piece).astype(BF)
+    if tiles == 0:
+        out_ref[:, :first] = own[:, :first].astype(BF)
+    out_ref[:, first + 4 * LANES :] = own[:, first + 4 * LANES :].astype(BF)
+
+
+def gather_last(ntno, naux, came):
+    size, width = came.shape
+    first = width - 5 * LANES
+    return sum(
+        mm(
+            row_spots(ntno, naux, size, parity),
+            came[:, first + 2 * parity * LANES : first + 2 * (parity + 1) * LANES],
+        )
+        for parity in range(2)
+    )
+
+
+def gather_pieces(came):
+    tiles = came.shape[1] // LANES - 5
+    return jnp.concatenate([came[:, x * LANES : (x + 1) * LANES] for x in range(tiles)], axis=0)
+
+
+def old_kernel(naux, old_ref, out_ref):
     share, nsq = old_ref.shape[1:]
     slab = nsq // naux
-    part = out_ref.shape[0] // naux
-    handed = mm(route_ref[...], arrived_ref[...]).astype(BF)
-    pieces = handed.shape[0] // out_ref.shape[0]
-    span = out_ref.shape[1] - pieces * LANES
-    for x in range(pieces):
-        out_ref[:, span + x * LANES : span + (x + 1) * LANES] = handed[
-            x * out_ref.shape[0] : (x + 1) * out_ref.shape[0]
-        ]
-    rows = []
+    size, width = out_ref.shape
+    part = size // naux
+    own, last = [], []
     for member in range(naux):
-        row = jnp.concatenate(
-            [
-                old_ref[member],
-                jnp.zeros((share, LANES * (nsq // LANES + 1) - nsq), F32),
-                old_ref[naux][:, member * slab : (member + 1) * slab],
-                jnp.zeros((share, span - LANES * (nsq // LANES + 1) - slab), F32),
-            ],
-            axis=1,
+        row = jnp.concatenate([old_ref[member], jnp.zeros((share, width - nsq), F32)], axis=1)
+        own.append(jnp.concatenate([row, jnp.zeros((part - share, width), F32)], axis=0))
+        last.append(
+            jnp.concatenate(
+                [
+                    old_ref[naux][:, member * slab : (member + 1) * slab],
+                    jnp.zeros((share, 2 * LANES - slab), F32),
+                ],
+                axis=1,
+            )
         )
-        rows.append(jnp.concatenate([row, jnp.zeros((part - share, span), F32)], axis=0))
-    out_ref[:, :span] = jnp.concatenate(rows, axis=0).astype(BF)
+    own, last = jnp.concatenate(own, axis=0), jnp.concatenate(last, axis=0).astype(BF)
+    spread(share * naux, naux, own, last, None, out_ref)
+
+
+def pack_kernel(route_ref, arrived_ref, old_ref, out_ref):
+    size = out_ref.shape[0]
+    handed = mm(route_ref[...], arrived_ref[...])
+    tiles = handed.shape[0] // size
+    for x in range(tiles):
+        low = x * LANES
+        piece = handed[x * size : (x + 1) * size] + old_ref[:, low : low + LANES].astype(F32)
+        out_ref[:, low : low + LANES] = piece.astype(BF)
+    out_ref[:, tiles * LANES :] = old_ref[:, tiles * LANES :]
 
 
 def block_mask(rows, row_block, cols, col_block):
@@ -197,16 +251,17 @@
     return row == lax.broadcasted_iota(jnp.int32, (rows, cols), 1) // col_block
 
 
-def fetch_order(naux, chunk, first):
+def fetch_order(naux, chunk, wide=None):
     size = naux * 6 * chunk
     here = jnp.arange(size)
     k, source, piece = here // (naux * chunk), (here // chunk) % naux, here % chunk
-    if first:
-        part = 6 * chunk // 3
-        at = k * chunk + piece
-        spot = (at // part) * (naux * part) + source * part + at % part
+    at = k * chunk + piece
+    if wide is None:
+        spot = source * 6 * chunk + at
     else:
-        spot = source * 6 * chunk + k * chunk + piece
+        share, part, tiles = wide
+        size = tiles * naux * part
+        spot = (at % tiles) * (naux * part) + source * part + share + at // tiles
     return (spot[:, None] == jnp.arange(size)[None, :]).astype(BF)
 
 
@@ -261,13 +316,6 @@
     for w in range(2):
         sent.append(residual(naux, chunk, halves[w], cover_ref[w], piece_ref[w], mats[w]))
     return new, halves, jnp.concatenate(sent, axis=0).astype(BF)
-
-
-def row_spots(ntno, naux, size):
-    share, part = ntno // naux, size // naux
-    a = lax.broadcasted_iota(jnp.int32, (ntno, size), 0)
-    there = lax.broadcasted_iota(jnp.int32, (ntno, size), 1)
-    return ((a // share) * part + a % share == there).astype(F32).astype(BF)
 
 
 def relayout_kernel(ntno, share, rows_ref, own_ref, last_ref, wide_ref):
@@ -304,14 +352,10 @@
     ntno, nsq = own_ref.shape
     slab = last_ref.shape[1]
     came = came_ref[...]
-    size = came.shape[0]
-    span = came.shape[1] - 3 * LANES
-    start = up(nsq, LANES)
-    fetched = jnp.concatenate(
-        [came[:, span + x * LANES : span + (x + 1) * LANES] for x in range(3)], axis=0
-    )
-    projs = project_both(naux, chunk, order_ref[...], fetched, cover_ref, piece_ref)
-    old = mm(row_spots(ntno, naux, size), came[:, :span])
+    pieces = gather_pieces(came)
+    projs = project_both(naux, chunk, order_ref[...], pieces, cover_ref, piece_ref)
+    old = mm(row_spots(ntno, naux, came.shape[0]), came)
+    old_last = gather_last(ntno, naux, came)
     new, _, sent = work_both(
         naux,
         chunk,
@@ -320,7 +364,7 @@
         piece_ref,
         col_ref,
         row_ref,
-        (old[:, :nsq], old[:, start : start + slab]),
+        (old[:, :nsq], old_last[:, :slab]),
         (own_mat_ref[...], last_mat_ref[...]),
     )
     own_ref[...] = new[0]
@@ -344,11 +388,10 @@
     last_mat_ref,
     out_ref,
     wide_ref,
+    edge_ref,
 ):
     ntno, nsq = own_ref.shape
-    size, width = out_ref.shape
-    span = width - 3 * LANES
-    start, slab = up(nsq, LANES), last_ref.shape[1]
+    slab = last_ref.shape[1]
     projs = project_both(naux, chunk, order_ref[...], came_ref[...], cover_ref, piece_ref)
     _, halves, sent = work_both(
         naux,
@@ -363,23 +406,25 @@
     )
     wide_ref[...] = jnp.zeros(wide_ref.shape, BF)
     wide_ref[:, :nsq] = halves[0]
-    wide_ref[:, start : start + slab] = halves[1]
-    out_ref[:, :span] = mm_tn(row_spots(ntno, naux, size), wide_ref[...]).astype(BF)
-    sent = mm_tn(last_order_ref[...], sent).astype(BF)
-    for x in range(3):
-        out_ref[:, span + x * LANES : span + (x + 1) * LANES] = sent[x * size : (x + 1) * size]
-
-
-def finish_kernel(naux, came_ref, out_ref):
+    edge_ref[...] = jnp.zeros(edge_ref.shape, BF)
+    edge_ref[:, :slab] = halves[1]
+    own = mm_tn(row_spots(ntno, naux, out_ref.shape[0]), wide_ref[...])
+    pieces = mm_tn(last_order_ref[...], sent)
+    spread(ntno, naux, own, edge_ref[...], pieces, out_ref)
+
+
+def finish_kernel(naux, came_ref, route_ref, out_ref, sent_ref):
     share, nsq = out_ref.shape[1:]
-    start, slab = up(nsq, LANES), nsq // naux
+    ntno, slab = share * naux, nsq // naux
     part = came_ref.shape[0] // naux
-    came = came_ref[:, : up(start + slab, LANES)].astype(F32)
+    came = came_ref[...]
+    sent_ref[...] = mm(route_ref[...], gather_pieces(came)).astype(BF)
+    edge = gather_last(ntno, naux, came)
+    came = came.astype(F32)
     last = []
     for member in range(naux):
-        rows = came[member * part : member * part + share]
-        out_ref[member] = rows[:, :nsq]
-        last.append(rows[:, start : start + slab])
+        out_ref[member] = came[member * part : member * part + share, :nsq]
+        last.append(edge[member * share : (member + 1) * share, :slab])
     out_ref[naux] = jnp.concatenate(last, axis=1)
 
 
@@ -432,12 +477,21 @@
 
     number = jnp.arange(naux * 6 * chunk)
     route = routing(number // (6 * chunk), number % (6 * chunk))
-    part = 6 * chunk // 3
+    part = 8
+    tiles = 6 * chunk // (part - share)
+    size, width = naux * part, start
+    number = jnp.arange(tiles * size)
+    place = number % part
     route_first = routing(
-        (number // part) % naux, number // (naux * part) * part + number % part
-    )
+        (number % size) // part, jnp.maximum(place - share, 0) * tiles + number // size
+    )
+    route_first = jnp.where((place >= share)[:, None], route_first, jnp.zeros((), BF))
+    packed_old = call(
+        functools.partial(old_kernel, naux), jax.ShapeDtypeStruct((size, width), BF)
+    )(triples_old)
     route_back, route_last = route.T, route_first.T
-    order, order_first = fetch_order(naux, chunk, False), fetch_order(naux, chunk, True)
+    order = fetch_order(naux, chunk)
+    order_first = fetch_order(naux, chunk, (share, part, tiles))
 
     live = jnp.arange(npno)[None, :] < pair_rank[:, None]
     live_p = lax.dynamic_slice_in_dim(live, member * prow, prow, 1)
@@ -475,24 +529,21 @@
 
     ready = (
         (serve, route, route_first, route_back, route_last, order, order_first)
-        + (pair_keep, pair_den, amps, flat, split, col, row)
+        + (pair_keep, pair_den, amps, flat, split, col, row, packed_old)
     )
     serve, route, route_first, route_back, route_last, order, order_first, *ready = (
         lax.optimization_barrier(ready)
     )
-    pair_keep, pair_den, amps, flat, split, col, row = ready
-    width = span + 3 * LANES
-
+    pair_keep, pair_den, amps, flat, split, col, row, packed_old = ready
     for step in range(PASSES):
         outgoing = jnp.where(pair_keep, amps.astype(BF), jnp.zeros((), BF))
         pad = serve.shape[1] - outgoing.shape[0]
         found = mm(serve, jnp.pad(outgoing, ((0, pad), (0, 0)))).astype(BF)
         arrived = swap(found.reshape(ntrip, chunk, LANES), "trip").reshape(slots, LANES)
         if step == 0:
-            packed = call(
-                functools.partial(pack_kernel, naux),
-                jax.ShapeDtypeStruct((naux * part, width), BF),
-            )(route_first, arrived, triples_old)
+            packed = call(pack_kernel, jax.ShapeDtypeStruct((size, width), BF))(
+                route_first, arrived, packed_old
+            )
             came = swap(packed.reshape(naux, part, width), "aux")
         else:
             handed = mm(route, arrived).astype(BF).reshape(naux, 6 * chunk, LANES)
@@ -529,8 +580,8 @@
         else:
             sent = call(
                 functools.partial(later_kernel, naux, chunk),
-                jax.ShapeDtypeStruct((naux * part, width), BF),
-                [pltpu.VMEM((ntno, span), BF)],
+                jax.ShapeDtypeStruct((size, width), BF),
+                [pltpu.VMEM((ntno, width), BF), pltpu.VMEM((ntno, 2 * LANES), BF)],
             )(
                 came.reshape(-1, LANES),
                 order,
@@ -544,13 +595,14 @@
                 own_mat,
                 last_mat,
             )
-            came = swap(sent.reshape(naux, part, width), "aux").reshape(naux * part, width)
-            triples_new = call(
+            came = swap(sent.reshape(naux, part, width), "aux").reshape(size, width)
+            triples_new, sent = call(
                 functools.partial(finish_kernel, naux),
-                jax.ShapeDtypeStruct((tdev, share, nsq), F32),
-            )(came)
-            back = [came[:, span + x * LANES : span + (x + 1) * LANES] for x in range(3)]
-            sent = mm(route_last, jnp.concatenate(back, axis=0))
+                (
+                    jax.ShapeDtypeStruct((tdev, share, nsq), F32),
+                    jax.ShapeDtypeStruct((slots, LANES), BF),
+                ),
+            )(came, route_last)
         sent = sent.astype(BF).reshape(ntrip, chunk, LANES)
         came = swap(sent, "trip").reshape(slots, LANES)
         total = mm_tn(serve, came)[: pdev * chunk]

time: 186 us -> 184 us (0.989)
  blocking collectives: 101 us -> 109 us
  waiting for transfers between devices: 20.4 us -> 14.7 us
  starting transfers between devices: 32.4 us -> 26.8 us
    all_to_all x7 -> x8, blocking collectives: 101 us -> 109 us  [swap(): return lax.all_to_all(x, axis, split_axis=0, concat_axis=0, tiled=True)]
    all_to_all x3 -> x2, waiting for transfers between devices: 20.4 us -> 14.7 us  [swap(): return lax.all_to_all(x, axis, split_axis=0, concat_axis=0, tiled=True)]
    all_to_all x3 -> x2, starting transfers between devices: 32.4 us -> 26.8 us  [swap(): return lax.all_to_all(x, axis, split_axis=0, concat_axis=0, tiled=True)]
  transfers between devices with their start and end apart: 4 -> 3, of which waited for: 3 -> 2; matrix products, arithmetic and copies ran while one was open for 2% -> 2% of each run, Pallas kernels for 1% -> 1%
where the time goes in v5:
time: 184 us; the launch traced here: 183 us
  blocking collectives  109 us (59%)
  starting transfers between devices  26.8 us (15%)
  waiting for transfers between devices  14.7 us (8%)
  between operations  14.4 us (8%)
  Pallas kernels  11.4 us (6%)
  local copies, waits for them, and re-layouts  3.2 us (2%)
  other arithmetic  2.13 us (1%)
    all_to_all x8, blocking collectives, swap(): return lax.all_to_all(x, axis, split_axis=0, concat_axis=0, tiled=True)  109 us
    all_to_all x2, starting transfers between devices, swap(): return lax.all_to_all(x, axis, split_axis=0, concat_axis=0, tiled=True)  26.8 us
    all_to_all x2, waiting for transfers between devices, swap(): return lax.all_to_all(x, axis, split_axis=0, concat_axis=0, tiled=True)  14.7 us
    pallas_call x1, Pallas kernels, integral_blocks(): call(functools.partial(blocks_kernel, naux, share), (jax.ShapeDtypeStruct...  4.9 us
  transfers between devices with their start and end apart: 3, of which 2 were waited for; matrix products, arithmetic and copies ran while one was open for 2% of the time, Pallas kernels for 1%

profile of v5, /device:TPU:1, one launch (start us, length us, event | category | flops | bytes accessed | tf_op | source)
XLA Modules:
  0.0 183.0 jit_solution(3645873803110923046)
XLA Ops:
  7.3 4.9 %shard_map.140 = (bf16[8,1808,128]{2,1,0:T(8,128)(2,1)}, bf16[64,4,128]{2,1,0:T(4,128)(2,1)}) custom-call(bf16[9,1600,128]{2,1,0:T(8,128)(2,1)} %bitcast.62, bf16[9,120,128]{2,1,0:T(8,128)(2,1)} %bitcast.70, s32[3,1,9]{2,1,0:T(1,128)} %bitcast.79, s32[3,9]{1,0:T(4,128)} %bitcast.80), custom_call_target="tpu_custom_call" | custom-call | tf_op jit(solution)/shard_map/pallas_call | solution.py:140
  12.2 19.2 %all-to-all-start = ((bf16[64,4,128]{2,1,0:T(4,128)(2,1)}), bf16[64,4,128]{2,1,0:T(4,128)(2,1)S(1)}, u32[]{:S(2)}, u32[]{:S(2)}) async-start(bf16[64,4,128]{2,1,0:T(4,128)(2,1)} %get-tuple-element.26), calls=%async_computation | async-start | bytes 131072 | tf_op jit(solution)/shard_map/all_to_all | solution.py:36
  31.5 0.1 copy.34
  31.6 0.8 constant_dynamic-slice_fusion.2
  32.4 0.1 copy.42
  32.5 0.1 copy.43
  32.6 0.1 broadcast_in_dim.98
  33.0 0.1 constant_dynamic-slice_fusion.4
  33.2 0.1 select_reduce_fusion.1
  33.3 0.1 select_reduce_fusion
  33.5 0.1 broadcast_and_fusion
  33.7 0.1 add_add_fusion
  33.8 0.1 fusion.10
  33.9 0.1 fusion.11.later_order_ref.order_ref
  34.0 0.1 fusion.6.order_ref.last_order_ref
  34.2 0.1 add.411
  34.3 0.1 add.404
  34.4 0.1 concatenate.3
  34.5 0.1 copy.37
  34.6 0.1 and.279
  34.8 0.2 shard_map.141.old_ref
  35.1 0.2 fusion.8.route_ref
  35.3 10.2 %all-to-all-done = bf16[64,4,128]{2,1,0:T(4,128)(2,1)S(1)} async-done(((bf16[64,4,128]{2,1,0:T(4,128)(2,1)}), bf16[64,4,128]{2,1,0:T(4,128)(2,1)S(1)}, u32[]{:S(2)}, u32[]{:S(2)}) %all-to-all-start) | async-done | bytes 65568 | tf_op jit(solution)/shard_map/all_to_all | solution.py:36
  45.5 0.1 convolution_convert_fusion.1
  45.7 18.1 %all_to_all.50 = bf16[64,4,128]{2,1,0:T(4,128)(2,1)S(1)} all-to-all(bf16[64,4,128]{2,1,0:T(4,128)(2,1)S(1)} %bitcast.72), channel_id=1, replica_groups=mesh['trip'=64,'aux'=8] {'trip'}, dimensions={0} | all-to-all | bytes 131072 | tf_op jit(solution)/shard_map/all_to_all | solution.py:36
  63.8 0.9 shard_map.142
  64.7 7.5 %all-to-all-start.2 = ((bf16[8,8,1664]{2,1,0:T(8,128)(2,1)}), bf16[8,8,1664]{2,1,0:T(8,128)(2,1)S(1)}, u32[]{:S(2)}, u32[]{:S(2)}) async-start(bf16[8,8,1664]{2,1,0:T(8,128)(2,1)} %bitcast.16), calls=%async_computation.2 | async-start | bytes 425984 | tf_op jit(solution)/shard_map/all_to_all | solution.py:36
  72.2 0.1 copy.39.col_ref
  72.3 1.0 copy-done.1
  73.4 0.5 shard_map.143
  73.8 4.4 %all-to-all-done.2 = bf16[8,8,1664]{2,1,0:T(8,128)(2,1)S(1)} async-done(((bf16[8,8,1664]{2,1,0:T(8,128)(2,1)}), bf16[8,8,1664]{2,1,0:T(8,128)(2,1)S(1)}, u32[]{:S(2)}, u32[]{:S(2)}) %all-to-all-start.2) | async-done | bytes 213024 | tf_op jit(solution)/shard_map/all_to_all | solution.py:36
  78.3 1.8 %shard_map.144 = (bf16[192,128]{1,0:T(8,128)(2,1)S(1)}, f32[40,1600]{1,0:T(8,128)S(1)}, f32[40,200]{1,0:T(8,128)S(1)}) custom-call(bf16[64,1664]{1,0:T(8,128)(2,1)S(1)} %bitcast.52, bf16[192,512]{1,0:T(8,128)(2,1)S(1)} %fusion.6.order_ref.last_order_ref, bf16[192,192]{1,0:T(8,128)(2,1)S(1)} %fusion.11.later_order_ref.order_ref, ...), custom_call_target="tpu_custom_call" | custom-call | tf_op jit(solution)/shard_map/pallas_call | solution.py:560
  80.1 8.1 %all_to_all.51 = bf16[8,24,128]{2,1,0:T(8,128)(2,1)S(1)} all-to-all(bf16[8,24,128]{2,1,0:T(8,128)(2,1)S(1)} %bitcast.61), channel_id=1, replica_groups=mesh['trip'=64,'aux'=8] {'aux'}, dimensions={0} | all-to-all | bytes 98304 | tf_op jit(solution)/shard_map/all_to_all | solution.py:36
  88.2 0.2 convolution_convert_fusion.2
  88.4 17.8 %all_to_all.52 = bf16[64,4,128]{2,1,0:T(4,128)(2,1)S(1)} all-to-all(bf16[64,4,128]{2,1,0:T(4,128)(2,1)S(1)} %bitcast.74), channel_id=1, replica_groups=mesh['trip'=64,'aux'=8] {'trip'}, dimensions={0} | all-to-all | bytes 131072 | tf_op jit(solution)/shard_map/all_to_all | solution.py:36
  106.2 0.2 fusion.16
  106.4 0.1 convolution_convert_fusion
  106.5 18.4 %all_to_all.53 = bf16[64,4,128]{2,1,0:T(4,128)(2,1)S(1)} all-to-all(bf16[64,4,128]{2,1,0:T(4,128)(2,1)S(1)} %bitcast.73), channel_id=1, replica_groups=mesh['trip'=64,'aux'=8] {'trip'}, dimensions={0} | all-to-all | bytes 131072 | tf_op jit(solution)/shard_map/all_to_all | solution.py:36
  125.0 0.2 convolution_convert_fusion.3
  125.1 10.0 %all_to_all.54 = bf16[8,24,128]{2,1,0:T(8,128)(2,1)S(1)} all-to-all(bf16[8,24,128]{2,1,0:T(8,128)(2,1)S(1)} %bitcast.76), channel_id=1, replica_groups=mesh['trip'=64,'aux'=8] {'aux'}, dimensions={0} | all-to-all | bytes 98304 | tf_op jit(solution)/shard_map/all_to_all | solution.py:36
  135.1 1.9 %shard_map.145 = bf16[64,1664]{1,0:T(8,128)(2,1)S(1)} custom-call(bf16[192,128]{1,0:T(8,128)(2,1)S(1)} %bitcast.59, bf16[192,192]{1,0:T(8,128)(2,1)S(1)} %fusion.11.later_order_ref.order_ref, bf16[192,512]{1,0:T(8,128)(2,1)S(1)} %fusion.6.order_ref.last_order_ref, bf16[2,120,64]{2,1,0:T(8,128)(2,1)S(1)} %bitcast.56, bf16[2,192,40]{2,1,0:T(8,128)(2,1)S(1)} %bitcast.51, ...), custom_call_target="tpu_custom_call" | custom-call | tf_op jit(solution)/shard_map/pallas_call | solution.py:581
  137.0 9.2 %all_to_all.55 = bf16[8,8,1664]{2,1,0:T(8,128)(2,1)S(1)} all-to-all(bf16[8,8,1664]{2,1,0:T(8,128)(2,1)S(1)} %bitcast.53), channel_id=1, replica_groups=mesh['trip'=64,'aux'=8] {'aux'}, dimensions={0} | all-to-all | bytes 425984 | tf_op jit(solution)/shard_map/all_to_all | solution.py:36
  146.2 1.1 shard_map.146
  147.3 17.9 %all_to_all.56 = bf16[64,4,128]{2,1,0:T(4,128)(2,1)S(1)} all-to-all(bf16[64,4,128]{2,1,0:T(4,128)(2,1)S(1)} %bitcast.60), channel_id=1, replica_groups=mesh['trip'=64,'aux'=8] {'trip'}, dimensions={0} | all-to-all | bytes 131072 | tf_op jit(solution)/shard_map/all_to_all | solution.py:36
  165.1 0.2 fusion.3
  165.4 10.0 %all_to_all.57 = bf16[8,64,128]{2,1,0:T(8,128)(2,1)S(1)} all-to-all(bf16[8,64,128]{2,1,0:T(8,128)(2,1)S(1)} %broadcast_in_dim.114), channel_id=1, replica_groups=mesh['trip'=64,'aux'=8] {'aux'}, dimensions={0} | all-to-all | bytes 262144 | tf_op jit(solution)/shard_map/all_to_all | solution.py:36
  175.3 0.1 reshape.362
  175.4 0.7 convert_add_fusion
  (50 shorter events, 1.0 us)
Async XLA Ops:
  7.2 65.2 %reduce-scatter.2.cloned.1.call-start = ((), (), s32[]{:S(2)}) async-start(), calls=%async_computation.11 | async-start | bytes 4165632 | tf_op jit(solution)/shard_map/reduce_scatter | solution.py:467
  7.2 24.3 %copy-start.5 = (s32[9,3,1]{0,2,1:T(1,128)S(1)}, s32[9,3,1]{0,2,1:T(1,128)}, u32[]{:S(2)}) copy-start(s32[9,3,1]{0,2,1:T(1,128)} %param.24) | copy-start | bytes 328
  7.2 25.4 %copy-start.6 = (f32[9,3]{0,1:T(4,128)S(1)}, f32[9,3]{0,1:T(4,128)}, u32[]{:S(2)}) copy-start(f32[9,3]{0,1:T(4,128)} %param.17) | copy-start | bytes 328
  7.2 25.5 %copy-start.4 = (f32[9,40]{1,0:T(8,128)S(1)}, f32[9,40]{1,0:T(8,128)}, u32[]{:S(2)}) copy-start(f32[9,40]{1,0:T(8,128)} %param.16) | copy-start | bytes 4324
  7.2 25.5 %copy-start.8 = (s32[9]{0:T(128)S(1)}, s32[9]{0:T(128)}, u32[]{:S(2)}) copy-start(s32[9]{0:T(128)} %param.18) | copy-start | bytes 112
  7.3 25.7 %copy-start.9 = (s32[16]{0:T(128)S(1)}, s32[16]{0:T(128)}, u32[]{:S(2)}) copy-start(s32[16]{0:T(128)} %param.23) | copy-start | bytes 196
  7.3 25.8 %copy-start.3 = (f32[16,64]{1,0:T(8,128)S(1)}, f32[16,64]{1,0:T(8,128)}, u32[]{:S(2)}) copy-start(f32[16,64]{1,0:T(8,128)} %param.21) | copy-start | bytes 12292
  7.3 25.9 %copy-start.2 = (bf16[16,4096]{1,0:T(8,128)(2,1)S(1)}, bf16[16,4096]{1,0:T(8,128)(2,1)}, u32[]{:S(2)}) copy-start(bf16[16,4096]{1,0:T(8,128)(2,1)} %param.20) | copy-start | bytes 393220
  7.3 26.4 %copy-start.7 = (f32[16]{0:T(128)S(1)}, f32[16]{0:T(128)}, u32[]{:S(2)}) copy-start(f32[16]{0:T(128)} %param.22) | copy-start | bytes 196
  12.2 22.6 %copy-start = (f32[9,5,1600]{2,1,0:T(8,128)S(1)}, f32[9,5,1600]{2,1,0:T(8,128)}, u32[]{:S(2)}) copy-start(f32[9,5,1600]{2,1,0:T(8,128)} %old_ref.1) | copy-start | bytes 864004
  12.2 33.3 %all-to-all-start = ((bf16[64,4,128]{2,1,0:T(4,128)(2,1)}), bf16[64,4,128]{2,1,0:T(4,128)(2,1)S(1)}, u32[]{:S(2)}, u32[]{:S(2)}) async-start(bf16[64,4,128]{2,1,0:T(4,128)(2,1)} %get-tuple-element.26), calls=%async_computation | async-start | bytes 131072 | tf_op jit(solution)/shard_map/all_to_all | solution.py:36
  64.7 13.6 %all-to-all-start.2 = ((bf16[8,8,1664]{2,1,0:T(8,128)(2,1)}), bf16[8,8,1664]{2,1,0:T(8,128)(2,1)S(1)}, u32[]{:S(2)}, u32[]{:S(2)}) async-start(bf16[8,8,1664]{2,1,0:T(8,128)(2,1)} %bitcast.16), calls=%async_computation.2 | async-start | bytes 425984 | tf_op jit(solution)/shard_map/all_to_all | solution.py:36
  72.3 1.0 copy-start.1
Sparse Core Ops, SparseCore 0:
  12.4 48.2 reduce-scatter.1

commit v6 on v5

--- a/solution.py
+++ b/solution.py
@@ -106,7 +106,7 @@
         arriving[n].wait()
         if end > naux:
             right = jnp.concatenate([occ_ref[naux], none], axis=0)
-            last_ref[...] = mm_nt(held_ref[naux], right)
+            last_ref[:nsq, :] = mm_nt(held_ref[naux], right)
         top = min(end, naux)
         for t in range(low, top, 2):
             left = jnp.concatenate([held_ref[t], held_ref[t + 1]], axis=1)
@@ -146,7 +146,7 @@
         [
             pltpu.VMEM((tdev, nsq, depth), BF),
             pltpu.VMEM((naux, rows, LANES), BF),
-            pltpu.VMEM((nsq, LANES), F32),
+            pltpu.VMEM((nsq + ntno, LANES), F32),
             pltpu.VMEM((tdev, occ_blocks.shape[2], depth), BF),
             pltpu.SMEM((3, 1, tdev), jnp.int32),
             pltpu.SMEM((3, tdev), jnp.int32),

time: 184 us -> 184 us (level)
  no operation moved by 1% of the time
where the time goes in v6:
time: 184 us; the launch traced here: 183 us
  blocking collectives  109 us (59%)
  starting transfers between devices  26.8 us (15%)
  waiting for transfers between devices  14.7 us (8%)
  between operations  14.4 us (8%)
  Pallas kernels  11.3 us (6%)
  local copies, waits for them, and re-layouts  3.2 us (2%)
  other arithmetic  2.13 us (1%)
    all_to_all x8, blocking collectives, swap(): return lax.all_to_all(x, axis, split_axis=0, concat_axis=0, tiled=True)  109 us
    all_to_all x2, starting transfers between devices, swap(): return lax.all_to_all(x, axis, split_axis=0, concat_axis=0, tiled=True)  26.8 us
    all_to_all x2, waiting for transfers between devices, swap(): return lax.all_to_all(x, axis, split_axis=0, concat_axis=0, tiled=True)  14.7 us
    pallas_call x1, Pallas kernels, integral_blocks(): call(functools.partial(blocks_kernel, naux, share), (jax.ShapeDtypeStruct...  4.9 us
  transfers between devices with their start and end apart: 3, of which 2 were waited for; matrix products, arithmetic and copies ran while one was open for 2% of the time, Pallas kernels for 1%

profile of v6, /device:TPU:1, one launch (start us, length us, event | category | flops | bytes accessed | tf_op | source)
XLA Modules:
  0.0 183.0 jit_solution(11809647842146698490)
XLA Ops:
  7.3 4.9 %shard_map.140 = (bf16[8,1808,128]{2,1,0:T(8,128)(2,1)}, bf16[64,4,128]{2,1,0:T(4,128)(2,1)}) custom-call(bf16[9,1600,128]{2,1,0:T(8,128)(2,1)} %bitcast.62, bf16[9,120,128]{2,1,0:T(8,128)(2,1)} %bitcast.70, s32[3,1,9]{2,1,0:T(1,128)} %bitcast.79, s32[3,9]{1,0:T(4,128)} %bitcast.80), custom_call_target="tpu_custom_call" | custom-call | tf_op jit(solution)/shard_map/pallas_call | solution.py:140
  12.2 19.3 %all-to-all-start = ((bf16[64,4,128]{2,1,0:T(4,128)(2,1)}), bf16[64,4,128]{2,1,0:T(4,128)(2,1)S(1)}, u32[]{:S(2)}, u32[]{:S(2)}) async-start(bf16[64,4,128]{2,1,0:T(4,128)(2,1)} %get-tuple-element.26), calls=%async_computation | async-start | bytes 131072 | tf_op jit(solution)/shard_map/all_to_all | solution.py:36
  31.5 0.1 copy.34
  31.6 0.8 constant_dynamic-slice_fusion.2
  32.4 0.1 copy.42
  32.5 0.1 copy.43
  32.6 0.1 broadcast_in_dim.98
  33.0 0.1 constant_dynamic-slice_fusion.4
  33.2 0.1 select_reduce_fusion.1
  33.3 0.1 select_reduce_fusion
  33.5 0.1 broadcast_and_fusion
  33.7 0.1 add_add_fusion
  33.8 0.1 fusion.10
  33.9 0.1 fusion.11.later_order_ref.order_ref
  34.0 0.1 fusion.6.order_ref.last_order_ref
  34.2 0.1 add.411
  34.3 0.1 add.404
  34.4 0.1 concatenate.3
  34.5 0.1 copy.37
  34.6 0.1 and.279
  34.8 0.2 shard_map.141.old_ref
  35.1 0.2 fusion.8.route_ref
  35.3 10.2 %all-to-all-done = bf16[64,4,128]{2,1,0:T(4,128)(2,1)S(1)} async-done(((bf16[64,4,128]{2,1,0:T(4,128)(2,1)}), bf16[64,4,128]{2,1,0:T(4,128)(2,1)S(1)}, u32[]{:S(2)}, u32[]{:S(2)}) %all-to-all-start) | async-done | bytes 65568 | tf_op jit(solution)/shard_map/all_to_all | solution.py:36
  45.5 0.1 convolution_convert_fusion.1
  45.7 18.1 %all_to_all.50 = bf16[64,4,128]{2,1,0:T(4,128)(2,1)S(1)} all-to-all(bf16[64,4,128]{2,1,0:T(4,128)(2,1)S(1)} %bitcast.72), channel_id=1, replica_groups=mesh['trip'=64,'aux'=8] {'trip'}, dimensions={0} | all-to-all | bytes 131072 | tf_op jit(solution)/shard_map/all_to_all | solution.py:36
  63.8 0.9 shard_map.142
  64.7 7.5 %all-to-all-start.2 = ((bf16[8,8,1664]{2,1,0:T(8,128)(2,1)}), bf16[8,8,1664]{2,1,0:T(8,128)(2,1)S(1)}, u32[]{:S(2)}, u32[]{:S(2)}) async-start(bf16[8,8,1664]{2,1,0:T(8,128)(2,1)} %bitcast.16), calls=%async_computation.2 | async-start | bytes 425984 | tf_op jit(solution)/shard_map/all_to_all | solution.py:36
  72.2 0.1 copy.39.col_ref
  72.3 1.0 copy-done.1
  73.4 0.5 shard_map.143
  73.8 4.4 %all-to-all-done.2 = bf16[8,8,1664]{2,1,0:T(8,128)(2,1)S(1)} async-done(((bf16[8,8,1664]{2,1,0:T(8,128)(2,1)}), bf16[8,8,1664]{2,1,0:T(8,128)(2,1)S(1)}, u32[]{:S(2)}, u32[]{:S(2)}) %all-to-all-start.2) | async-done | bytes 213024 | tf_op jit(solution)/shard_map/all_to_all | solution.py:36
  78.3 1.8 %shard_map.144 = (bf16[192,128]{1,0:T(8,128)(2,1)S(1)}, f32[40,1600]{1,0:T(8,128)S(1)}, f32[40,200]{1,0:T(8,128)S(1)}) custom-call(bf16[64,1664]{1,0:T(8,128)(2,1)S(1)} %bitcast.52, bf16[192,512]{1,0:T(8,128)(2,1)S(1)} %fusion.6.order_ref.last_order_ref, bf16[192,192]{1,0:T(8,128)(2,1)S(1)} %fusion.11.later_order_ref.order_ref, ...), custom_call_target="tpu_custom_call" | custom-call | tf_op jit(solution)/shard_map/pallas_call | solution.py:560
  80.1 8.1 %all_to_all.51 = bf16[8,24,128]{2,1,0:T(8,128)(2,1)S(1)} all-to-all(bf16[8,24,128]{2,1,0:T(8,128)(2,1)S(1)} %bitcast.61), channel_id=1, replica_groups=mesh['trip'=64,'aux'=8] {'aux'}, dimensions={0} | all-to-all | bytes 98304 | tf_op jit(solution)/shard_map/all_to_all | solution.py:36
  88.2 0.2 convolution_convert_fusion.2
  88.4 17.8 %all_to_all.52 = bf16[64,4,128]{2,1,0:T(4,128)(2,1)S(1)} all-to-all(bf16[64,4,128]{2,1,0:T(4,128)(2,1)S(1)} %bitcast.74), channel_id=1, replica_groups=mesh['trip'=64,'aux'=8] {'trip'}, dimensions={0} | all-to-all | bytes 131072 | tf_op jit(solution)/shard_map/all_to_all | solution.py:36
  106.2 0.2 fusion.16
  106.4 0.1 convolution_convert_fusion
  106.5 18.4 %all_to_all.53 = bf16[64,4,128]{2,1,0:T(4,128)(2,1)S(1)} all-to-all(bf16[64,4,128]{2,1,0:T(4,128)(2,1)S(1)} %bitcast.73), channel_id=1, replica_groups=mesh['trip'=64,'aux'=8] {'trip'}, dimensions={0} | all-to-all | bytes 131072 | tf_op jit(solution)/shard_map/all_to_all | solution.py:36
  125.0 0.2 convolution_convert_fusion.3
  125.1 10.0 %all_to_all.54 = bf16[8,24,128]{2,1,0:T(8,128)(2,1)S(1)} all-to-all(bf16[8,24,128]{2,1,0:T(8,128)(2,1)S(1)} %bitcast.76), channel_id=1, replica_groups=mesh['trip'=64,'aux'=8] {'aux'}, dimensions={0} | all-to-all | bytes 98304 | tf_op jit(solution)/shard_map/all_to_all | solution.py:36
  135.1 1.9 %shard_map.145 = bf16[64,1664]{1,0:T(8,128)(2,1)S(1)} custom-call(bf16[192,128]{1,0:T(8,128)(2,1)S(1)} %bitcast.59, bf16[192,192]{1,0:T(8,128)(2,1)S(1)} %fusion.11.later_order_ref.order_ref, bf16[192,512]{1,0:T(8,128)(2,1)S(1)} %fusion.6.order_ref.last_order_ref, bf16[2,120,64]{2,1,0:T(8,128)(2,1)S(1)} %bitcast.56, bf16[2,192,40]{2,1,0:T(8,128)(2,1)S(1)} %bitcast.51, ...), custom_call_target="tpu_custom_call" | custom-call | tf_op jit(solution)/shard_map/pallas_call | solution.py:581
  137.0 9.2 %all_to_all.55 = bf16[8,8,1664]{2,1,0:T(8,128)(2,1)S(1)} all-to-all(bf16[8,8,1664]{2,1,0:T(8,128)(2,1)S(1)} %bitcast.53), channel_id=1, replica_groups=mesh['trip'=64,'aux'=8] {'aux'}, dimensions={0} | all-to-all | bytes 425984 | tf_op jit(solution)/shard_map/all_to_all | solution.py:36
  146.2 1.1 shard_map.146
  147.3 17.9 %all_to_all.56 = bf16[64,4,128]{2,1,0:T(4,128)(2,1)S(1)} all-to-all(bf16[64,4,128]{2,1,0:T(4,128)(2,1)S(1)} %bitcast.60), channel_id=1, replica_groups=mesh['trip'=64,'aux'=8] {'trip'}, dimensions={0} | all-to-all | bytes 131072 | tf_op jit(solution)/shard_map/all_to_all | solution.py:36
  165.1 0.2 fusion.3
  165.4 10.0 %all_to_all.57 = bf16[8,64,128]{2,1,0:T(8,128)(2,1)S(1)} all-to-all(bf16[8,64,128]{2,1,0:T(8,128)(2,1)S(1)} %broadcast_in_dim.114), channel_id=1, replica_groups=mesh['trip'=64,'aux'=8] {'aux'}, dimensions={0} | all-to-all | bytes 262144 | tf_op jit(solution)/shard_map/all_to_all | solution.py:36
  175.3 0.1 reshape.362
  175.4 0.7 convert_add_fusion
  (50 shorter events, 1.0 us)
Async XLA Ops:
  7.2 65.2 %reduce-scatter.2.cloned.1.call-start = ((), (), s32[]{:S(2)}) async-start(), calls=%async_computation.11 | async-start | bytes 4165632 | tf_op jit(solution)/shard_map/reduce_scatter | solution.py:467
  7.2 24.3 %copy-start.5 = (s32[9,3,1]{0,2,1:T(1,128)S(1)}, s32[9,3,1]{0,2,1:T(1,128)}, u32[]{:S(2)}) copy-start(s32[9,3,1]{0,2,1:T(1,128)} %param.24) | copy-start | bytes 328
  7.2 25.4 %copy-start.6 = (f32[9,3]{0,1:T(4,128)S(1)}, f32[9,3]{0,1:T(4,128)}, u32[]{:S(2)}) copy-start(f32[9,3]{0,1:T(4,128)} %param.17) | copy-start | bytes 328
  7.2 25.5 %copy-start.4 = (f32[9,40]{1,0:T(8,128)S(1)}, f32[9,40]{1,0:T(8,128)}, u32[]{:S(2)}) copy-start(f32[9,40]{1,0:T(8,128)} %param.16) | copy-start | bytes 4324
  7.2 25.5 %copy-start.8 = (s32[9]{0:T(128)S(1)}, s32[9]{0:T(128)}, u32[]{:S(2)}) copy-start(s32[9]{0:T(128)} %param.18) | copy-start | bytes 112
  7.3 25.7 %copy-start.9 = (s32[16]{0:T(128)S(1)}, s32[16]{0:T(128)}, u32[]{:S(2)}) copy-start(s32[16]{0:T(128)} %param.23) | copy-start | bytes 196
  7.3 25.8 %copy-start.3 = (f32[16,64]{1,0:T(8,128)S(1)}, f32[16,64]{1,0:T(8,128)}, u32[]{:S(2)}) copy-start(f32[16,64]{1,0:T(8,128)} %param.21) | copy-start | bytes 12292
  7.3 25.9 %copy-start.2 = (bf16[16,4096]{1,0:T(8,128)(2,1)S(1)}, bf16[16,4096]{1,0:T(8,128)(2,1)}, u32[]{:S(2)}) copy-start(bf16[16,4096]{1,0:T(8,128)(2,1)} %param.20) | copy-start | bytes 393220
  7.3 26.4 %copy-start.7 = (f32[16]{0:T(128)S(1)}, f32[16]{0:T(128)}, u32[]{:S(2)}) copy-start(f32[16]{0:T(128)} %param.22) | copy-start | bytes 196
  12.2 22.6 %copy-start = (f32[9,5,1600]{2,1,0:T(8,128)S(1)}, f32[9,5,1600]{2,1,0:T(8,128)}, u32[]{:S(2)}) copy-start(f32[9,5,1600]{2,1,0:T(8,128)} %old_ref.1) | copy-start | bytes 864004
  12.2 33.3 %all-to-all-start = ((bf16[64,4,128]{2,1,0:T(4,128)(2,1)}), bf16[64,4,128]{2,1,0:T(4,128)(2,1)S(1)}, u32[]{:S(2)}, u32[]{:S(2)}) async-start(bf16[64,4,128]{2,1,0:T(4,128)(2,1)} %get-tuple-element.26), calls=%async_computation | async-start | bytes 131072 | tf_op jit(solution)/shard_map/all_to_all | solution.py:36
  64.7 13.6 %all-to-all-start.2 = ((bf16[8,8,1664]{2,1,0:T(8,128)(2,1)}), bf16[8,8,1664]{2,1,0:T(8,128)(2,1)S(1)}, u32[]{:S(2)}, u32[]{:S(2)}) async-start(bf16[8,8,1664]{2,1,0:T(8,128)(2,1)} %bitcast.16), calls=%async_computation.2 | async-start | bytes 425984 | tf_op jit(solution)/shard_map/all_to_all | solution.py:36
  72.3 1.0 copy-start.1
Sparse Core Ops, SparseCore 0:
  12.4 48.2 reduce-scatter.1

commit v7 on v6

--- a/solution.py
+++ b/solution.py
@@ -377,7 +377,6 @@
     chunk,
     came_ref,
     order_ref,
-    last_order_ref,
     cover_ref,
     piece_ref,
     col_ref,
@@ -386,12 +385,11 @@
     last_ref,
     own_mat_ref,
     last_mat_ref,
-    out_ref,
-    wide_ref,
-    edge_ref,
+    sent_ref,
+    new_ref,
 ):
-    ntno, nsq = own_ref.shape
-    slab = last_ref.shape[1]
+    nsq, slab = own_ref.shape[1], last_ref.shape[1]
+    start = up(nsq, LANES)
     projs = project_both(naux, chunk, order_ref[...], came_ref[...], cover_ref, piece_ref)
     _, halves, sent = work_both(
         naux,
@@ -404,27 +402,21 @@
         (own_ref[...], last_ref[...]),
         (own_mat_ref[...], last_mat_ref[...]),
     )
-    wide_ref[...] = jnp.zeros(wide_ref.shape, BF)
-    wide_ref[:, :nsq] = halves[0]
-    edge_ref[...] = jnp.zeros(edge_ref.shape, BF)
-    edge_ref[:, :slab] = halves[1]
-    own = mm_tn(row_spots(ntno, naux, out_ref.shape[0]), wide_ref[...])
-    pieces = mm_tn(last_order_ref[...], sent)
-    spread(ntno, naux, own, edge_ref[...], pieces, out_ref)
-
-
-def finish_kernel(naux, came_ref, route_ref, out_ref, sent_ref):
-    share, nsq = out_ref.shape[1:]
-    ntno, slab = share * naux, nsq // naux
-    part = came_ref.shape[0] // naux
-    came = came_ref[...]
-    sent_ref[...] = mm(route_ref[...], gather_pieces(came)).astype(BF)
-    edge = gather_last(ntno, naux, came)
-    came = came.astype(F32)
+    new_ref[...] = jnp.zeros(new_ref.shape, BF)
+    new_ref[:, :nsq] = halves[0]
+    new_ref[:, start : start + slab] = halves[1]
+    sent_ref[...] = mm_tn(order_ref[...], sent).astype(BF)
+
+
+def finish_kernel(came_ref, out_ref):
+    nsq = out_ref.shape[2]
+    naux = came_ref.shape[0]
+    start, slab = up(nsq, LANES), nsq // naux
     last = []
     for member in range(naux):
-        out_ref[member] = came[member * part : member * part + share, :nsq]
-        last.append(edge[member * share : (member + 1) * share, :slab])
+        rows = came_ref[member].astype(F32)
+        out_ref[member] = rows[:, :nsq]
+        last.append(rows[:, start : start + slab])
     out_ref[naux] = jnp.concatenate(last, axis=1)
 
 
@@ -489,7 +481,7 @@
     packed_old = call(
         functools.partial(old_kernel, naux), jax.ShapeDtypeStruct((size, width), BF)
     )(triples_old)
-    route_back, route_last = route.T, route_first.T
+    route_back = route.T
     order = fetch_order(naux, chunk)
     order_first = fetch_order(naux, chunk, (share, part, tiles))
 
@@ -528,10 +520,10 @@
     split = split.reshape(2, 3 * npno, ntno)
 
     ready = (
-        (serve, route, route_first, route_back, route_last, order, order_first)
+        (serve, route, route_first, route_back, order, order_first)
         + (pair_keep, pair_den, amps, flat, split, col, row, packed_old)
     )
-    serve, route, route_first, route_back, route_last, order, order_first, *ready = (
+    serve, route, route_first, route_back, order, order_first, *ready = (
         lax.optimization_barrier(ready)
     )
     pair_keep, pair_den, amps, flat, split, col, row, packed_old = ready
@@ -578,14 +570,15 @@
             came = swap(sent.reshape(naux, 6 * chunk, LANES), "aux")
             sent = mm(route_back, came.reshape(naux * 6 * chunk, LANES))
         else:
-            sent = call(
+            sent, new = call(
                 functools.partial(later_kernel, naux, chunk),
-                jax.ShapeDtypeStruct((size, width), BF),
-                [pltpu.VMEM((ntno, width), BF), pltpu.VMEM((ntno, 2 * LANES), BF)],
+                (
+                    jax.ShapeDtypeStruct((naux * 6 * chunk, LANES), BF),
+                    jax.ShapeDtypeStruct((ntno, span), BF),
+                ),
             )(
                 came.reshape(-1, LANES),
                 order,
-                order_first,
                 flat,
                 split,
                 col,
@@ -595,14 +588,11 @@
                 own_mat,
                 last_mat,
             )
-            came = swap(sent.reshape(naux, part, width), "aux").reshape(size, width)
-            triples_new, sent = call(
-                functools.partial(finish_kernel, naux),
-                (
-                    jax.ShapeDtypeStruct((tdev, share, nsq), F32),
-                    jax.ShapeDtypeStruct((slots, LANES), BF),
-                ),
-            )(came, route_last)
+            new = lax.all_gather(new, "aux", axis=0, tiled=False)
+            new = lax.dynamic_slice_in_dim(new, member * share, share, 1)
+            triples_new = call(finish_kernel, jax.ShapeDtypeStruct((tdev, share, nsq), F32))(new)
+            came = swap(sent.reshape(naux, 6 * chunk, LANES), "aux")
+            sent = mm(route_back, came.reshape(naux * 6 * chunk, LANES))
         sent = sent.astype(BF).reshape(ntrip, chunk, LANES)
         came = swap(sent, "trip").reshape(slots, LANES)
         total = mm_tn(serve, came)[: pdev * chunk]
@@ -611,7 +601,8 @@
         amps = amps + change
 
     gains = jnp.broadcast_to(gain.astype(BF)[None], (naux, pdev * chunk, LANES))
-    gains = swap(gains, "aux").reshape(naux, pdev, prow * npno).transpose(1, 0, 2)
+    gains, triples_new = lax.optimization_barrier((swap(gains, "aux"), triples_new))
+    gains = gains.reshape(naux, pdev, prow * npno).transpose(1, 0, 2)
     pairs_new = pair_amps.astype(F32) + gains.reshape(pdev, npno * npno).astype(F32)
     return triples_new, pairs_new
 

time: 184 us -> 183 us (level)
  blocking collectives: 109 us -> 98.1 us
  starting transfers between devices: 26.8 us -> 32.5 us
  waiting for transfers between devices: 14.7 us -> 18.1 us
    all_to_all x8 -> x7, blocking collectives: 109 us -> 98.1 us  [swap(): return lax.all_to_all(x, axis, split_axis=0, concat_axis=0, tiled=True)]
    all_to_all x2 -> x3, starting transfers between devices: 26.8 us -> 32.4 us  [swap(): return lax.all_to_all(x, axis, split_axis=0, concat_axis=0, tiled=True)]
    all_to_all x2 -> x3, waiting for transfers between devices: 14.7 us -> 18.1 us  [swap(): return lax.all_to_all(x, axis, split_axis=0, concat_axis=0, tiled=True)]
  transfers between devices with their start and end apart: 3 -> 5, of which waited for: 2 -> 3; matrix products, arithmetic and copies ran while one was open for 2% -> 3% of each run, Pallas kernels for 1% -> 1%
where the time goes in v7:
time: 183 us
  blocking collectives  98.1 us (54%)
  starting transfers between devices  32.5 us (18%)
  waiting for transfers between devices  18.1 us (10%)
  between operations  14.4 us (8%)
  Pallas kernels  11.3 us (6%)
  local copies, waits for them, and re-layouts  4.95 us (3%)
  other arithmetic  2.05 us (1%)
    all_to_all x7, blocking collectives, swap(): return lax.all_to_all(x, axis, split_axis=0, concat_axis=0, tiled=True)  98.1 us
    all_to_all x3, starting transfers between devices, swap(): return lax.all_to_all(x, axis, split_axis=0, concat_axis=0, tiled=True)  32.4 us
    all_to_all x3, waiting for transfers between devices, swap(): return lax.all_to_all(x, axis, split_axis=0, concat_axis=0, tiled=True)  18.1 us
    pallas_call x1, Pallas kernels, integral_blocks(): call(functools.partial(blocks_kernel, naux, share), (jax.ShapeDtypeStruct...  4.89 us
  transfers between devices with their start and end apart: 5, of which 3 were waited for; matrix products, arithmetic and copies ran while one was open for 3% of the time, Pallas kernels for 1%

profile of v7, /device:TPU:1, one launch (start us, length us, event | category | flops | bytes accessed | tf_op | source)
XLA Modules:
  0.0 182.5 jit_solution(12173719975841410046)
XLA Ops:
  7.3 4.9 %shard_map.140 = (bf16[8,1808,128]{2,1,0:T(8,128)(2,1)}, bf16[64,4,128]{2,1,0:T(4,128)(2,1)}) custom-call(bf16[9,1600,128]{2,1,0:T(8,128)(2,1)} %bitcast.63, bf16[9,120,128]{2,1,0:T(8,128)(2,1)} %bitcast.71, s32[3,1,9]{2,1,0:T(1,128)} %bitcast.83, s32[3,9]{1,0:T(4,128)} %bitcast.84), custom_call_target="tpu_custom_call" | custom-call | tf_op jit(solution)/shard_map/pallas_call | solution.py:140
  12.2 19.3 %all-to-all-start = ((bf16[64,4,128]{2,1,0:T(4,128)(2,1)}), bf16[64,4,128]{2,1,0:T(4,128)(2,1)S(1)}, u32[]{:S(2)}, u32[]{:S(2)}) async-start(bf16[64,4,128]{2,1,0:T(4,128)(2,1)} %get-tuple-element.27), calls=%async_computation | async-start | bytes 131072 | tf_op jit(solution)/shard_map/all_to_all | solution.py:36
  31.5 0.1 copy.34
  31.6 0.8 constant_dynamic-slice_fusion.2
  32.4 0.1 copy.42
  32.5 0.1 copy.43
  32.6 0.1 broadcast_in_dim.94
  33.2 0.1 select_reduce_fusion.1
  33.3 0.1 select_reduce_fusion
  33.5 0.1 broadcast_and_fusion
  33.7 0.1 add_add_fusion
  33.8 0.1 fusion.8
  33.9 0.1 fusion.9.later_order_ref.order_ref
  34.0 0.1 fusion.5.order_ref
  34.2 0.1 add.403
  34.4 0.1 copy.37
  34.6 0.1 and.277
  34.7 0.2 shard_map.141.old_ref
  35.0 0.2 fusion.6.route_ref
  35.2 10.3 %all-to-all-done = bf16[64,4,128]{2,1,0:T(4,128)(2,1)S(1)} async-done(((bf16[64,4,128]{2,1,0:T(4,128)(2,1)}), bf16[64,4,128]{2,1,0:T(4,128)(2,1)S(1)}, u32[]{:S(2)}, u32[]{:S(2)}) %all-to-all-start) | async-done | bytes 65568 | tf_op jit(solution)/shard_map/all_to_all | solution.py:36
  45.5 0.1 convolution_convert_fusion.1
  45.6 18.0 %all_to_all.50 = bf16[64,4,128]{2,1,0:T(4,128)(2,1)S(1)} all-to-all(bf16[64,4,128]{2,1,0:T(4,128)(2,1)S(1)} %bitcast.73), channel_id=1, replica_groups=mesh['trip'=64,'aux'=8] {'trip'}, dimensions={0} | all-to-all | bytes 131072 | tf_op jit(solution)/shard_map/all_to_all | solution.py:36
  63.7 0.9 shard_map.142
  64.6 7.7 %all-to-all-start.2 = ((bf16[8,8,1664]{2,1,0:T(8,128)(2,1)}), bf16[8,8,1664]{2,1,0:T(8,128)(2,1)S(1)}, u32[]{:S(2)}, u32[]{:S(2)}) async-start(bf16[8,8,1664]{2,1,0:T(8,128)(2,1)} %bitcast.16), calls=%async_computation.2 | async-start | bytes 425984 | tf_op jit(solution)/shard_map/all_to_all | solution.py:36
  72.2 0.1 copy.39.col_ref
  72.4 1.0 copy-done.1
  73.4 0.5 shard_map.143
  73.9 4.4 %all-to-all-done.2 = bf16[8,8,1664]{2,1,0:T(8,128)(2,1)S(1)} async-done(((bf16[8,8,1664]{2,1,0:T(8,128)(2,1)}), bf16[8,8,1664]{2,1,0:T(8,128)(2,1)S(1)}, u32[]{:S(2)}, u32[]{:S(2)}) %all-to-all-start.2) | async-done | bytes 213024 | tf_op jit(solution)/shard_map/all_to_all | solution.py:36
  78.3 1.8 %shard_map.144 = (bf16[192,128]{1,0:T(8,128)(2,1)S(1)}, f32[40,1600]{1,0:T(8,128)S(1)}, f32[40,200]{1,0:T(8,128)S(1)}) custom-call(bf16[64,1664]{1,0:T(8,128)(2,1)S(1)} %bitcast.55, bf16[192,512]{1,0:T(8,128)(2,1)S(1)} %fusion.5.order_ref, bf16[192,192]{1,0:T(8,128)(2,1)S(1)} %fusion.9.later_order_ref.order_ref, bf16[2,120,64]{2,1,0:T(8,128)(2,1)S(1)} %bitcast.56, ...), custom_call_target="tpu_custom_call" | custom-call | tf_op jit(solution)/shard_map/pallas_call | solution.py:552
  80.1 8.1 %all_to_all.51 = bf16[8,24,128]{2,1,0:T(8,128)(2,1)S(1)} all-to-all(bf16[8,24,128]{2,1,0:T(8,128)(2,1)S(1)} %bitcast.62), channel_id=1, replica_groups=mesh['trip'=64,'aux'=8] {'aux'}, dimensions={0} | all-to-all | bytes 98304 | tf_op jit(solution)/shard_map/all_to_all | solution.py:36
  88.2 0.2 convolution_convert_fusion.3
  88.4 17.8 %all_to_all.52 = bf16[64,4,128]{2,1,0:T(4,128)(2,1)S(1)} all-to-all(bf16[64,4,128]{2,1,0:T(4,128)(2,1)S(1)} %bitcast.76), channel_id=1, replica_groups=mesh['trip'=64,'aux'=8] {'trip'}, dimensions={0} | all-to-all | bytes 131072 | tf_op jit(solution)/shard_map/all_to_all | solution.py:36
  106.2 0.2 fusion.14
  106.4 0.1 convolution_convert_fusion
  106.6 18.4 %all_to_all.53 = bf16[64,4,128]{2,1,0:T(4,128)(2,1)S(1)} all-to-all(bf16[64,4,128]{2,1,0:T(4,128)(2,1)S(1)} %bitcast.74), channel_id=1, replica_groups=mesh['trip'=64,'aux'=8] {'trip'}, dimensions={0} | all-to-all | bytes 131072 | tf_op jit(solution)/shard_map/all_to_all | solution.py:36
  125.0 0.2 convolution_convert_fusion.4
  125.2 10.0 %all_to_all.54 = bf16[8,24,128]{2,1,0:T(8,128)(2,1)S(1)} all-to-all(bf16[8,24,128]{2,1,0:T(8,128)(2,1)S(1)} %bitcast.77), channel_id=1, replica_groups=mesh['trip'=64,'aux'=8] {'aux'}, dimensions={0} | all-to-all | bytes 98304 | tf_op jit(solution)/shard_map/all_to_all | solution.py:36
  135.1 2.1 %shard_map.145 = (bf16[192,128]{1,0:T(8,128)(2,1)S(1)}, bf16[40,1920]{1,0:T(8,128)(2,1)}) custom-call(bf16[192,128]{1,0:T(8,128)(2,1)S(1)} %bitcast.60, bf16[192,192]{1,0:T(8,128)(2,1)S(1)} %fusion.9.later_order_ref.order_ref, bf16[2,120,64]{2,1,0:T(8,128)(2,1)S(1)} %bitcast.57, bf16[2,192,40]{2,1,0:T(8,128)(2,1)S(1)} %bitcast.54, ...), custom_call_target="tpu_custom_call" | custom-call | tf_op jit(solution)/shard_map/pallas_call | solution.py:573
  137.3 7.9 %all_to_all.55 = bf16[8,24,128]{2,1,0:T(8,128)(2,1)S(1)} all-to-all(bf16[8,24,128]{2,1,0:T(8,128)(2,1)S(1)} %bitcast.61), channel_id=1, replica_groups=mesh['trip'=64,'aux'=8] {'aux'}, dimensions={0} | all-to-all | bytes 98304 | tf_op jit(solution)/shard_map/all_to_all | solution.py:36
  145.2 0.2 convolution_convert_fusion.2
  145.4 17.8 %all_to_all.56 = bf16[64,4,128]{2,1,0:T(4,128)(2,1)S(1)} all-to-all(bf16[64,4,128]{2,1,0:T(4,128)(2,1)S(1)} %bitcast.75), channel_id=1, replica_groups=mesh['trip'=64,'aux'=8] {'trip'}, dimensions={0} | all-to-all | bytes 131072 | tf_op jit(solution)/shard_map/all_to_all | solution.py:36
  163.2 0.2 fusion.3
  163.4 0.7 broadcast_in_dim.108
  164.0 5.5 %all-to-all-start.9 = ((bf16[8,64,128]{2,1,0:T(8,128)(2,1)}), bf16[8,64,128]{2,1,0:T(8,128)(2,1)S(1)}, u32[]{:S(2)}, u32[]{:S(2)}) async-start(bf16[8,64,128]{2,1,0:T(8,128)(2,1)} %broadcast_in_dim.108), calls=%async_computation.10 | async-start | bytes 262144 | tf_op jit(solution)/shard_map/all_to_all | solution.py:36
  169.5 1.1 constant_dynamic-slice_fusion.5.came_ref
  170.6 0.9 shard_map.146
  171.5 3.3 %all-to-all-done.9 = bf16[8,64,128]{2,1,0:T(8,128)(2,1)S(1)} async-done(((bf16[8,64,128]{2,1,0:T(8,128)(2,1)}), bf16[8,64,128]{2,1,0:T(8,128)(2,1)S(1)}, u32[]{:S(2)}, u32[]{:S(2)}) %all-to-all-start.9) | async-done | bytes 131104 | tf_op jit(solution)/shard_map/all_to_all | solution.py:36
  174.9 0.7 convert_add_fusion
  (55 shorter events, 1.2 us)
Async XLA Ops:
  7.2 65.2 %reduce-scatter.2.cloned.1.call-start = ((), (), s32[]{:S(2)}) async-start(), calls=%async_computation.11 | async-start | bytes 4165632 | tf_op jit(solution)/shard_map/reduce_scatter | solution.py:459
  7.2 24.3 %copy-start.5 = (s32[9,3,1]{0,2,1:T(1,128)S(1)}, s32[9,3,1]{0,2,1:T(1,128)}, u32[]{:S(2)}) copy-start(s32[9,3,1]{0,2,1:T(1,128)} %param.24) | copy-start | bytes 328
  7.2 25.4 %copy-start.6 = (f32[9,3]{0,1:T(4,128)S(1)}, f32[9,3]{0,1:T(4,128)}, u32[]{:S(2)}) copy-start(f32[9,3]{0,1:T(4,128)} %param.17) | copy-start | bytes 328
  7.2 25.5 %copy-start.4 = (f32[9,40]{1,0:T(8,128)S(1)}, f32[9,40]{1,0:T(8,128)}, u32[]{:S(2)}) copy-start(f32[9,40]{1,0:T(8,128)} %param.16) | copy-start | bytes 4324
  7.2 25.5 %copy-start.8 = (s32[9]{0:T(128)S(1)}, s32[9]{0:T(128)}, u32[]{:S(2)}) copy-start(s32[9]{0:T(128)} %param.18) | copy-start | bytes 112
  7.3 25.7 %copy-start.9 = (s32[16]{0:T(128)S(1)}, s32[16]{0:T(128)}, u32[]{:S(2)}) copy-start(s32[16]{0:T(128)} %param.23) | copy-start | bytes 196
  7.3 25.8 %copy-start.3 = (f32[16,64]{1,0:T(8,128)S(1)}, f32[16,64]{1,0:T(8,128)}, u32[]{:S(2)}) copy-start(f32[16,64]{1,0:T(8,128)} %param.21) | copy-start | bytes 12292
  7.3 25.9 %copy-start.2 = (bf16[16,4096]{1,0:T(8,128)(2,1)S(1)}, bf16[16,4096]{1,0:T(8,128)(2,1)}, u32[]{:S(2)}) copy-start(bf16[16,4096]{1,0:T(8,128)(2,1)} %param.20) | copy-start | bytes 393220
  7.3 26.4 %copy-start.7 = (f32[16]{0:T(128)S(1)}, f32[16]{0:T(128)}, u32[]{:S(2)}) copy-start(f32[16]{0:T(128)} %param.22) | copy-start | bytes 196
  12.2 22.5 %copy-start = (f32[9,5,1600]{2,1,0:T(8,128)S(1)}, f32[9,5,1600]{2,1,0:T(8,128)}, u32[]{:S(2)}) copy-start(f32[9,5,1600]{2,1,0:T(8,128)} %old_ref.1) | copy-start | bytes 864004
  12.2 33.3 %all-to-all-start = ((bf16[64,4,128]{2,1,0:T(4,128)(2,1)}), bf16[64,4,128]{2,1,0:T(4,128)(2,1)S(1)}, u32[]{:S(2)}, u32[]{:S(2)}) async-start(bf16[64,4,128]{2,1,0:T(4,128)(2,1)} %get-tuple-element.27), calls=%async_computation | async-start | bytes 131072 | tf_op jit(solution)/shard_map/all_to_all | solution.py:36
  64.6 13.7 %all-to-all-start.2 = ((bf16[8,8,1664]{2,1,0:T(8,128)(2,1)}), bf16[8,8,1664]{2,1,0:T(8,128)(2,1)S(1)}, u32[]{:S(2)}, u32[]{:S(2)}) async-start(bf16[8,8,1664]{2,1,0:T(8,128)(2,1)} %bitcast.16), calls=%async_computation.2 | async-start | bytes 425984 | tf_op jit(solution)/shard_map/all_to_all | solution.py:36
  72.2 97.3 %all-gather.3.cloned.1.call-start = ((), (), s32[]{:S(2)}) async-start(), calls=%async_computation.12 | async-start | bytes 1382400 | tf_op jit(solution)/shard_map/all_gather | solution.py:591
  72.4 1.0 copy-start.1
  164.0 10.8 %all-to-all-start.9 = ((bf16[8,64,128]{2,1,0:T(8,128)(2,1)}), bf16[8,64,128]{2,1,0:T(8,128)(2,1)S(1)}, u32[]{:S(2)}, u32[]{:S(2)}) async-start(bf16[8,64,128]{2,1,0:T(8,128)(2,1)} %broadcast_in_dim.108), calls=%async_computation.10 | async-start | bytes 262144 | tf_op jit(solution)/shard_map/all_to_all | solution.py:36
Sparse Core Ops, SparseCore 0:
  12.3 48.3 reduce-scatter.1
  137.4 19.7 all-gather.2

commit v8 on v7

--- a/solution.py
+++ b/solution.py
@@ -25,11 +25,6 @@
 
 def mm_tn(x, y):
     return lax.dot_general(x, y, (((0,), (0,)), ((), ())), preferred_element_type=F32)
-
-
-def high_low(x):
-    high = x.astype(BF)
-    return high, (x - high.astype(F32)).astype(BF)
 
 
 def swap(x, axis):
@@ -282,10 +277,8 @@
     npno, width = covers.shape[1], covers.shape[0]
     half_rows = naux * chunk
     mask = block_mask(3 * npno, npno, width, width // 3)
-    high, low = high_low(mm_nt(new, matrix))
-    left = jnp.where(mask, mm(pieces, high) + mm(pieces, low), 0.0)
-    high, low = high_low(left)
-    back = mm(high, covers) + mm(low, covers)
+    left = mm(pieces, mm_nt(new, matrix).astype(BF))
+    back = mm(jnp.where(mask, left, 0.0).astype(BF), covers)
     packed = []
     for k in range(3):
         block = back[2 * k * half_rows : 2 * (k + 1) * half_rows]

time: 183 us -> 183 us (level)
  no operation moved by 1% of the time
where the time goes in v8:
time: 183 us; the launch traced here: 182 us
  blocking collectives  98.1 us (54%)
  starting transfers between devices  32.5 us (18%)
  waiting for transfers between devices  18.1 us (10%)
  between operations  14.4 us (8%)
  Pallas kernels  11.1 us (6%)
  local copies, waits for them, and re-layouts  4.95 us (3%)
  other arithmetic  2.05 us (1%)
    all_to_all x7, blocking collectives, swap(): return lax.all_to_all(x, axis, split_axis=0, concat_axis=0, tiled=True)  98.1 us
    all_to_all x3, starting transfers between devices, swap(): return lax.all_to_all(x, axis, split_axis=0, concat_axis=0, tiled=True)  32.4 us
    all_to_all x3, waiting for transfers between devices, swap(): return lax.all_to_all(x, axis, split_axis=0, concat_axis=0, tiled=True)  18.1 us
    pallas_call x1, Pallas kernels, integral_blocks(): call(functools.partial(blocks_kernel, naux, share), (jax.ShapeDtypeStruct...  4.89 us
  transfers between devices with their start and end apart: 5, of which 3 were waited for; matrix products, arithmetic and copies ran while one was open for 3% of the time, Pallas kernels for 1%

profile of v8, /device:TPU:1, one launch (start us, length us, event | category | flops | bytes accessed | tf_op | source)
XLA Modules:
  0.0 182.2 jit_solution(9661633156513771686)
XLA Ops:
  7.3 4.9 %shard_map.140 = (bf16[8,1808,128]{2,1,0:T(8,128)(2,1)}, bf16[64,4,128]{2,1,0:T(4,128)(2,1)}) custom-call(bf16[9,1600,128]{2,1,0:T(8,128)(2,1)} %bitcast.63, bf16[9,120,128]{2,1,0:T(8,128)(2,1)} %bitcast.71, s32[3,1,9]{2,1,0:T(1,128)} %bitcast.83, s32[3,9]{1,0:T(4,128)} %bitcast.84), custom_call_target="tpu_custom_call" | custom-call | tf_op jit(solution)/shard_map/pallas_call | solution.py:135
  12.2 19.3 %all-to-all-start = ((bf16[64,4,128]{2,1,0:T(4,128)(2,1)}), bf16[64,4,128]{2,1,0:T(4,128)(2,1)S(1)}, u32[]{:S(2)}, u32[]{:S(2)}) async-start(bf16[64,4,128]{2,1,0:T(4,128)(2,1)} %get-tuple-element.27), calls=%async_computation | async-start | bytes 131072 | tf_op jit(solution)/shard_map/all_to_all | solution.py:31
  31.5 0.1 copy.34
  31.6 0.8 constant_dynamic-slice_fusion.2
  32.4 0.1 copy.42
  32.5 0.1 copy.43
  32.6 0.1 broadcast_in_dim.94
  33.2 0.1 select_reduce_fusion.1
  33.3 0.1 select_reduce_fusion
  33.5 0.1 broadcast_and_fusion
  33.7 0.1 add_add_fusion
  33.8 0.1 fusion.8
  33.9 0.1 fusion.9.later_order_ref.order_ref
  34.0 0.1 fusion.5.order_ref
  34.2 0.1 add.403
  34.4 0.1 copy.37
  34.6 0.1 and.277
  34.7 0.2 shard_map.141.old_ref
  35.0 0.2 fusion.6.route_ref
  35.2 10.3 %all-to-all-done = bf16[64,4,128]{2,1,0:T(4,128)(2,1)S(1)} async-done(((bf16[64,4,128]{2,1,0:T(4,128)(2,1)}), bf16[64,4,128]{2,1,0:T(4,128)(2,1)S(1)}, u32[]{:S(2)}, u32[]{:S(2)}) %all-to-all-start) | async-done | bytes 65568 | tf_op jit(solution)/shard_map/all_to_all | solution.py:31
  45.5 0.1 convolution_convert_fusion.1
  45.6 18.0 %all_to_all.50 = bf16[64,4,128]{2,1,0:T(4,128)(2,1)S(1)} all-to-all(bf16[64,4,128]{2,1,0:T(4,128)(2,1)S(1)} %bitcast.73), channel_id=1, replica_groups=mesh['trip'=64,'aux'=8] {'trip'}, dimensions={0} | all-to-all | bytes 131072 | tf_op jit(solution)/shard_map/all_to_all | solution.py:31
  63.7 0.9 shard_map.142
  64.6 7.7 %all-to-all-start.2 = ((bf16[8,8,1664]{2,1,0:T(8,128)(2,1)}), bf16[8,8,1664]{2,1,0:T(8,128)(2,1)S(1)}, u32[]{:S(2)}, u32[]{:S(2)}) async-start(bf16[8,8,1664]{2,1,0:T(8,128)(2,1)} %bitcast.16), calls=%async_computation.2 | async-start | bytes 425984 | tf_op jit(solution)/shard_map/all_to_all | solution.py:31
  72.2 0.1 copy.39.col_ref
  72.4 1.0 copy-done.1
  73.4 0.5 shard_map.143
  73.9 4.4 %all-to-all-done.2 = bf16[8,8,1664]{2,1,0:T(8,128)(2,1)S(1)} async-done(((bf16[8,8,1664]{2,1,0:T(8,128)(2,1)}), bf16[8,8,1664]{2,1,0:T(8,128)(2,1)S(1)}, u32[]{:S(2)}, u32[]{:S(2)}) %all-to-all-start.2) | async-done | bytes 213024 | tf_op jit(solution)/shard_map/all_to_all | solution.py:31
  78.3 1.7 shard_map.144
  80.0 8.1 %all_to_all.51 = bf16[8,24,128]{2,1,0:T(8,128)(2,1)S(1)} all-to-all(bf16[8,24,128]{2,1,0:T(8,128)(2,1)S(1)} %bitcast.62), channel_id=1, replica_groups=mesh['trip'=64,'aux'=8] {'aux'}, dimensions={0} | all-to-all | bytes 98304 | tf_op jit(solution)/shard_map/all_to_all | solution.py:31
  88.1 0.2 convolution_convert_fusion.3
  88.3 17.8 %all_to_all.52 = bf16[64,4,128]{2,1,0:T(4,128)(2,1)S(1)} all-to-all(bf16[64,4,128]{2,1,0:T(4,128)(2,1)S(1)} %bitcast.76), channel_id=1, replica_groups=mesh['trip'=64,'aux'=8] {'trip'}, dimensions={0} | all-to-all | bytes 131072 | tf_op jit(solution)/shard_map/all_to_all | solution.py:31
  106.1 0.2 fusion.14
  106.3 0.1 convolution_convert_fusion
  106.4 18.4 %all_to_all.53 = bf16[64,4,128]{2,1,0:T(4,128)(2,1)S(1)} all-to-all(bf16[64,4,128]{2,1,0:T(4,128)(2,1)S(1)} %bitcast.74), channel_id=1, replica_groups=mesh['trip'=64,'aux'=8] {'trip'}, dimensions={0} | all-to-all | bytes 131072 | tf_op jit(solution)/shard_map/all_to_all | solution.py:31
  124.9 0.2 convolution_convert_fusion.4
  125.0 10.0 %all_to_all.54 = bf16[8,24,128]{2,1,0:T(8,128)(2,1)S(1)} all-to-all(bf16[8,24,128]{2,1,0:T(8,128)(2,1)S(1)} %bitcast.77), channel_id=1, replica_groups=mesh['trip'=64,'aux'=8] {'aux'}, dimensions={0} | all-to-all | bytes 98304 | tf_op jit(solution)/shard_map/all_to_all | solution.py:31
  135.0 2.0 %shard_map.145 = (bf16[192,128]{1,0:T(8,128)(2,1)S(1)}, bf16[40,1920]{1,0:T(8,128)(2,1)}) custom-call(bf16[192,128]{1,0:T(8,128)(2,1)S(1)} %bitcast.60, bf16[192,192]{1,0:T(8,128)(2,1)S(1)} %fusion.9.later_order_ref.order_ref, bf16[2,120,64]{2,1,0:T(8,128)(2,1)S(1)} %bitcast.57, bf16[2,192,40]{2,1,0:T(8,128)(2,1)S(1)} %bitcast.54, ...), custom_call_target="tpu_custom_call" | custom-call | tf_op jit(solution)/shard_map/pallas_call | solution.py:566
  137.0 7.9 %all_to_all.55 = bf16[8,24,128]{2,1,0:T(8,128)(2,1)S(1)} all-to-all(bf16[8,24,128]{2,1,0:T(8,128)(2,1)S(1)} %bitcast.61), channel_id=1, replica_groups=mesh['trip'=64,'aux'=8] {'aux'}, dimensions={0} | all-to-all | bytes 98304 | tf_op jit(solution)/shard_map/all_to_all | solution.py:31
  144.9 0.2 convolution_convert_fusion.2
  145.1 17.8 %all_to_all.56 = bf16[64,4,128]{2,1,0:T(4,128)(2,1)S(1)} all-to-all(bf16[64,4,128]{2,1,0:T(4,128)(2,1)S(1)} %bitcast.75), channel_id=1, replica_groups=mesh['trip'=64,'aux'=8] {'trip'}, dimensions={0} | all-to-all | bytes 131072 | tf_op jit(solution)/shard_map/all_to_all | solution.py:31
  162.9 0.2 fusion.3
  163.1 0.7 broadcast_in_dim.108
  163.8 5.5 %all-to-all-start.9 = ((bf16[8,64,128]{2,1,0:T(8,128)(2,1)}), bf16[8,64,128]{2,1,0:T(8,128)(2,1)S(1)}, u32[]{:S(2)}, u32[]{:S(2)}) async-start(bf16[8,64,128]{2,1,0:T(8,128)(2,1)} %broadcast_in_dim.108), calls=%async_computation.10 | async-start | bytes 262144 | tf_op jit(solution)/shard_map/all_to_all | solution.py:31
  169.3 1.1 constant_dynamic-slice_fusion.5.came_ref
  170.4 0.9 shard_map.146
  171.2 3.3 %all-to-all-done.9 = bf16[8,64,128]{2,1,0:T(8,128)(2,1)S(1)} async-done(((bf16[8,64,128]{2,1,0:T(8,128)(2,1)}), bf16[8,64,128]{2,1,0:T(8,128)(2,1)S(1)}, u32[]{:S(2)}, u32[]{:S(2)}) %all-to-all-start.9) | async-done | bytes 131104 | tf_op jit(solution)/shard_map/all_to_all | solution.py:31
  174.7 0.7 convert_add_fusion
  (55 shorter events, 1.2 us)
Async XLA Ops:
  7.2 65.2 %reduce-scatter.2.cloned.1.call-start = ((), (), s32[]{:S(2)}) async-start(), calls=%async_computation.11 | async-start | bytes 4165632 | tf_op jit(solution)/shard_map/reduce_scatter | solution.py:452
  7.2 24.3 %copy-start.5 = (s32[9,3,1]{0,2,1:T(1,128)S(1)}, s32[9,3,1]{0,2,1:T(1,128)}, u32[]{:S(2)}) copy-start(s32[9,3,1]{0,2,1:T(1,128)} %param.24) | copy-start | bytes 328
  7.2 25.4 %copy-start.6 = (f32[9,3]{0,1:T(4,128)S(1)}, f32[9,3]{0,1:T(4,128)}, u32[]{:S(2)}) copy-start(f32[9,3]{0,1:T(4,128)} %param.17) | copy-start | bytes 328
  7.2 25.5 %copy-start.4 = (f32[9,40]{1,0:T(8,128)S(1)}, f32[9,40]{1,0:T(8,128)}, u32[]{:S(2)}) copy-start(f32[9,40]{1,0:T(8,128)} %param.16) | copy-start | bytes 4324
  7.2 25.5 %copy-start.8 = (s32[9]{0:T(128)S(1)}, s32[9]{0:T(128)}, u32[]{:S(2)}) copy-start(s32[9]{0:T(128)} %param.18) | copy-start | bytes 112
  7.3 25.7 %copy-start.9 = (s32[16]{0:T(128)S(1)}, s32[16]{0:T(128)}, u32[]{:S(2)}) copy-start(s32[16]{0:T(128)} %param.23) | copy-start | bytes 196
  7.3 25.8 %copy-start.3 = (f32[16,64]{1,0:T(8,128)S(1)}, f32[16,64]{1,0:T(8,128)}, u32[]{:S(2)}) copy-start(f32[16,64]{1,0:T(8,128)} %param.21) | copy-start | bytes 12292
  7.3 25.9 %copy-start.2 = (bf16[16,4096]{1,0:T(8,128)(2,1)S(1)}, bf16[16,4096]{1,0:T(8,128)(2,1)}, u32[]{:S(2)}) copy-start(bf16[16,4096]{1,0:T(8,128)(2,1)} %param.20) | copy-start | bytes 393220
  7.3 26.4 %copy-start.7 = (f32[16]{0:T(128)S(1)}, f32[16]{0:T(128)}, u32[]{:S(2)}) copy-start(f32[16]{0:T(128)} %param.22) | copy-start | bytes 196
  12.2 22.5 %copy-start = (f32[9,5,1600]{2,1,0:T(8,128)S(1)}, f32[9,5,1600]{2,1,0:T(8,128)}, u32[]{:S(2)}) copy-start(f32[9,5,1600]{2,1,0:T(8,128)} %old_ref.1) | copy-start | bytes 864004
  12.2 33.3 %all-to-all-start = ((bf16[64,4,128]{2,1,0:T(4,128)(2,1)}), bf16[64,4,128]{2,1,0:T(4,128)(2,1)S(1)}, u32[]{:S(2)}, u32[]{:S(2)}) async-start(bf16[64,4,128]{2,1,0:T(4,128)(2,1)} %get-tuple-element.27), calls=%async_computation | async-start | bytes 131072 | tf_op jit(solution)/shard_map/all_to_all | solution.py:31
  64.6 13.7 %all-to-all-start.2 = ((bf16[8,8,1664]{2,1,0:T(8,128)(2,1)}), bf16[8,8,1664]{2,1,0:T(8,128)(2,1)S(1)}, u32[]{:S(2)}, u32[]{:S(2)}) async-start(bf16[8,8,1664]{2,1,0:T(8,128)(2,1)} %bitcast.16), calls=%async_computation.2 | async-start | bytes 425984 | tf_op jit(solution)/shard_map/all_to_all | solution.py:31
  72.2 97.0 %all-gather.3.cloned.1.call-start = ((), (), s32[]{:S(2)}) async-start(), calls=%async_computation.12 | async-start | bytes 1382400 | tf_op jit(solution)/shard_map/all_gather | solution.py:584
  72.4 1.0 copy-start.1
  163.8 10.8 %all-to-all-start.9 = ((bf16[8,64,128]{2,1,0:T(8,128)(2,1)}), bf16[8,64,128]{2,1,0:T(8,128)(2,1)S(1)}, u32[]{:S(2)}, u32[]{:S(2)}) async-start(bf16[8,64,128]{2,1,0:T(8,128)(2,1)} %broadcast_in_dim.108), calls=%async_computation.10 | async-start | bytes 262144 | tf_op jit(solution)/shard_map/all_to_all | solution.py:31
Sparse Core Ops, SparseCore 0:
  12.3 48.3 reduce-scatter.1
  137.1 19.7 all-gather.2
